TPU v7x, 256 devices: a whole 4x4x8 slice. The times are simulated.
256 devices in a mesh: row: 32 (over y, x, core), col: 8 (over z).
Axes of the slice: x: 4, y: 4, z: 8, core: 2. Of those that a mesh axis runs over, the one named last changes fastest.
Arguments:
- activations: bfloat16 [512, 12288], P('row', 'col'), may hold values from -6 to 6
- w_in: bfloat16 [12288, 24576], P('col', 'row'), may hold values from -0.0546875 to 0.0546875
- bias_in: float32 [24576], P('row'), may hold values from -5 to 5
- w_out: bfloat16 [24576, 12288], P('row', 'col'), may hold values from -0.0390625 to 0.0390625
- cotangent: bfloat16 [512, 12288], P('row', 'col'), may hold values from -6 to 6
Outputs:
- outputs: bfloat16 [512, 12288], P('row', 'col')
- input_grad: bfloat16 [512, 12288], P('row', 'col')
- w_in_grad: bfloat16 [12288, 24576], P('col', 'row')
- w_out_grad: bfloat16 [24576, 12288], P('row', 'col')
- bias_grad: float32 [24576], P('row')
All inputs are finite; a program needn't handle non-finite values.
Results may differ from a plain program's by a relative error of at most 0.005.
Values may be sent and summed in bfloat16 or wider, within the bound.
No kernel may reach another device: no remote copies, remote signals or barrier semaphores. Data moves between devices by JAX's collectives and lax.ppermute only.
A program may use at most 64 MiB of HBM per device.

v0:
```python
import math

import jax
import jax.numpy as jnp
from jax import lax
from jax.sharding import PartitionSpec as P

TOKENS = 512


root_coef = math.sqrt(2.0 / math.pi)


def gelu_tanh(values):
    inner = root_coef * (values + 0.044715 * values * values * values)
    return 0.5 * values * (1.0 + jnp.tanh(inner))


def gelu_slope(values):
    inner = root_coef * (values + 0.044715 * values * values * values)
    tanh_val = jnp.tanh(inner)
    return 0.5 * (1.0 + tanh_val) + 0.5 * values * (1.0 - tanh_val * tanh_val) * root_coef * (
        1.0 + 3.0 * 0.044715 * values * values
    )


def contract_rows(left, right):
    return lax.dot_general(
        left, right, (((0,), (0,)), ((), ())), preferred_element_type=jnp.float32
    )


def contract_cols(left, right):
    return lax.dot_general(
        left, right, (((1,), (1,)), ((), ())), preferred_element_type=jnp.float32
    )


def local(activations, w_in, bias_in, w_out, cotangent):
    grad_scale = jnp.float32(1.0 / math.sqrt(TOKENS))
    all_inputs = lax.all_gather(activations, "row", axis=0, tiled=True)
    pre_part = jnp.dot(all_inputs, w_in, preferred_element_type=jnp.float32)
    pre_act = lax.psum(pre_part, "col") + bias_in
    hidden = gelu_tanh(pre_act).astype(jnp.bfloat16)
    rows_here = hidden
    outputs = lax.psum_scatter(
        jnp.dot(rows_here, w_out, preferred_element_type=jnp.float32),
        "row",
        scatter_dimension=0,
        tiled=True,
    ).astype(jnp.bfloat16)
    all_grads = lax.all_gather(cotangent, "row", axis=0, tiled=True)
    grad_part = contract_cols(all_grads, w_out)
    hidden_grad = lax.psum(grad_part, "col")
    pre_grad = hidden_grad * gelu_slope(pre_act)
    bias_grad = jnp.sum(pre_grad, axis=0) * grad_scale
    pre_grad_b = pre_grad.astype(jnp.bfloat16)
    w_out_grad = (contract_rows(hidden, all_grads) * grad_scale).astype(jnp.bfloat16)
    w_in_sum = contract_rows(all_inputs, pre_grad_b)
    w_in_grad = (w_in_sum * grad_scale).astype(jnp.bfloat16)
    rows_here = pre_grad_b
    input_grad = lax.psum_scatter(
        contract_cols(rows_here, w_in), "row", scatter_dimension=0, tiled=True
    ).astype(jnp.bfloat16)
    return (outputs, input_grad, w_in_grad, w_out_grad, bias_grad)


def solution(mesh):
    placed = (P("row", "col"), P("col", "row"), P("row"), P("row", "col"), P("row", "col"))
    return jax.shard_map(
        local,
        mesh=mesh,
        in_specs=placed,
        out_specs=(P("row", "col"), P("row", "col"), P("col", "row"), P("row", "col"), P("row")),
        check_vma=False,
    )
```

profile of v0, /device:TPU:4, one launch (start us, length us, event | category | flops | bytes accessed | tf_op | source)
XLA Modules:
  0.0 400.3 jit_solution(16350672839215347127)
XLA Ops:
  7.2 0.0 copy-start
  7.2 0.0 all-gather.3.cloned.1.call-start
  7.2 0.7 all-gather.3.cloned.1.call-update
  7.9 0.0 all-gather.5.cloned.1.call-start
  8.0 0.7 all-gather.5.cloned.1.call-update
  8.7 0.0 all-reduce.3.cloned.1.call-start
  8.7 52.6 %all-gather.3.cloned.1.call-done = bf16[512,1536]{1,0:T(8,128)(2,1)} async-done(((bf16[16,1536]{1,0:T(8,128)(2,1)}), bf16[512,1536]{1,0:T(8,128)(2,1)}) %all-gather.3.cloned.1.call-update) | async-done | bytes 1572880 | tf_op jit(solution)/shard_map/all_gather | solution.py:41
  61.4 0.0 copy-done
  61.4 3.9 fusion.13
  65.3 46.3 %all-gather.5.cloned.1.call-done = bf16[512,1536]{1,0:T(8,128)(2,1)} async-done(((bf16[16,1536]{1,0:T(8,128)(2,1)}), bf16[512,1536]{1,0:T(8,128)(2,1)}) %all-gather.5.cloned.1.call-update) | async-done | bytes 1572880 | tf_op jit(solution)/shard_map/all_gather | solution.py:52
  111.6 4.7 %fusion.14 = f32[512,768]{1,0:T(8,128)} fusion(bf16[512,1536]{1,0:T(8,128)(2,1)} %all-gather.5.cloned.1.call-done, bf16[768,1536]{1,0:T(8,128)(2,1)} %param.8), kind=kOutput, calls=%fused_computation.19 | convolution fusion | flops 1207959552 | bytes 5505024 | tf_op jit(solution)/shard_map/dot_general | solution.py:34
  116.3 0.0 copy-start.1
  116.3 0.0 all-reduce.3.cloned.1.call-update
  116.3 0.0 reduce-scatter.5.cloned.1.call-start
  116.3 91.6 %all-reduce.3.cloned.1.call-done = (f32[512,768]{1,0:T(8,128)}, f32[512,768]{1,0:T(8,128)}) async-done(((f32[512,768]{1,0:T(8,128)}, f32[512,768]{1,0:T(8,128)}), (f32[512,768]{1,0:T(8,128)}, f32[512,768]{1,0:T(8,128)})) %all-reduce.3.cloned.1.call-update) | async-done | bytes 3145744 | tf_op jit(solution)/shard_map/psum | solution.py:43
  207.9 0.0 copy-done.1
  207.9 3.0 fusion.11
  210.9 3.1 fusion.8
  214.0 0.0 reduce-scatter.5.cloned.1.call-update
  214.1 0.0 reduce-scatter.3.cloned.1.call-start
  214.1 5.3 %fusion.10 = f32[512,1536]{1,0:T(8,128)} fusion(bf16[768,1536]{1,0:T(8,128)(2,1)} %param.8, f32[512,768]{1,0:T(8,128)} %get-tuple-element.10, f32[768]{0:T(1024)S(1)} %copy-done.1), kind=kOutput, calls=%fused_computation.16 | convolution fusion | flops 1211891712 | bytes 7080960 | tf_op jit(solution)/shard_map/dot_general | solution.py:47
  219.4 0.0 reduce-scatter.3.cloned.1.call-update
  219.5 4.2 %fusion = bf16[1536,768]{0,1:T(8,128)(2,1)} fusion(bf16[512,1536]{1,0:T(8,128)(2,1)} %all-gather.3.cloned.1.call-done, bf16[512,768]{1,0:T(8,128)(2,1)S(1)} %get-tuple-element.13), kind=kOutput, calls=%fused_computation.2 | convolution fusion | flops 1210318848 | bytes 4718592 | tf_op jit(solution)/shard_map/dot_general | solution.py:28
  223.7 4.3 %copy.10 = bf16[1536,768]{1,0:T(8,128)(2,1)} copy(bf16[1536,768]{0,1:T(8,128)(2,1)} %fusion) | data formatting | bytes 4718592
  228.0 0.6 broadcast_multiply_fusion
  228.6 5.0 %multiply_convert_fusion = bf16[768,1536]{1,0:T(8,128)(2,1)} fusion(bf16[512,1536]{1,0:T(8,128)(2,1)} %all-gather.5.cloned.1.call-done, f32[512,768]{1,0:T(8,128)} %get-tuple-element.10, f32[768]{0:T(1024)S(1)} %copy-done.1), kind=kOutput, calls=%fused_computation | convolution fusion | flops 1214251008 | bytes 5508096 | tf_op jit(solution)/shard_map/dot_general | solution.py:28
  233.5 67.1 %reduce-scatter.5.cloned.1.call-done = f32[16,1536]{1,0:T(8,128)} async-done(((f32[512,1536]{1,0:T(8,128)}), f32[16,1536]{1,0:T(8,128)}) %reduce-scatter.5.cloned.1.call-update) | async-done | bytes 98320 | tf_op jit(solution)/shard_map/reduce_scatter | solution.py:62
  300.6 1.5 convert_element_type.24
  302.1 90.2 %reduce-scatter.3.cloned.1.call-done = f32[16,1536]{1,0:T(8,128)} async-done(((f32[512,1536]{1,0:T(8,128)}), f32[16,1536]{1,0:T(8,128)}) %reduce-scatter.3.cloned.1.call-update) | async-done | bytes 98320 | tf_op jit(solution)/shard_map/reduce_scatter | solution.py:46
  392.3 1.5 convert_element_type.22
Async XLA Ops:
  7.2 54.2 %copy-start = (bf16[1536,768]{1,0:T(8,128)(2,1)S(1)}, bf16[1536,768]{1,0:T(8,128)(2,1)}, u32[]{:S(2)}) copy-start(bf16[1536,768]{1,0:T(8,128)(2,1)} %param.6) | copy-start | bytes 7077892
  7.2 54.2 %all-gather.3.cloned.1.call-start = ((), (), s32[]{:S(2)}) async-start(), calls=%async_computation.2 | async-start | bytes 1622016 | tf_op jit(solution)/shard_map/all_gather | solution.py:41
  7.9 103.7 %all-gather.5.cloned.1.call-start = ((), (), s32[]{:S(2)}) async-start(), calls=%async_computation.4 | async-start | bytes 1622016 | tf_op jit(solution)/shard_map/all_gather | solution.py:52
  8.7 199.3 %all-reduce.3.cloned.1.call-start = ((), (), s32[]{:S(2)}) async-start(), calls=%async_computation.6 | async-start | bytes 6291456 | tf_op jit(solution)/shard_map/psum | solution.py:43
  116.3 91.7 %copy-start.1 = (f32[768]{0:T(1024)S(1)}, f32[768]{0:T(1024)}, u32[]{:S(2)}) copy-start(f32[768]{0:T(1024)} %param.7) | copy-start | bytes 9220
  116.3 184.3 %reduce-scatter.5.cloned.1.call-start = ((), (), s32[]{:S(2)}) async-start(), calls=%async_computation.5 | async-start | bytes 3244032 | tf_op jit(solution)/shard_map/reduce_scatter | solution.py:62
  214.1 178.2 %reduce-scatter.3.cloned.1.call-start = ((), (), s32[]{:S(2)}) async-start(), calls=%async_computation.3 | async-start | bytes 3244032 | tf_op jit(solution)/shard_map/reduce_scatter | solution.py:46
Sparse Core Ops, SparseCore 0:
  10.6 50.7 all-gather.2
  63.9 47.6 all-gather.4
  116.4 91.4 all-reduce.2
  214.2 86.3 reduce-scatter.4
  304.9 87.3 reduce-scatter.2
where the time goes:
time: 401 us; the launch traced here: 400 us
  waiting for transfers between devices  349 us (87%)
  matrix products  26.2 us (7%)
  between operations  13.8 us (3%)
  other arithmetic  6.62 us (2%)
  local copies, waits for them, and re-layouts  4.3 us (1%)
    psum x1, waiting for transfers between devices, local(): pre_act = lax.psum(pre_part, 'col') + bias_in  91.6 us
    reduce_scatter x1, waiting for transfers between devices, local(): lax.psum_scatter(jnp.dot(rows_here, w_out, preferred_element_type=jnp.flo...  90.2 us
    reduce_scatter x1, waiting for transfers between devices, local(): lax.psum_scatter(contract_cols(rows_here, w_in), 'row', scatter_dimension...  67.1 us
    all_gather x1, waiting for transfers between devices, local(): all_inputs = lax.all_gather(activations, 'row', axis=0, tiled=True)  52.6 us
    all_gather x1, waiting for transfers between devices, local(): all_grads = lax.all_gather(cotangent, 'row', axis=0, tiled=True)  46.3 us
    dot_general x2, matrix products, contract_rows(): lax.dot_general(left, right, (((0,), (0,)), ((), ())), preferred_element_...  9.18 us
  transfers between devices with their start and end apart: 5, of which 5 were waited for; matrix products, arithmetic and copies ran while one was open for 6% of the time, Pallas kernels for 0%

commit v1 on v0

v1 whole, which is shorter than its diff:
```python
import math

import jax
import jax.numpy as jnp
from jax import lax
from jax.sharding import PartitionSpec as P

TOKENS = 512
HALF = 256
BF16 = jnp.bfloat16
F32 = jnp.float32

root_coef = math.sqrt(2.0 / math.pi)


def gelu_and_slope(values):
    inner = root_coef * (values + 0.044715 * values * values * values)
    tanh_val = jnp.tanh(inner)
    gelu = 0.5 * values * (1.0 + tanh_val)
    slope = 0.5 * (1.0 + tanh_val) + 0.5 * values * (1.0 - tanh_val * tanh_val) * root_coef * (
        1.0 + 3.0 * 0.044715 * values * values
    )
    return gelu, slope


def matmul(left, right):
    return jnp.dot(left, right, preferred_element_type=F32)


def contract_rows(left, right):
    return lax.dot_general(
        left, right, (((0,), (0,)), ((), ())), preferred_element_type=F32
    )


def contract_cols(left, right):
    return lax.dot_general(
        left, right, (((1,), (1,)), ((), ())), preferred_element_type=F32
    )


def row_of(y, x, core):
    return (y * 4 + x) * 2 + core


def ring_partner(at, size, odd_links):
    return (at + 1) % size if (at % 2 == 1) == odd_links else (at - 1) % size


def plane_swap(values, kind, first):
    pairs = []
    for y in range(4):
        for x in range(4):
            for core in range(2):
                along_x = (core == 0) == first
                at = x if along_x else y
                to = (at + 2) % 4 if kind == 2 else ring_partner(at, 4, kind == 3)
                pairs.append((row_of(y, x, core), row_of(y, to, core) if along_x else row_of(to, x, core)))
    return lax.ppermute(values, "row", pairs)


def swap_cores(values):
    return lax.ppermute(values, "row", [(i, i ^ 1) for i in range(32)])


def col_swap(values, odd_links):
    return lax.ppermute(values, "col", [(i, ring_partner(i, 8, odd_links)) for i in range(8)])


def local(activations, w_in, bias_in, w_out, cotangent):
    grad_scale = jnp.float32(1.0 / math.sqrt(TOKENS))
    features = activations.shape[1]
    hidden_here = w_in.shape[1]
    me = lax.axis_index("col")
    way = 1 - 2 * (me % 2)

    mine = jnp.stack([activations, cotangent])
    got = {k: plane_swap(mine, k, True) for k in (2, 1, 3)}
    line = jnp.stack([mine, got[1], got[2], got[3]], axis=1)
    got = {k: plane_swap(line, k, False) for k in (2, 1, 3)}
    own = jnp.stack([line, got[1], got[2], got[3]], axis=1).reshape(2, HALF, features)
    other = swap_cores(own)

    def first_products(tokens):
        return matmul(tokens[0], w_in), contract_cols(tokens[1], w_out)

    own_parts = first_products(own)

    def part(halves, j):
        at = ((me + way * j) % 8) * 32
        return jnp.stack(
            [jnp.stack([lax.dynamic_slice_in_dim(x, at, 32, 0) for x in half]) for half in halves]
        )

    far_own = part([own_parts], 4).astype(BF16)
    far_own, other = lax.optimization_barrier((far_own, other))
    from_even = col_swap(far_own, False)
    other_parts = first_products(other)
    from_odd = col_swap(part([other_parts], 4).astype(BF16), True)
    halves = [own_parts, other_parts]
    to_odd = jnp.concatenate([part([own_parts], -3) + from_even.astype(F32), part([other_parts], -3)])
    to_even = jnp.concatenate([part([own_parts], 3), part([other_parts], 3) + from_odd.astype(F32)])
    for j in (2, 1):
        from_odd = col_swap(to_odd.astype(BF16), True)
        from_even = col_swap(to_even.astype(BF16), False)
        to_odd = part(halves, -j) + from_even.astype(F32)
        to_even = part(halves, j) + from_odd.astype(F32)
    from_odd = col_swap(to_odd.astype(BF16), True)
    from_even = col_swap(to_even.astype(BF16), False)
    total = part(halves, 0) + from_even.astype(F32) + from_odd.astype(F32)

    hidden_mine, slope = gelu_and_slope(total[:, 0] + bias_in)
    both = jnp.stack([hidden_mine.astype(BF16), (total[:, 1] * slope).astype(BF16)], axis=1)

    everything = jnp.zeros((2, 2, 8, 32, hidden_here), BF16)
    evens, odds = [both], [both]
    for _ in range(3):
        from_even, from_odd = col_swap(odds[-1], False), col_swap(evens[-1], True)
        evens.append(from_even)
        odds.append(from_odd)
    opposite = jnp.concatenate([col_swap(odds[3][:1], False), col_swap(evens[3][1:], True)])
    for j, block in enumerate(evens + [opposite] + odds[:0:-1]):
        everything = lax.dynamic_update_slice_in_dim(everything, block[:, :, None], (me + way * j) % 8, 2)
    everything = everything.reshape(2, 2, HALF, hidden_here)

    came_out = swap_cores(matmul(everything[1, 0], w_out).astype(BF16))
    came_grad = swap_cores(contract_cols(everything[1, 1], w_in).astype(BF16))
    kept_out = matmul(everything[0, 0], w_out) + came_out.astype(F32)
    kept_grad = contract_cols(everything[0, 1], w_in) + came_grad.astype(F32)
    kept = [
        jnp.stack([x.reshape(4, 4, 16, features)[k] for x in (kept_out, kept_grad)]) for k in range(4)
    ]
    sent = [x.astype(BF16) for x in kept[1:]]
    everything, own, other, *sent = lax.optimization_barrier((everything, own, other, *sent))
    came = {k: plane_swap(sent[k - 1], k, False) for k in (2, 1, 3)}
    plane_sum = kept[0]
    for k in (1, 2, 3):
        plane_sum = plane_sum + came[k].astype(F32)
    came = {k: plane_swap(plane_sum[:, k].astype(BF16), k, True) for k in (2, 1, 3)}
    line_sum = plane_sum[:, 0]
    for k in (1, 2, 3):
        line_sum = line_sum + came[k].astype(F32)
    result = line_sum.astype(BF16)

    hidden = everything[:, 0].reshape(TOKENS, hidden_here)
    pre_grad = everything[:, 1].reshape(TOKENS, hidden_here)
    all_inputs = jnp.concatenate([own[0], other[0]])
    all_grads = jnp.concatenate([own[1], other[1]])
    bias_grad = jnp.sum(pre_grad.astype(F32), axis=0) * grad_scale
    w_out_grad = (contract_rows(hidden, all_grads) * grad_scale).astype(BF16)
    w_in_grad = (contract_rows(all_inputs, pre_grad) * grad_scale).astype(BF16)
    return (result[0], result[1], w_in_grad, w_out_grad, bias_grad)


def solution(mesh):
    placed = (P("row", "col"), P("col", "row"), P("row"), P("row", "col"), P("row", "col"))
    return jax.shard_map(
        local,
        mesh=mesh,
        in_specs=placed,
        out_specs=(P("row", "col"), P("row", "col"), P("col", "row"), P("row", "col"), P("row")),
        check_vma=False,
    )
```

time: 401 us -> 129 us (0.32)
  waiting for transfers between devices: 349 us -> 66.7 us
  starting transfers between devices: 0.2 us -> 38.6 us
  matrix products: 26.2 us -> 12 us
  between operations: 13.8 us -> 1.21 us
    reduce_scatter x2 -> x0, waiting for transfers between devices: 157 us -> none  [the longest x1 90.2 us: local(): lax.psum_scatter(jnp.dot(rows_here, w_out, preferred_element_type=jnp.flo...]
    all_gather x2 -> x0, waiting for transfers between devices: 98.9 us -> none  [the longest x1 52.6 us: local(): all_inputs = lax.all_gather(activations, 'row', axis=0, tiled=True)]
    psum x1 -> x0, waiting for transfers between devices: 91.6 us -> none  [local(): pre_act = lax.psum(pre_part, 'col') + bias_in]
    ppermute x0 -> x31, waiting for transfers between devices: none -> 66.7 us  [the longest x16 40.7 us: col_swap(): lax.ppermute(values, 'col', [(i, ring_partner(i, 8, odd_links)) for i in...]
    ppermute x0 -> x31, starting transfers between devices: none -> 38.6 us  [the longest x16 21.1 us: col_swap(): lax.ppermute(values, 'col', [(i, ring_partner(i, 8, odd_links)) for i in...]
    dot_general x2 -> x4, matrix products: 9.24 us -> 3.09 us  [matmul(): return jnp.dot(left, right, preferred_element_type=F32)]
    dot_general x2 -> x4, matrix products: 7.8 us -> 3.23 us  [contract_cols(): lax.dot_general(left, right, (((1,), (1,)), ((), ())), preferred_element_...]
  transfers between devices with their start and end apart: 5 -> 31, of which waited for: 5 -> 23; matrix products, arithmetic and copies ran while one was open for 6% -> 8% of each run, Pallas kernels for 0% -> 0%
where the time goes in v1:
time: 129 us; the launch traced here: 128 us
  waiting for transfers between devices  66.7 us (52%)
  starting transfers between devices  38.6 us (30%)
  matrix products  12 us (9%)
  local copies, waits for them, and re-layouts  5.02 us (4%)
  other arithmetic  4.83 us (4%)
    ppermute x16, waiting for transfers between devices, col_swap(): lax.ppermute(values, 'col', [(i, ring_partner(i, 8, odd_links)) for i in...  40.7 us
    ppermute x12, waiting for transfers between devices, plane_swap(): return lax.ppermute(values, 'row', pairs)  24.2 us
    ppermute x16, starting transfers between devices, col_swap(): lax.ppermute(values, 'col', [(i, ring_partner(i, 8, odd_links)) for i in...  21.1 us
    ppermute x12, starting transfers between devices, plane_swap(): return lax.ppermute(values, 'row', pairs)  17.4 us
    dot_general x2, matrix products, contract_rows(): lax.dot_general(left, right, (((0,), (0,)), ((), ())), preferred_element_...  5.67 us
    dot_general x4, matrix products, contract_cols(): lax.dot_general(left, right, (((1,), (1,)), ((), ())), preferred_element_...  3.23 us
    unnamed x16, local copies, waits for them, and re-layouts  3.22 us
    dot_general x4, matrix products, matmul(): return jnp.dot(left, right, preferred_element_type=F32)  3.09 us
  transfers between devices with their start and end apart: 31, of which 23 were waited for; matrix products, arithmetic and copies ran while one was open for 8% of the time, Pallas kernels for 0%

profile of v1, /device:TPU:4, one launch (start us, length us, event | category | flops | bytes accessed | tf_op | source)
XLA Modules:
  0.0 128.4 jit_solution(12645077843920171064)
XLA Ops:
  0.6 1.0 fusion.47
  1.6 2.3 %collective-permute-start.1 = (bf16[2,16,1536]{2,1,0:T(8,128)(2,1)S(1)}, bf16[2,16,1536]{2,1,0:T(8,128)(2,1)S(1)}, u32[]{:S(2)}, u32[]{:S(2)}) collective-permute-start(bf16[2,16,1536]{2,1,0:T(8,128)(2,1)S(1)} %get-tuple-element.79), channel_id=1, source_target_pairs={{0,32},{8,136},{16,48},{24,152},{32,0},{40,168},{48,16},{56,184},{... | collective-permute-start | bytes 294920 | tf_op jit(solution)/shard_map/ppermute | solution.py:59
  4.3 1.5 %collective-permute-start.2 = (bf16[2,16,1536]{2,1,0:T(8,128)(2,1)S(1)}, bf16[2,16,1536]{2,1,0:T(8,128)(2,1)S(1)}, u32[]{:S(2)}, u32[]{:S(2)}) collective-permute-start(bf16[2,16,1536]{2,1,0:T(8,128)(2,1)S(1)} %get-tuple-element.79), channel_id=1, source_target_pairs={{0,48},{8,200},{16,32},{24,216},{32,16},{40,232},{48,0},{56,248},{... | collective-permute-start | bytes 294920 | tf_op jit(solution)/shard_map/ppermute | solution.py:59
  5.8 2.0 %collective-permute-done.1 = bf16[2,16,1536]{2,1,0:T(8,128)(2,1)S(1)} collective-permute-done((bf16[2,16,1536]{2,1,0:T(8,128)(2,1)S(1)}, bf16[2,16,1536]{2,1,0:T(8,128)(2,1)S(1)}, u32[]{:S(2)}, u32[]{:S(2)}) %collective-permute-start.1) | collective-permute-done | bytes 98336 | tf_op jit(solution)/shard_map/ppermute | solution.py:59
  8.9 0.8 fusion.48
  9.8 3.2 %collective-permute-start.4 = (bf16[2,4,16,1536]{3,2,1,0:T(8,128)(2,1)}, bf16[2,4,16,1536]{3,2,1,0:T(8,128)(2,1)S(1)}, u32[]{:S(2)}, u32[]{:S(2)}) collective-permute-start(bf16[2,4,16,1536]{3,2,1,0:T(8,128)(2,1)} %get-tuple-element.75), channel_id=1, source_target_pairs={{0,128},{8,40},{16,144},{24,56},{32,160},{40,8},{48,176},{56,24},{... | collective-permute-start | bytes 1179656 | tf_op jit(solution)/shard_map/ppermute | solution.py:59
  14.0 5.3 %collective-permute-done.4 = bf16[2,4,16,1536]{3,2,1,0:T(8,128)(2,1)S(1)} collective-permute-done((bf16[2,4,16,1536]{3,2,1,0:T(8,128)(2,1)}, bf16[2,4,16,1536]{3,2,1,0:T(8,128)(2,1)S(1)}, u32[]{:S(2)}, u32[]{:S(2)}) %collective-permute-start.4) | collective-permute-done | bytes 393248 | tf_op jit(solution)/shard_map/ppermute | solution.py:59
  19.3 4.5 %collective-permute-done.3 = bf16[2,4,16,1536]{3,2,1,0:T(8,128)(2,1)S(1)} collective-permute-done((bf16[2,4,16,1536]{3,2,1,0:T(8,128)(2,1)}, bf16[2,4,16,1536]{3,2,1,0:T(8,128)(2,1)S(1)}, u32[]{:S(2)}, u32[]{:S(2)}) %collective-permute-start.3) | collective-permute-done | bytes 393248 | tf_op jit(solution)/shard_map/ppermute | solution.py:59
  23.8 1.2 pad_maximum_fusion
  25.2 1.0 copy-done.1
  26.2 1.1 copy-done.3
  27.3 0.8 fusion.58
  28.1 0.8 fusion.57
  29.6 0.8 fusion.8
  30.7 0.8 fusion.10
  31.7 2.0 %collective-permute-start.11 = (bf16[1,2,32,768]{3,2,1,0:T(8,128)(2,1)S(1)}, bf16[1,2,32,768]{3,2,1,0:T(8,128)(2,1)S(1)}, u32[]{:S(2)}, u32[]{:S(2)}) collective-permute-start(bf16[1,2,32,768]{3,2,1,0:T(8,128)(2,1)S(1)} %pad_maximum_fusion.9), channel_id=1, source_target_pairs={{0,1},{1,0},{2,3},{3,2},{4,5},{5,4},{6,7},{7,6},{8,9},{9,8},{10,11... | collective-permute-start | bytes 294920 | tf_op jit(solution)/shard_map/ppermute | solution.py:67
  33.7 5.0 %collective-permute-start.7 = (bf16[1,2,32,768]{3,2,1,0:T(8,128)(2,1)S(1)}, bf16[1,2,32,768]{3,2,1,0:T(8,128)(2,1)S(1)}, u32[]{:S(2)}, u32[]{:S(2)}) collective-permute-start(bf16[1,2,32,768]{3,2,1,0:T(8,128)(2,1)S(1)} %pad_maximum_fusion.10), channel_id=1, source_target_pairs={{0,7},{1,2},{2,1},{3,4},{4,3},{5,6},{6,5},{7,0},{8,15},{9,10},{10,... | collective-permute-start | bytes 294920 | tf_op jit(solution)/shard_map/ppermute | solution.py:67
  38.8 2.7 %collective-permute-done.7 = bf16[1,2,32,768]{3,2,1,0:T(8,128)(2,1)S(1)} collective-permute-done((bf16[1,2,32,768]{3,2,1,0:T(8,128)(2,1)S(1)}, bf16[1,2,32,768]{3,2,1,0:T(8,128)(2,1)S(1)}, u32[]{:S(2)}, u32[]{:S(2)}) %collective-permute-start.7) | collective-permute-done | bytes 98336 | tf_op jit(solution)/shard_map/ppermute | solution.py:67
  41.8 3.1 %collective-permute-start.12 = (bf16[2,2,32,768]{3,2,1,0:T(8,128)(2,1)S(1)}, bf16[2,2,32,768]{3,2,1,0:T(8,128)(2,1)S(1)}, u32[]{:S(2)}, u32[]{:S(2)}) collective-permute-start(bf16[2,2,32,768]{3,2,1,0:T(8,128)(2,1)S(1)} %pad_maximum_fusion.6), channel_id=1, source_target_pairs={{0,7},{1,2},{2,1},{3,4},{4,3},{5,6},{6,5},{7,0},{8,15},{9,10},{10,... | collective-permute-start | bytes 589832 | tf_op jit(solution)/shard_map/ppermute | solution.py:67
  44.9 2.9 %collective-permute-done.8 = bf16[2,2,32,768]{3,2,1,0:T(8,128)(2,1)S(1)} collective-permute-done((bf16[2,2,32,768]{3,2,1,0:T(8,128)(2,1)S(1)}, bf16[2,2,32,768]{3,2,1,0:T(8,128)(2,1)S(1)}, u32[]{:S(2)}, u32[]{:S(2)}) %collective-permute-start.8) | collective-permute-done | bytes 196640 | tf_op jit(solution)/shard_map/ppermute | solution.py:67
  47.9 2.7 %collective-permute-start.9 = (bf16[2,2,32,768]{3,2,1,0:T(8,128)(2,1)S(1)}, bf16[2,2,32,768]{3,2,1,0:T(8,128)(2,1)S(1)}, u32[]{:S(2)}, u32[]{:S(2)}) collective-permute-start(bf16[2,2,32,768]{3,2,1,0:T(8,128)(2,1)S(1)} %fusion.18), channel_id=1, source_target_pairs={{0,7},{1,2},{2,1},{3,4},{4,3},{5,6},{6,5},{7,0},{8,15},{9,10},{10,... | collective-permute-start | bytes 589832 | tf_op jit(solution)/shard_map/ppermute | solution.py:67
  50.7 4.2 %collective-permute-done.9 = bf16[2,2,32,768]{3,2,1,0:T(8,128)(2,1)S(1)} collective-permute-done((bf16[2,2,32,768]{3,2,1,0:T(8,128)(2,1)S(1)}, bf16[2,2,32,768]{3,2,1,0:T(8,128)(2,1)S(1)}, u32[]{:S(2)}, u32[]{:S(2)}) %collective-permute-start.9) | collective-permute-done | bytes 196640 | tf_op jit(solution)/shard_map/ppermute | solution.py:67
  55.0 2.9 %collective-permute-done.13 = bf16[2,2,32,768]{3,2,1,0:T(8,128)(2,1)S(1)} collective-permute-done((bf16[2,2,32,768]{3,2,1,0:T(8,128)(2,1)S(1)}, bf16[2,2,32,768]{3,2,1,0:T(8,128)(2,1)S(1)}, u32[]{:S(2)}, u32[]{:S(2)}) %collective-permute-start.13) | collective-permute-done | bytes 196640 | tf_op jit(solution)/shard_map/ppermute | solution.py:67
  57.9 1.1 collective-permute-start.14
  59.1 1.5 %collective-permute-done.10 = bf16[2,2,32,768]{3,2,1,0:T(8,128)(2,1)S(1)} collective-permute-done((bf16[2,2,32,768]{3,2,1,0:T(8,128)(2,1)S(1)}, bf16[2,2,32,768]{3,2,1,0:T(8,128)(2,1)S(1)}, u32[]{:S(2)}, u32[]{:S(2)}) %collective-permute-start.10) | collective-permute-done | bytes 196640 | tf_op jit(solution)/shard_map/ppermute | solution.py:67
  60.6 6.0 %collective-permute-done.14 = bf16[2,2,32,768]{3,2,1,0:T(8,128)(2,1)S(1)} collective-permute-done((bf16[2,2,32,768]{3,2,1,0:T(8,128)(2,1)S(1)}, bf16[2,2,32,768]{3,2,1,0:T(8,128)(2,1)S(1)}, u32[]{:S(2)}, u32[]{:S(2)}) %collective-permute-start.14) | collective-permute-done | bytes 196640 | tf_op jit(solution)/shard_map/ppermute | solution.py:67
  67.2 2.1 %collective-permute-start.16 = (bf16[2,2,32,768]{3,2,1,0:T(8,128)(2,1)S(1)}, bf16[2,2,32,768]{3,2,1,0:T(8,128)(2,1)S(1)}, u32[]{:S(2)}, u32[]{:S(2)}) collective-permute-start(bf16[2,2,32,768]{3,2,1,0:T(8,128)(2,1)S(1)} %pad_maximum_fusion.7), channel_id=1, source_target_pairs={{0,7},{1,2},{2,1},{3,4},{4,3},{5,6},{6,5},{7,0},{8,15},{9,10},{10,... | collective-permute-start | bytes 589832 | tf_op jit(solution)/shard_map/ppermute | solution.py:67
  69.5 5.5 %collective-permute-done.15 = bf16[2,2,32,768]{3,2,1,0:T(8,128)(2,1)S(1)} collective-permute-done((bf16[2,2,32,768]{3,2,1,0:T(8,128)(2,1)S(1)}, bf16[2,2,32,768]{3,2,1,0:T(8,128)(2,1)S(1)}, u32[]{:S(2)}, u32[]{:S(2)}) %collective-permute-start.15) | collective-permute-done | bytes 196640 | tf_op jit(solution)/shard_map/ppermute | solution.py:67
  75.0 0.9 collective-permute-start.17
  76.0 6.6 %collective-permute-done.18 = bf16[2,2,32,768]{3,2,1,0:T(8,128)(2,1)S(1)} collective-permute-done((bf16[2,2,32,768]{3,2,1,0:T(8,128)(2,1)S(1)}, bf16[2,2,32,768]{3,2,1,0:T(8,128)(2,1)S(1)}, u32[]{:S(2)}, u32[]{:S(2)}) %collective-permute-start.18) | collective-permute-done | bytes 196640 | tf_op jit(solution)/shard_map/ppermute | solution.py:67
  82.6 1.4 %collective-permute-start.20 = (bf16[2,2,32,768]{3,2,1,0:T(8,128)(2,1)S(1)}, bf16[2,2,32,768]{3,2,1,0:T(8,128)(2,1)S(1)}, u32[]{:S(2)}, u32[]{:S(2)}) collective-permute-start(bf16[2,2,32,768]{3,2,1,0:T(8,128)(2,1)S(1)} %collective-permute-done.17), channel_id=1, source_target_pairs={{0,7},{1,2},{2,1},{3,4},{4,3},{5,6},{6,5},{7,0},{8,15},{9,10},{10,... | collective-permute-start | bytes 589832 | tf_op jit(solution)/shard_map/ppermute | solution.py:67
  84.0 4.3 %collective-permute-done.19 = bf16[2,2,32,768]{3,2,1,0:T(8,128)(2,1)S(1)} collective-permute-done((bf16[2,2,32,768]{3,2,1,0:T(8,128)(2,1)S(1)}, bf16[2,2,32,768]{3,2,1,0:T(8,128)(2,1)S(1)}, u32[]{:S(2)}, u32[]{:S(2)}) %collective-permute-start.19) | collective-permute-done | bytes 196640 | tf_op jit(solution)/shard_map/ppermute | solution.py:67
  88.3 1.5 %collective-permute-start.22 = (bf16[1,2,32,768]{3,2,1,0:T(8,128)(2,1)S(1)}, bf16[1,2,32,768]{3,2,1,0:T(8,128)(2,1)S(1)}, u32[]{:S(2)}, u32[]{:S(2)}) collective-permute-start(bf16[1,2,32,768]{3,2,1,0:T(8,128)(2,1)S(1)} %slice.176), channel_id=1, source_target_pairs={{0,7},{1,2},{2,1},{3,4},{4,3},{5,6},{6,5},{7,0},{8,15},{9,10},{10,... | collective-permute-start | bytes 294920 | tf_op jit(solution)/shard_map/ppermute | solution.py:67
  90.4 3.8 %collective-permute-done.22 = bf16[1,2,32,768]{3,2,1,0:T(8,128)(2,1)S(1)} collective-permute-done((bf16[1,2,32,768]{3,2,1,0:T(8,128)(2,1)S(1)}, bf16[1,2,32,768]{3,2,1,0:T(8,128)(2,1)S(1)}, u32[]{:S(2)}, u32[]{:S(2)}) %collective-permute-start.22) | collective-permute-done | bytes 98336 | tf_op jit(solution)/shard_map/ppermute | solution.py:67
  94.6 0.8 convolution_convert_fusion
  97.8 0.8 fusion.55
  99.4 0.8 fusion.56
  100.5 1.4 %collective-permute-start.25 = (bf16[2,4,16,1536]{3,2,0,1:T(8,128)(2,1)S(1)}, bf16[2,4,16,1536]{3,2,0,1:T(8,128)(2,1)S(1)}, u32[]{:S(2)}, u32[]{:S(2)}) collective-permute-start(bf16[2,4,16,1536]{3,2,0,1:T(8,128)(2,1)S(1)} %pad_maximum_fusion.2), channel_id=1, source_target_pairs={{0,64},{8,24},{16,80},{24,8},{32,96},{40,56},{48,112},{56,40},{64,... | collective-permute-start | bytes 1179656 | tf_op jit(solution)/shard_map/ppermute | solution.py:59
  101.9 2.8 %collective-permute-start.26 = (bf16[2,4,16,1536]{3,2,0,1:T(8,128)(2,1)S(1)}, bf16[2,4,16,1536]{3,2,0,1:T(8,128)(2,1)S(1)}, u32[]{:S(2)}, u32[]{:S(2)}) collective-permute-start(bf16[2,4,16,1536]{3,2,0,1:T(8,128)(2,1)S(1)} %pad_maximum_fusion.3), channel_id=1, source_target_pairs={{0,128},{8,40},{16,144},{24,56},{32,160},{40,8},{48,176},{56,24},{... | collective-permute-start | bytes 1179656 | tf_op jit(solution)/shard_map/ppermute | solution.py:59
  105.5 2.8 %multiply_convert_fusion = bf16[768,1536]{1,0:T(8,128)(2,1)} fusion(bf16[512,768]{1,0:T(8,128)(2,1)S(1)} %bitcast.271, bf16[256,1536]{1,0:T(8,128)(2,1)S(1)} %get-tuple-element.25, bf16[256,1536]{1,0:T(8,128)(2,1)S(1)} %get-tuple-element.23), kind=kOutput, calls=%fused_computation | convolution fusion | flops 1213464576 | bytes 4718592 | tf_op jit(solution)/shard_map/dot_general | solution.py:31
  108.6 2.8 %multiply_convert_fusion.1 = bf16[1536,768]{1,0:T(8,128)(2,1)} fusion(bf16[512,768]{1,0:T(8,128)(2,1)S(1)} %bitcast.270, bf16[256,1536]{1,0:T(8,128)(2,1)S(1)} %get-tuple-element.26, bf16[256,1536]{1,0:T(8,128)(2,1)S(1)} %get-tuple-element.24), kind=kOutput, calls=%fused_computation.1 | convolution fusion | flops 1213464576 | bytes 4718592 | tf_op jit(solution)/shard_map/dot_general | solution.py:31
  111.4 3.4 %collective-permute-done.26 = bf16[2,4,16,1536]{3,2,0,1:T(8,128)(2,1)S(1)} collective-permute-done((bf16[2,4,16,1536]{3,2,0,1:T(8,128)(2,1)S(1)}, bf16[2,4,16,1536]{3,2,0,1:T(8,128)(2,1)S(1)}, u32[]{:S(2)}, u32[]{:S(2)}) %collective-permute-start.26) | collective-permute-done | bytes 393248 | tf_op jit(solution)/shard_map/ppermute | solution.py:59
  114.9 3.1 %collective-permute-done.27 = bf16[2,4,16,1536]{3,2,0,1:T(8,128)(2,1)S(1)} collective-permute-done((bf16[2,4,16,1536]{3,2,0,1:T(8,128)(2,1)S(1)}, bf16[2,4,16,1536]{3,2,0,1:T(8,128)(2,1)S(1)}, u32[]{:S(2)}, u32[]{:S(2)}) %collective-permute-start.27) | collective-permute-done | bytes 393248 | tf_op jit(solution)/shard_map/ppermute | solution.py:59
  118.2 1.3 %collective-permute-start.28 = (bf16[2,16,1536]{2,1,0:T(8,128)(2,1)S(1)}, bf16[2,16,1536]{2,1,0:T(8,128)(2,1)S(1)}, u32[]{:S(2)}, u32[]{:S(2)}) collective-permute-start(bf16[2,16,1536]{2,1,0:T(8,128)(2,1)S(1)} %get-tuple-element.71), channel_id=1, source_target_pairs={{0,16},{8,72},{16,0},{24,88},{32,48},{40,104},{48,32},{56,120},{64... | collective-permute-start | bytes 294920 | tf_op jit(solution)/shard_map/ppermute | solution.py:59
  119.5 2.1 %collective-permute-start.30 = (bf16[2,16,1536]{2,1,0:T(8,128)(2,1)S(1)}, bf16[2,16,1536]{2,1,0:T(8,128)(2,1)S(1)}, u32[]{:S(2)}, u32[]{:S(2)}) collective-permute-start(bf16[2,16,1536]{2,1,0:T(8,128)(2,1)S(1)} %get-tuple-element.72), channel_id=1, source_target_pairs={{0,48},{8,200},{16,32},{24,216},{32,16},{40,232},{48,0},{56,248},{... | collective-permute-start | bytes 294920 | tf_op jit(solution)/shard_map/ppermute | solution.py:59
  121.6 0.8 collective-permute-start.29
  123.0 1.2 collective-permute-done.30
  124.2 3.5 %collective-permute-done.29 = bf16[2,16,1536]{2,1,0:T(8,128)(2,1)S(1)} collective-permute-done((bf16[2,16,1536]{2,1,0:T(8,128)(2,1)S(1)}, bf16[2,16,1536]{2,1,0:T(8,128)(2,1)S(1)}, u32[]{:S(2)}, u32[]{:S(2)}) %collective-permute-start.29) | collective-permute-done | bytes 98336 | tf_op jit(solution)/shard_map/ppermute | solution.py:59
  (101 shorter events, 12.1 us)
Async XLA Ops:
  0.6 27.5 %copy-start = (bf16[1536,768]{1,0:T(8,128)(2,1)S(1)}, bf16[1536,768]{1,0:T(8,128)(2,1)}, u32[]{:S(2)}) copy-start(bf16[1536,768]{1,0:T(8,128)(2,1)} %param.6) | copy-start | bytes 7077892
  1.6 6.2 %collective-permute-start.1 = (bf16[2,16,1536]{2,1,0:T(8,128)(2,1)S(1)}, bf16[2,16,1536]{2,1,0:T(8,128)(2,1)S(1)}, u32[]{:S(2)}, u32[]{:S(2)}) collective-permute-start(bf16[2,16,1536]{2,1,0:T(8,128)(2,1)S(1)} %get-tuple-element.79), channel_id=1, source_target_pairs={{0,32},{8,136},{16,48},{24,152},{32,0},{40,168},{48,16},{56,184},{... | collective-permute-start | bytes 294920 | tf_op jit(solution)/shard_map/ppermute | solution.py:59
  4.0 4.6 %collective-permute-start = (bf16[2,16,1536]{2,1,0:T(8,128)(2,1)S(1)}, bf16[2,16,1536]{2,1,0:T(8,128)(2,1)S(1)}, u32[]{:S(2)}, u32[]{:S(2)}) collective-permute-start(bf16[2,16,1536]{2,1,0:T(8,128)(2,1)S(1)} %get-tuple-element.79), channel_id=1, source_target_pairs={{0,16},{8,72},{16,0},{24,88},{32,48},{40,104},{48,32},{56,120},{64... | collective-permute-start | bytes 294920 | tf_op jit(solution)/shard_map/ppermute | solution.py:59
  4.3 4.6 %collective-permute-start.2 = (bf16[2,16,1536]{2,1,0:T(8,128)(2,1)S(1)}, bf16[2,16,1536]{2,1,0:T(8,128)(2,1)S(1)}, u32[]{:S(2)}, u32[]{:S(2)}) collective-permute-start(bf16[2,16,1536]{2,1,0:T(8,128)(2,1)S(1)} %get-tuple-element.79), channel_id=1, source_target_pairs={{0,48},{8,200},{16,32},{24,216},{32,16},{40,232},{48,0},{56,248},{... | collective-permute-start | bytes 294920 | tf_op jit(solution)/shard_map/ppermute | solution.py:59
  9.8 9.6 %collective-permute-start.4 = (bf16[2,4,16,1536]{3,2,1,0:T(8,128)(2,1)}, bf16[2,4,16,1536]{3,2,1,0:T(8,128)(2,1)S(1)}, u32[]{:S(2)}, u32[]{:S(2)}) collective-permute-start(bf16[2,4,16,1536]{3,2,1,0:T(8,128)(2,1)} %get-tuple-element.75), channel_id=1, source_target_pairs={{0,128},{8,40},{16,144},{24,56},{32,160},{40,8},{48,176},{56,24},{... | collective-permute-start | bytes 1179656 | tf_op jit(solution)/shard_map/ppermute | solution.py:59
  13.0 10.9 %collective-permute-start.3 = (bf16[2,4,16,1536]{3,2,1,0:T(8,128)(2,1)}, bf16[2,4,16,1536]{3,2,1,0:T(8,128)(2,1)S(1)}, u32[]{:S(2)}, u32[]{:S(2)}) collective-permute-start(bf16[2,4,16,1536]{3,2,1,0:T(8,128)(2,1)} %get-tuple-element.75), channel_id=1, source_target_pairs={{0,64},{8,24},{16,80},{24,8},{32,96},{40,56},{48,112},{56,40},{64,... | collective-permute-start | bytes 1179656 | tf_op jit(solution)/shard_map/ppermute | solution.py:59
  13.6 10.2 %collective-permute-start.5 = (bf16[2,4,16,1536]{3,2,1,0:T(8,128)(2,1)}, bf16[2,4,16,1536]{3,2,1,0:T(8,128)(2,1)}, u32[]{:S(2)}, u32[]{:S(2)}) collective-permute-start(bf16[2,4,16,1536]{3,2,1,0:T(8,128)(2,1)} %get-tuple-element.75), channel_id=1, source_target_pairs={{0,192},{8,56},{16,208},{24,40},{32,224},{40,24},{48,240},{56,8},{... | collective-permute-start | bytes 1179656 | tf_op jit(solution)/shard_map/ppermute | solution.py:59
  25.0 1.1 copy-start.1
  25.1 2.2 %copy-start.3 = (bf16[768,1536]{1,0:T(8,128)(2,1)S(1)}, bf16[768,1536]{1,0:T(8,128)(2,1)}, u32[]{:S(2)}) copy-start(bf16[768,1536]{1,0:T(8,128)(2,1)} %param.8) | copy-start | bytes 7077892
  26.2 3.4 %collective-permute-start.6 = (bf16[2,256,1536]{2,1,0:T(8,128)(2,1)S(1)}, bf16[2,256,1536]{2,1,0:T(8,128)(2,1)S(1)}, u32[]{:S(2)}, u32[]{:S(2)}) collective-permute-start(bf16[2,256,1536]{2,1,0:T(8,128)(2,1)S(1)} %bitcast.260), channel_id=1, source_target_pairs={{0,8},{8,0},{16,24},{24,16},{32,40},{40,32},{48,56},{56,48},{64,72... | collective-permute-start | bytes 4718600 | tf_op jit(solution)/shard_map/ppermute | solution.py:63
  29.6 1.1 copy-start.5
  31.7 10.0 %collective-permute-start.11 = (bf16[1,2,32,768]{3,2,1,0:T(8,128)(2,1)S(1)}, bf16[1,2,32,768]{3,2,1,0:T(8,128)(2,1)S(1)}, u32[]{:S(2)}, u32[]{:S(2)}) collective-permute-start(bf16[1,2,32,768]{3,2,1,0:T(8,128)(2,1)S(1)} %pad_maximum_fusion.9), channel_id=1, source_target_pairs={{0,1},{1,0},{2,3},{3,2},{4,5},{5,4},{6,7},{7,6},{8,9},{9,8},{10,11... | collective-permute-start | bytes 294920 | tf_op jit(solution)/shard_map/ppermute | solution.py:67
  33.7 7.8 %collective-permute-start.7 = (bf16[1,2,32,768]{3,2,1,0:T(8,128)(2,1)S(1)}, bf16[1,2,32,768]{3,2,1,0:T(8,128)(2,1)S(1)}, u32[]{:S(2)}, u32[]{:S(2)}) collective-permute-start(bf16[1,2,32,768]{3,2,1,0:T(8,128)(2,1)S(1)} %pad_maximum_fusion.10), channel_id=1, source_target_pairs={{0,7},{1,2},{2,1},{3,4},{4,3},{5,6},{6,5},{7,0},{8,15},{9,10},{10,... | collective-permute-start | bytes 294920 | tf_op jit(solution)/shard_map/ppermute | solution.py:67
  41.6 6.2 %collective-permute-start.8 = (bf16[2,2,32,768]{3,2,1,0:T(8,128)(2,1)S(1)}, bf16[2,2,32,768]{3,2,1,0:T(8,128)(2,1)S(1)}, u32[]{:S(2)}, u32[]{:S(2)}) collective-permute-start(bf16[2,2,32,768]{3,2,1,0:T(8,128)(2,1)S(1)} %pad_maximum_fusion.5), channel_id=1, source_target_pairs={{0,1},{1,0},{2,3},{3,2},{4,5},{5,4},{6,7},{7,6},{8,9},{9,8},{10,11... | collective-permute-start | bytes 589832 | tf_op jit(solution)/shard_map/ppermute | solution.py:67
  41.8 8.7 %collective-permute-start.12 = (bf16[2,2,32,768]{3,2,1,0:T(8,128)(2,1)S(1)}, bf16[2,2,32,768]{3,2,1,0:T(8,128)(2,1)S(1)}, u32[]{:S(2)}, u32[]{:S(2)}) collective-permute-start(bf16[2,2,32,768]{3,2,1,0:T(8,128)(2,1)S(1)} %pad_maximum_fusion.6), channel_id=1, source_target_pairs={{0,7},{1,2},{2,1},{3,4},{4,3},{5,6},{6,5},{7,0},{8,15},{9,10},{10,... | collective-permute-start | bytes 589832 | tf_op jit(solution)/shard_map/ppermute | solution.py:67
  47.9 7.0 %collective-permute-start.9 = (bf16[2,2,32,768]{3,2,1,0:T(8,128)(2,1)S(1)}, bf16[2,2,32,768]{3,2,1,0:T(8,128)(2,1)S(1)}, u32[]{:S(2)}, u32[]{:S(2)}) collective-permute-start(bf16[2,2,32,768]{3,2,1,0:T(8,128)(2,1)S(1)} %fusion.18), channel_id=1, source_target_pairs={{0,7},{1,2},{2,1},{3,4},{4,3},{5,6},{6,5},{7,0},{8,15},{9,10},{10,... | collective-permute-start | bytes 589832 | tf_op jit(solution)/shard_map/ppermute | solution.py:67
  50.6 7.3 %collective-permute-start.13 = (bf16[2,2,32,768]{3,2,1,0:T(8,128)(2,1)S(1)}, bf16[2,2,32,768]{3,2,1,0:T(8,128)(2,1)S(1)}, u32[]{:S(2)}, u32[]{:S(2)}) collective-permute-start(bf16[2,2,32,768]{3,2,1,0:T(8,128)(2,1)S(1)} %fusion.20), channel_id=1, source_target_pairs={{0,1},{1,0},{2,3},{3,2},{4,5},{5,4},{6,7},{7,6},{8,9},{9,8},{10,11... | collective-permute-start | bytes 589832 | tf_op jit(solution)/shard_map/ppermute | solution.py:67
  54.9 11.8 %copy-start.7 = (f32[768]{0:T(1024)S(1)}, f32[768]{0:T(1024)}, u32[]{:S(2)}) copy-start(f32[768]{0:T(1024)} %param.7) | copy-start | bytes 9220
  54.9 5.8 %collective-permute-start.10 = (bf16[2,2,32,768]{3,2,1,0:T(8,128)(2,1)S(1)}, bf16[2,2,32,768]{3,2,1,0:T(8,128)(2,1)S(1)}, u32[]{:S(2)}, u32[]{:S(2)}) collective-permute-start(bf16[2,2,32,768]{3,2,1,0:T(8,128)(2,1)S(1)} %fusion.17), channel_id=1, source_target_pairs={{0,1},{1,0},{2,3},{3,2},{4,5},{5,4},{6,7},{7,6},{8,9},{9,8},{10,11... | collective-permute-start | bytes 589832 | tf_op jit(solution)/shard_map/ppermute | solution.py:67
  57.9 8.7 %collective-permute-start.14 = (bf16[2,2,32,768]{3,2,1,0:T(8,128)(2,1)S(1)}, bf16[2,2,32,768]{3,2,1,0:T(8,128)(2,1)S(1)}, u32[]{:S(2)}, u32[]{:S(2)}) collective-permute-start(bf16[2,2,32,768]{3,2,1,0:T(8,128)(2,1)S(1)} %fusion.19), channel_id=1, source_target_pairs={{0,7},{1,2},{2,1},{3,4},{4,3},{5,6},{6,5},{7,0},{8,15},{9,10},{10,... | collective-permute-start | bytes 589832 | tf_op jit(solution)/shard_map/ppermute | solution.py:67
  66.9 8.1 %collective-permute-start.15 = (bf16[2,2,32,768]{3,2,1,0:T(8,128)(2,1)S(1)}, bf16[2,2,32,768]{3,2,1,0:T(8,128)(2,1)S(1)}, u32[]{:S(2)}, u32[]{:S(2)}) collective-permute-start(bf16[2,2,32,768]{3,2,1,0:T(8,128)(2,1)S(1)} %pad_maximum_fusion.7), channel_id=1, source_target_pairs={{0,1},{1,0},{2,3},{3,2},{4,5},{5,4},{6,7},{7,6},{8,9},{9,8},{10,11... | collective-permute-start | bytes 589832 | tf_op jit(solution)/shard_map/ppermute | solution.py:67
  67.2 7.9 %collective-permute-start.16 = (bf16[2,2,32,768]{3,2,1,0:T(8,128)(2,1)S(1)}, bf16[2,2,32,768]{3,2,1,0:T(8,128)(2,1)S(1)}, u32[]{:S(2)}, u32[]{:S(2)}) collective-permute-start(bf16[2,2,32,768]{3,2,1,0:T(8,128)(2,1)S(1)} %pad_maximum_fusion.7), channel_id=1, source_target_pairs={{0,7},{1,2},{2,1},{3,4},{4,3},{5,6},{6,5},{7,0},{8,15},{9,10},{10,... | collective-permute-start | bytes 589832 | tf_op jit(solution)/shard_map/ppermute | solution.py:67
  75.0 7.6 %collective-permute-start.18 = (bf16[2,2,32,768]{3,2,1,0:T(8,128)(2,1)S(1)}, bf16[2,2,32,768]{3,2,1,0:T(8,128)(2,1)S(1)}, u32[]{:S(2)}, u32[]{:S(2)}) collective-permute-start(bf16[2,2,32,768]{3,2,1,0:T(8,128)(2,1)S(1)} %collective-permute-done.15), channel_id=1, source_target_pairs={{0,7},{1,2},{2,1},{3,4},{4,3},{5,6},{6,5},{7,0},{8,15},{9,10},{10,... | collective-permute-start | bytes 589832 | tf_op jit(solution)/shard_map/ppermute | solution.py:67
  75.0 7.6 %collective-permute-start.17 = (bf16[2,2,32,768]{3,2,1,0:T(8,128)(2,1)S(1)}, bf16[2,2,32,768]{3,2,1,0:T(8,128)(2,1)S(1)}, u32[]{:S(2)}, u32[]{:S(2)}) collective-permute-start(bf16[2,2,32,768]{3,2,1,0:T(8,128)(2,1)S(1)} %collective-permute-done.16), channel_id=1, source_target_pairs={{0,1},{1,0},{2,3},{3,2},{4,5},{5,4},{6,7},{7,6},{8,9},{9,8},{10,11... | collective-permute-start | bytes 589832 | tf_op jit(solution)/shard_map/ppermute | solution.py:67
  82.6 5.7 %collective-permute-start.19 = (bf16[2,2,32,768]{3,2,1,0:T(8,128)(2,1)S(1)}, bf16[2,2,32,768]{3,2,1,0:T(8,128)(2,1)S(1)}, u32[]{:S(2)}, u32[]{:S(2)}) collective-permute-start(bf16[2,2,32,768]{3,2,1,0:T(8,128)(2,1)S(1)} %collective-permute-done.18), channel_id=1, source_target_pairs={{0,1},{1,0},{2,3},{3,2},{4,5},{5,4},{6,7},{7,6},{8,9},{9,8},{10,11... | collective-permute-start | bytes 589832 | tf_op jit(solution)/shard_map/ppermute | solution.py:67
  82.6 7.1 %collective-permute-start.20 = (bf16[2,2,32,768]{3,2,1,0:T(8,128)(2,1)S(1)}, bf16[2,2,32,768]{3,2,1,0:T(8,128)(2,1)S(1)}, u32[]{:S(2)}, u32[]{:S(2)}) collective-permute-start(bf16[2,2,32,768]{3,2,1,0:T(8,128)(2,1)S(1)} %collective-permute-done.17), channel_id=1, source_target_pairs={{0,7},{1,2},{2,1},{3,4},{4,3},{5,6},{6,5},{7,0},{8,15},{9,10},{10,... | collective-permute-start | bytes 589832 | tf_op jit(solution)/shard_map/ppermute | solution.py:67
  88.3 5.9 %collective-permute-start.22 = (bf16[1,2,32,768]{3,2,1,0:T(8,128)(2,1)S(1)}, bf16[1,2,32,768]{3,2,1,0:T(8,128)(2,1)S(1)}, u32[]{:S(2)}, u32[]{:S(2)}) collective-permute-start(bf16[1,2,32,768]{3,2,1,0:T(8,128)(2,1)S(1)} %slice.176), channel_id=1, source_target_pairs={{0,7},{1,2},{2,1},{3,4},{4,3},{5,6},{6,5},{7,0},{8,15},{9,10},{10,... | collective-permute-start | bytes 294920 | tf_op jit(solution)/shard_map/ppermute | solution.py:67
  89.8 4.7 %collective-permute-start.21 = (bf16[1,2,32,768]{3,2,1,0:T(8,128)(2,1)S(1)}, bf16[1,2,32,768]{3,2,1,0:T(8,128)(2,1)S(1)}, u32[]{:S(2)}, u32[]{:S(2)}) collective-permute-start(bf16[1,2,32,768]{3,2,1,0:T(8,128)(2,1)S(1)} %slice.175), channel_id=1, source_target_pairs={{0,1},{1,0},{2,3},{3,2},{4,5},{5,4},{6,7},{7,6},{8,9},{9,8},{10,11... | collective-permute-start | bytes 294920 | tf_op jit(solution)/shard_map/ppermute | solution.py:67
  94.6 1.7 %copy-start.4 = (bf16[768,1536]{1,0:T(8,128)(2,1)S(1)}, bf16[768,1536]{1,0:T(8,128)(2,1)}, u32[]{:S(2)}) copy-start(bf16[768,1536]{1,0:T(8,128)(2,1)} %param.8) | copy-start | bytes 7077892
  95.4 2.4 %collective-permute-start.24 = (bf16[256,1536]{1,0:T(8,128)(2,1)S(1)}, bf16[256,1536]{1,0:T(8,128)(2,1)S(1)}, u32[]{:S(2)}, u32[]{:S(2)}) collective-permute-start(bf16[256,1536]{1,0:T(8,128)(2,1)S(1)} %convolution_convert_fusion), channel_id=1, source_target_pairs={{0,8},{8,0},{16,24},{24,16},{32,40},{40,32},{48,56},{56,48},{64,72... | collective-permute-start | bytes 2359304 | tf_op jit(solution)/shard_map/ppermute | solution.py:63
  97.0 2.4 %collective-permute-start.23 = (bf16[256,1536]{1,0:T(8,128)(2,1)S(1)}, bf16[256,1536]{1,0:T(8,128)(2,1)S(1)}, u32[]{:S(2)}, u32[]{:S(2)}) collective-permute-start(bf16[256,1536]{1,0:T(8,128)(2,1)S(1)} %convolution_convert_fusion.1), channel_id=1, source_target_pairs={{0,8},{8,0},{16,24},{24,16},{32,40},{40,32},{48,56},{56,48},{64,72... | collective-permute-start | bytes 2359304 | tf_op jit(solution)/shard_map/ppermute | solution.py:63
  100.4 4.9 %copy-start.2 = (bf16[2,4,4,16,1536]{4,3,2,1,0:T(8,128)(2,1)S(1)}, bf16[2,4,4,16,1536]{4,3,2,1,0:T(8,128)(2,1)}, u32[]{:S(2)}) copy-start(bf16[2,4,4,16,1536]{4,3,2,1,0:T(8,128)(2,1)} %copy-done.1) | copy-start | bytes 4718596
  100.5 4.9 %copy-start.6 = (bf16[2,256,1536]{2,1,0:T(8,128)(2,1)S(1)}, bf16[2,256,1536]{2,1,0:T(8,128)(2,1)}, u32[]{:S(2)}) copy-start(bf16[2,256,1536]{2,1,0:T(8,128)(2,1)} %copy-done.5) | copy-start | bytes 4718596
  100.5 10.9 %collective-permute-start.25 = (bf16[2,4,16,1536]{3,2,0,1:T(8,128)(2,1)S(1)}, bf16[2,4,16,1536]{3,2,0,1:T(8,128)(2,1)S(1)}, u32[]{:S(2)}, u32[]{:S(2)}) collective-permute-start(bf16[2,4,16,1536]{3,2,0,1:T(8,128)(2,1)S(1)} %pad_maximum_fusion.2), channel_id=1, source_target_pairs={{0,64},{8,24},{16,80},{24,8},{32,96},{40,56},{48,112},{56,40},{64,... | collective-permute-start | bytes 1179656 | tf_op jit(solution)/shard_map/ppermute | solution.py:59
  101.9 12.9 %collective-permute-start.26 = (bf16[2,4,16,1536]{3,2,0,1:T(8,128)(2,1)S(1)}, bf16[2,4,16,1536]{3,2,0,1:T(8,128)(2,1)S(1)}, u32[]{:S(2)}, u32[]{:S(2)}) collective-permute-start(bf16[2,4,16,1536]{3,2,0,1:T(8,128)(2,1)S(1)} %pad_maximum_fusion.3), channel_id=1, source_target_pairs={{0,128},{8,40},{16,144},{24,56},{32,160},{40,8},{48,176},{56,24},{... | collective-permute-start | bytes 1179656 | tf_op jit(solution)/shard_map/ppermute | solution.py:59
  104.8 13.2 %collective-permute-start.27 = (bf16[2,4,16,1536]{3,2,0,1:T(8,128)(2,1)S(1)}, bf16[2,4,16,1536]{3,2,0,1:T(8,128)(2,1)S(1)}, u32[]{:S(2)}, u32[]{:S(2)}) collective-permute-start(bf16[2,4,16,1536]{3,2,0,1:T(8,128)(2,1)S(1)} %pad_maximum_fusion.4), channel_id=1, source_target_pairs={{0,192},{8,56},{16,208},{24,40},{32,224},{40,24},{48,240},{56,8},{... | collective-permute-start | bytes 1179656 | tf_op jit(solution)/shard_map/ppermute | solution.py:59
  118.2 4.8 %collective-permute-start.28 = (bf16[2,16,1536]{2,1,0:T(8,128)(2,1)S(1)}, bf16[2,16,1536]{2,1,0:T(8,128)(2,1)S(1)}, u32[]{:S(2)}, u32[]{:S(2)}) collective-permute-start(bf16[2,16,1536]{2,1,0:T(8,128)(2,1)S(1)} %get-tuple-element.71), channel_id=1, source_target_pairs={{0,16},{8,72},{16,0},{24,88},{32,48},{40,104},{48,32},{56,120},{64... | collective-permute-start | bytes 294920 | tf_op jit(solution)/shard_map/ppermute | solution.py:59
  119.5 4.7 %collective-permute-start.30 = (bf16[2,16,1536]{2,1,0:T(8,128)(2,1)S(1)}, bf16[2,16,1536]{2,1,0:T(8,128)(2,1)S(1)}, u32[]{:S(2)}, u32[]{:S(2)}) collective-permute-start(bf16[2,16,1536]{2,1,0:T(8,128)(2,1)S(1)} %get-tuple-element.72), channel_id=1, source_target_pairs={{0,48},{8,200},{16,32},{24,216},{32,16},{40,232},{48,0},{56,248},{... | collective-permute-start | bytes 294920 | tf_op jit(solution)/shard_map/ppermute | solution.py:59
  121.6 6.1 %collective-permute-start.29 = (bf16[2,16,1536]{2,1,0:T(8,128)(2,1)S(1)}, bf16[2,16,1536]{2,1,0:T(8,128)(2,1)S(1)}, u32[]{:S(2)}, u32[]{:S(2)}) collective-permute-start(bf16[2,16,1536]{2,1,0:T(8,128)(2,1)S(1)} %get-tuple-element.73), channel_id=1, source_target_pairs={{0,32},{8,136},{16,48},{24,152},{32,0},{40,168},{48,16},{56,184},{... | collective-permute-start | bytes 294920 | tf_op jit(solution)/shard_map/ppermute | solution.py:59

commit v2 on v1

--- a/solution.py
+++ b/solution.py
@@ -76,7 +76,7 @@
 
     mine = jnp.stack([activations, cotangent])
     got = {k: plane_swap(mine, k, True) for k in (2, 1, 3)}
-    line = jnp.stack([mine, got[1], got[2], got[3]], axis=1)
+    line = lax.optimization_barrier(jnp.stack([mine, got[1], got[2], got[3]], axis=1))
     got = {k: plane_swap(line, k, False) for k in (2, 1, 3)}
     own = jnp.stack([line, got[1], got[2], got[3]], axis=1).reshape(2, HALF, features)
     other = swap_cores(own)
@@ -98,6 +98,9 @@
     other_parts = first_products(other)
     from_odd = col_swap(part([other_parts], 4).astype(BF16), True)
     halves = [own_parts, other_parts]
+    from_even, own, other = lax.optimization_barrier((from_even, own, other))
+    all_inputs = jnp.concatenate([own[0], other[0]])
+    all_grads = jnp.concatenate([own[1], other[1]])
     to_odd = jnp.concatenate([part([own_parts], -3) + from_even.astype(F32), part([other_parts], -3)])
     to_even = jnp.concatenate([part([own_parts], 3), part([other_parts], 3) + from_odd.astype(F32)])
     for j in (2, 1):
@@ -109,6 +112,7 @@
     from_even = col_swap(to_even.astype(BF16), False)
     total = part(halves, 0) + from_even.astype(F32) + from_odd.astype(F32)
 
+    total, all_inputs, all_grads = lax.optimization_barrier((total, all_inputs, all_grads))
     hidden_mine, slope = gelu_and_slope(total[:, 0] + bias_in)
     both = jnp.stack([hidden_mine.astype(BF16), (total[:, 1] * slope).astype(BF16)], axis=1)
 
@@ -131,7 +135,7 @@
         jnp.stack([x.reshape(4, 4, 16, features)[k] for x in (kept_out, kept_grad)]) for k in range(4)
     ]
     sent = [x.astype(BF16) for x in kept[1:]]
-    everything, own, other, *sent = lax.optimization_barrier((everything, own, other, *sent))
+    everything, all_inputs, all_grads, *sent = lax.optimization_barrier((everything, all_inputs, all_grads, *sent))
     came = {k: plane_swap(sent[k - 1], k, False) for k in (2, 1, 3)}
     plane_sum = kept[0]
     for k in (1, 2, 3):
@@ -144,8 +148,6 @@
 
     hidden = everything[:, 0].reshape(TOKENS, hidden_here)
     pre_grad = everything[:, 1].reshape(TOKENS, hidden_here)
-    all_inputs = jnp.concatenate([own[0], other[0]])
-    all_grads = jnp.concatenate([own[1], other[1]])
     bias_grad = jnp.sum(pre_grad.astype(F32), axis=0) * grad_scale
     w_out_grad = (contract_rows(hidden, all_grads) * grad_scale).astype(BF16)
     w_in_grad = (contract_rows(all_inputs, pre_grad) * grad_scale).astype(BF16)

time: 129 us -> 127 us (0.984)
  waiting for transfers between devices: 66.7 us -> 64 us
  other arithmetic: 4.83 us -> 6.51 us
    concatenate x0 -> x2, other arithmetic: none -> 2.49 us  [the longest x1 1.25 us: local(): all_grads = jnp.concatenate([own[1], other[1]])]
    ppermute x16, waiting for transfers between devices: 40.7 us -> 38.6 us  [col_swap(): lax.ppermute(values, 'col', [(i, ring_partner(i, 8, odd_links)) for i in...]
    unnamed x16 -> x12, local copies, waits for them, and re-layouts: 3.22 us -> 3.35 us
  transfers between devices with their start and end apart: 31 -> 31, of which waited for: 23 -> 23; matrix products, arithmetic and copies ran while one was open for 8% -> 10% of each run, Pallas kernels for 0% -> 0%
where the time goes in v2:
time: 127 us
  waiting for transfers between devices  64 us (50%)
  starting transfers between devices  38.2 us (30%)
  matrix products  12 us (9%)
  other arithmetic  6.51 us (5%)
  local copies, waits for them, and re-layouts  5.21 us (4%)
    ppermute x16, waiting for transfers between devices, col_swap(): lax.ppermute(values, 'col', [(i, ring_partner(i, 8, odd_links)) for i in...  38.6 us
    ppermute x12, waiting for transfers between devices, plane_swap(): return lax.ppermute(values, 'row', pairs)  23.9 us
    ppermute x16, starting transfers between devices, col_swap(): lax.ppermute(values, 'col', [(i, ring_partner(i, 8, odd_links)) for i in...  20.6 us
    ppermute x12, starting transfers between devices, plane_swap(): return lax.ppermute(values, 'row', pairs)  17.3 us
    dot_general x2, matrix products, contract_rows(): lax.dot_general(left, right, (((0,), (0,)), ((), ())), preferred_element_...  5.66 us
    unnamed x12, local copies, waits for them, and re-layouts  3.35 us
    dot_general x4, matrix products, contract_cols(): lax.dot_general(left, right, (((1,), (1,)), ((), ())), preferred_element_...  3.24 us
    dot_general x4, matrix products, matmul(): return jnp.dot(left, right, preferred_element_type=F32)  3.09 us
  transfers between devices with their start and end apart: 31, of which 23 were waited for; matrix products, arithmetic and copies ran while one was open for 10% of the time, Pallas kernels for 0%

profile of v2, /device:TPU:4, one launch (start us, length us, event | category | flops | bytes accessed | tf_op | source)
XLA Modules:
  0.0 127.1 jit_solution(11615115871712627283)
XLA Ops:
  0.6 1.0 fusion.39
  1.6 2.3 %collective-permute-start.1 = (bf16[2,16,1536]{2,1,0:T(8,128)(2,1)S(1)}, bf16[2,16,1536]{2,1,0:T(8,128)(2,1)S(1)}, u32[]{:S(2)}, u32[]{:S(2)}) collective-permute-start(bf16[2,16,1536]{2,1,0:T(8,128)(2,1)S(1)} %get-tuple-element.89), channel_id=1, source_target_pairs={{0,32},{8,136},{16,48},{24,152},{32,0},{40,168},{48,16},{56,184},{... | collective-permute-start | bytes 294920 | tf_op jit(solution)/shard_map/ppermute | solution.py:59
  4.3 1.5 %collective-permute-start.2 = (bf16[2,16,1536]{2,1,0:T(8,128)(2,1)S(1)}, bf16[2,16,1536]{2,1,0:T(8,128)(2,1)S(1)}, u32[]{:S(2)}, u32[]{:S(2)}) collective-permute-start(bf16[2,16,1536]{2,1,0:T(8,128)(2,1)S(1)} %get-tuple-element.89), channel_id=1, source_target_pairs={{0,48},{8,200},{16,32},{24,216},{32,16},{40,232},{48,0},{56,248},{... | collective-permute-start | bytes 294920 | tf_op jit(solution)/shard_map/ppermute | solution.py:59
  5.8 2.0 %collective-permute-done.1 = bf16[2,16,1536]{2,1,0:T(8,128)(2,1)S(1)} collective-permute-done((bf16[2,16,1536]{2,1,0:T(8,128)(2,1)S(1)}, bf16[2,16,1536]{2,1,0:T(8,128)(2,1)S(1)}, u32[]{:S(2)}, u32[]{:S(2)}) %collective-permute-start.1) | collective-permute-done | bytes 98336 | tf_op jit(solution)/shard_map/ppermute | solution.py:59
  9.0 3.1 %collective-permute-start.5 = (bf16[2,4,16,1536]{3,2,1,0:T(8,128)(2,1)S(1)}, bf16[2,4,16,1536]{3,2,1,0:T(8,128)(2,1)S(1)}, u32[]{:S(2)}, u32[]{:S(2)}) collective-permute-start(bf16[2,4,16,1536]{3,2,1,0:T(8,128)(2,1)S(1)} %pad_maximum_fusion.3), channel_id=1, source_target_pairs={{0,192},{8,56},{16,208},{24,40},{32,224},{40,24},{48,240},{56,8},{... | collective-permute-start | bytes 1179656 | tf_op jit(solution)/shard_map/ppermute | solution.py:59
  13.2 9.1 %collective-permute-done.5 = bf16[2,4,16,1536]{3,2,1,0:T(8,128)(2,1)S(1)} collective-permute-done((bf16[2,4,16,1536]{3,2,1,0:T(8,128)(2,1)S(1)}, bf16[2,4,16,1536]{3,2,1,0:T(8,128)(2,1)S(1)}, u32[]{:S(2)}, u32[]{:S(2)}) %collective-permute-start.5) | collective-permute-done | bytes 393248 | tf_op jit(solution)/shard_map/ppermute | solution.py:59
  22.3 1.0 collective-permute-done.3
  23.3 1.2 pad_maximum_fusion
  24.8 1.4 %copy-done.1 = bf16[768,1536]{1,0:T(8,128)(2,1)S(1)} copy-done((bf16[768,1536]{1,0:T(8,128)(2,1)S(1)}, bf16[768,1536]{1,0:T(8,128)(2,1)}, u32[]{:S(2)}) %copy-start.1) | copy-done | bytes 2359320
  26.2 0.8 fusion.49
  27.0 0.8 fusion.48
  28.2 0.8 fusion.2
  29.0 0.8 fusion.4
  29.9 2.0 %collective-permute-start.11 = (bf16[1,2,32,768]{3,2,1,0:T(8,128)(2,1)S(1)}, bf16[1,2,32,768]{3,2,1,0:T(8,128)(2,1)S(1)}, u32[]{:S(2)}, u32[]{:S(2)}) collective-permute-start(bf16[1,2,32,768]{3,2,1,0:T(8,128)(2,1)S(1)} %pad_maximum_fusion.11), channel_id=1, source_target_pairs={{0,1},{1,0},{2,3},{3,2},{4,5},{5,4},{6,7},{7,6},{8,9},{9,8},{10,11... | collective-permute-start | bytes 294920 | tf_op jit(solution)/shard_map/ppermute | solution.py:67
  31.9 5.0 %collective-permute-start.7 = (bf16[1,2,32,768]{3,2,1,0:T(8,128)(2,1)S(1)}, bf16[1,2,32,768]{3,2,1,0:T(8,128)(2,1)S(1)}, u32[]{:S(2)}, u32[]{:S(2)}) collective-permute-start(bf16[1,2,32,768]{3,2,1,0:T(8,128)(2,1)S(1)} %pad_maximum_fusion.12), channel_id=1, source_target_pairs={{0,7},{1,2},{2,1},{3,4},{4,3},{5,6},{6,5},{7,0},{8,15},{9,10},{10,... | collective-permute-start | bytes 294920 | tf_op jit(solution)/shard_map/ppermute | solution.py:67
  37.1 2.7 %collective-permute-done.7 = bf16[1,2,32,768]{3,2,1,0:T(8,128)(2,1)S(1)} collective-permute-done((bf16[1,2,32,768]{3,2,1,0:T(8,128)(2,1)S(1)}, bf16[1,2,32,768]{3,2,1,0:T(8,128)(2,1)S(1)}, u32[]{:S(2)}, u32[]{:S(2)}) %collective-permute-start.7) | collective-permute-done | bytes 98336 | tf_op jit(solution)/shard_map/ppermute | solution.py:67
  40.0 3.1 %collective-permute-start.12 = (bf16[2,2,32,768]{3,2,1,0:T(8,128)(2,1)S(1)}, bf16[2,2,32,768]{3,2,1,0:T(8,128)(2,1)S(1)}, u32[]{:S(2)}, u32[]{:S(2)}) collective-permute-start(bf16[2,2,32,768]{3,2,1,0:T(8,128)(2,1)S(1)} %pad_maximum_fusion.8), channel_id=1, source_target_pairs={{0,7},{1,2},{2,1},{3,4},{4,3},{5,6},{6,5},{7,0},{8,15},{9,10},{10,... | collective-permute-start | bytes 589832 | tf_op jit(solution)/shard_map/ppermute | solution.py:67
  43.3 1.2 pad_maximum_fusion.2
  44.5 1.5 %collective-permute-done.8 = bf16[2,2,32,768]{3,2,1,0:T(8,128)(2,1)S(1)} collective-permute-done((bf16[2,2,32,768]{3,2,1,0:T(8,128)(2,1)S(1)}, bf16[2,2,32,768]{3,2,1,0:T(8,128)(2,1)S(1)}, u32[]{:S(2)}, u32[]{:S(2)}) %collective-permute-start.8) | collective-permute-done | bytes 196640 | tf_op jit(solution)/shard_map/ppermute | solution.py:67
  46.1 2.6 %collective-permute-start.9 = (bf16[2,2,32,768]{3,2,1,0:T(8,128)(2,1)S(1)}, bf16[2,2,32,768]{3,2,1,0:T(8,128)(2,1)S(1)}, u32[]{:S(2)}, u32[]{:S(2)}) collective-permute-start(bf16[2,2,32,768]{3,2,1,0:T(8,128)(2,1)S(1)} %fusion.12), channel_id=1, source_target_pairs={{0,7},{1,2},{2,1},{3,4},{4,3},{5,6},{6,5},{7,0},{8,15},{9,10},{10,... | collective-permute-start | bytes 589832 | tf_op jit(solution)/shard_map/ppermute | solution.py:67
  48.9 4.2 %collective-permute-done.9 = bf16[2,2,32,768]{3,2,1,0:T(8,128)(2,1)S(1)} collective-permute-done((bf16[2,2,32,768]{3,2,1,0:T(8,128)(2,1)S(1)}, bf16[2,2,32,768]{3,2,1,0:T(8,128)(2,1)S(1)}, u32[]{:S(2)}, u32[]{:S(2)}) %collective-permute-start.9) | collective-permute-done | bytes 196640 | tf_op jit(solution)/shard_map/ppermute | solution.py:67
  53.2 2.9 %collective-permute-done.13 = bf16[2,2,32,768]{3,2,1,0:T(8,128)(2,1)S(1)} collective-permute-done((bf16[2,2,32,768]{3,2,1,0:T(8,128)(2,1)S(1)}, bf16[2,2,32,768]{3,2,1,0:T(8,128)(2,1)S(1)}, u32[]{:S(2)}, u32[]{:S(2)}) %collective-permute-start.13) | collective-permute-done | bytes 196640 | tf_op jit(solution)/shard_map/ppermute | solution.py:67
  56.1 1.3 %collective-permute-start.14 = (bf16[2,2,32,768]{3,2,1,0:T(8,128)(2,1)S(1)}, bf16[2,2,32,768]{3,2,1,0:T(8,128)(2,1)S(1)}, u32[]{:S(2)}, u32[]{:S(2)}) collective-permute-start(bf16[2,2,32,768]{3,2,1,0:T(8,128)(2,1)S(1)} %fusion.13), channel_id=1, source_target_pairs={{0,7},{1,2},{2,1},{3,4},{4,3},{5,6},{6,5},{7,0},{8,15},{9,10},{10,... | collective-permute-start | bytes 589832 | tf_op jit(solution)/shard_map/ppermute | solution.py:67
  57.5 1.2 pad_maximum_fusion.1
  58.8 6.5 %collective-permute-done.14 = bf16[2,2,32,768]{3,2,1,0:T(8,128)(2,1)S(1)} collective-permute-done((bf16[2,2,32,768]{3,2,1,0:T(8,128)(2,1)S(1)}, bf16[2,2,32,768]{3,2,1,0:T(8,128)(2,1)S(1)}, u32[]{:S(2)}, u32[]{:S(2)}) %collective-permute-start.14) | collective-permute-done | bytes 196640 | tf_op jit(solution)/shard_map/ppermute | solution.py:67
  65.7 2.0 %collective-permute-start.16 = (bf16[2,2,32,768]{3,2,1,0:T(8,128)(2,1)S(1)}, bf16[2,2,32,768]{3,2,1,0:T(8,128)(2,1)S(1)}, u32[]{:S(2)}, u32[]{:S(2)}) collective-permute-start(bf16[2,2,32,768]{3,2,1,0:T(8,128)(2,1)S(1)} %pad_maximum_fusion.9), channel_id=1, source_target_pairs={{0,7},{1,2},{2,1},{3,4},{4,3},{5,6},{6,5},{7,0},{8,15},{9,10},{10,... | collective-permute-start | bytes 589832 | tf_op jit(solution)/shard_map/ppermute | solution.py:67
  67.9 5.5 %collective-permute-done.15 = bf16[2,2,32,768]{3,2,1,0:T(8,128)(2,1)S(1)} collective-permute-done((bf16[2,2,32,768]{3,2,1,0:T(8,128)(2,1)S(1)}, bf16[2,2,32,768]{3,2,1,0:T(8,128)(2,1)S(1)}, u32[]{:S(2)}, u32[]{:S(2)}) %collective-permute-start.15) | collective-permute-done | bytes 196640 | tf_op jit(solution)/shard_map/ppermute | solution.py:67
  73.5 1.0 collective-permute-start.17
  74.5 6.7 %collective-permute-done.18 = bf16[2,2,32,768]{3,2,1,0:T(8,128)(2,1)S(1)} collective-permute-done((bf16[2,2,32,768]{3,2,1,0:T(8,128)(2,1)S(1)}, bf16[2,2,32,768]{3,2,1,0:T(8,128)(2,1)S(1)}, u32[]{:S(2)}, u32[]{:S(2)}) %collective-permute-start.18) | collective-permute-done | bytes 196640 | tf_op jit(solution)/shard_map/ppermute | solution.py:67
  81.3 1.4 %collective-permute-start.20 = (bf16[2,2,32,768]{3,2,1,0:T(8,128)(2,1)S(1)}, bf16[2,2,32,768]{3,2,1,0:T(8,128)(2,1)S(1)}, u32[]{:S(2)}, u32[]{:S(2)}) collective-permute-start(bf16[2,2,32,768]{3,2,1,0:T(8,128)(2,1)S(1)} %collective-permute-done.17), channel_id=1, source_target_pairs={{0,7},{1,2},{2,1},{3,4},{4,3},{5,6},{6,5},{7,0},{8,15},{9,10},{10,... | collective-permute-start | bytes 589832 | tf_op jit(solution)/shard_map/ppermute | solution.py:67
  82.7 4.2 %collective-permute-done.19 = bf16[2,2,32,768]{3,2,1,0:T(8,128)(2,1)S(1)} collective-permute-done((bf16[2,2,32,768]{3,2,1,0:T(8,128)(2,1)S(1)}, bf16[2,2,32,768]{3,2,1,0:T(8,128)(2,1)S(1)}, u32[]{:S(2)}, u32[]{:S(2)}) %collective-permute-start.19) | collective-permute-done | bytes 196640 | tf_op jit(solution)/shard_map/ppermute | solution.py:67
  86.9 0.8 collective-permute-start.22
  88.2 0.9 collective-permute-start.21
  89.1 3.8 %collective-permute-done.22 = bf16[1,2,32,768]{3,2,1,0:T(8,128)(2,1)S(1)} collective-permute-done((bf16[1,2,32,768]{3,2,1,0:T(8,128)(2,1)S(1)}, bf16[1,2,32,768]{3,2,1,0:T(8,128)(2,1)S(1)}, u32[]{:S(2)}, u32[]{:S(2)}) %collective-permute-start.22) | collective-permute-done | bytes 98336 | tf_op jit(solution)/shard_map/ppermute | solution.py:67
  93.0 0.8 convolution_convert_fusion
  96.2 0.8 fusion.46
  97.8 0.8 fusion.47
  98.9 1.7 %collective-permute-start.25 = (bf16[2,4,16,1536]{3,2,0,1:T(8,128)(2,1)S(1)}, bf16[2,4,16,1536]{3,2,0,1:T(8,128)(2,1)S(1)}, u32[]{:S(2)}, u32[]{:S(2)}) collective-permute-start(bf16[2,4,16,1536]{3,2,0,1:T(8,128)(2,1)S(1)} %pad_maximum_fusion.4), channel_id=1, source_target_pairs={{0,64},{8,24},{16,80},{24,8},{32,96},{40,56},{48,112},{56,40},{64,... | collective-permute-start | bytes 1179656 | tf_op jit(solution)/shard_map/ppermute | solution.py:59
  100.5 2.9 %collective-permute-start.26 = (bf16[2,4,16,1536]{3,2,0,1:T(8,128)(2,1)S(1)}, bf16[2,4,16,1536]{3,2,0,1:T(8,128)(2,1)S(1)}, u32[]{:S(2)}, u32[]{:S(2)}) collective-permute-start(bf16[2,4,16,1536]{3,2,0,1:T(8,128)(2,1)S(1)} %pad_maximum_fusion.5), channel_id=1, source_target_pairs={{0,128},{8,40},{16,144},{24,56},{32,160},{40,8},{48,176},{56,24},{... | collective-permute-start | bytes 1179656 | tf_op jit(solution)/shard_map/ppermute | solution.py:59
  103.7 2.8 %multiply_convert_fusion = bf16[768,1536]{1,0:T(8,128)(2,1)} fusion(bf16[512,768]{1,0:T(8,128)(2,1)S(1)} %bitcast.273, bf16[512,1536]{1,0:T(8,128)(2,1)S(1)} %copy-done.3), kind=kOutput, calls=%fused_computation | convolution fusion | flops 1210318848 | bytes 4718592 | tf_op jit(solution)/shard_map/dot_general | solution.py:31
  106.7 1.2 copy-done.4
  107.9 2.8 %multiply_convert_fusion.1 = bf16[1536,768]{1,0:T(8,128)(2,1)} fusion(bf16[512,1536]{1,0:T(8,128)(2,1)S(1)} %copy-done.4, bf16[512,768]{1,0:T(8,128)(2,1)S(1)} %bitcast.272), kind=kOutput, calls=%fused_computation.1 | convolution fusion | flops 1210318848 | bytes 4718592 | tf_op jit(solution)/shard_map/dot_general | solution.py:31
  110.7 2.8 %collective-permute-done.26 = bf16[2,4,16,1536]{3,2,0,1:T(8,128)(2,1)S(1)} collective-permute-done((bf16[2,4,16,1536]{3,2,0,1:T(8,128)(2,1)S(1)}, bf16[2,4,16,1536]{3,2,0,1:T(8,128)(2,1)S(1)}, u32[]{:S(2)}, u32[]{:S(2)}) %collective-permute-start.26) | collective-permute-done | bytes 393248 | tf_op jit(solution)/shard_map/ppermute | solution.py:59
  113.5 3.1 %collective-permute-done.27 = bf16[2,4,16,1536]{3,2,0,1:T(8,128)(2,1)S(1)} collective-permute-done((bf16[2,4,16,1536]{3,2,0,1:T(8,128)(2,1)S(1)}, bf16[2,4,16,1536]{3,2,0,1:T(8,128)(2,1)S(1)}, u32[]{:S(2)}, u32[]{:S(2)}) %collective-permute-start.27) | collective-permute-done | bytes 393248 | tf_op jit(solution)/shard_map/ppermute | solution.py:59
  116.9 1.3 %collective-permute-start.28 = (bf16[2,16,1536]{2,1,0:T(8,128)(2,1)S(1)}, bf16[2,16,1536]{2,1,0:T(8,128)(2,1)S(1)}, u32[]{:S(2)}, u32[]{:S(2)}) collective-permute-start(bf16[2,16,1536]{2,1,0:T(8,128)(2,1)S(1)} %get-tuple-element.83), channel_id=1, source_target_pairs={{0,16},{8,72},{16,0},{24,88},{32,48},{40,104},{48,32},{56,120},{64... | collective-permute-start | bytes 294920 | tf_op jit(solution)/shard_map/ppermute | solution.py:59
  118.2 2.1 %collective-permute-start.30 = (bf16[2,16,1536]{2,1,0:T(8,128)(2,1)S(1)}, bf16[2,16,1536]{2,1,0:T(8,128)(2,1)S(1)}, u32[]{:S(2)}, u32[]{:S(2)}) collective-permute-start(bf16[2,16,1536]{2,1,0:T(8,128)(2,1)S(1)} %get-tuple-element.84), channel_id=1, source_target_pairs={{0,48},{8,200},{16,32},{24,216},{32,16},{40,232},{48,0},{56,248},{... | collective-permute-start | bytes 294920 | tf_op jit(solution)/shard_map/ppermute | solution.py:59
  121.7 1.2 collective-permute-done.30
  122.9 3.5 %collective-permute-done.29 = bf16[2,16,1536]{2,1,0:T(8,128)(2,1)S(1)} collective-permute-done((bf16[2,16,1536]{2,1,0:T(8,128)(2,1)S(1)}, bf16[2,16,1536]{2,1,0:T(8,128)(2,1)S(1)}, u32[]{:S(2)}, u32[]{:S(2)}) %collective-permute-start.29) | collective-permute-done | bytes 98336 | tf_op jit(solution)/shard_map/ppermute | solution.py:59
  (98 shorter events, 11.4 us)
Async XLA Ops:
  0.6 26.4 %copy-start = (bf16[1536,768]{1,0:T(8,128)(2,1)S(1)}, bf16[1536,768]{1,0:T(8,128)(2,1)}, u32[]{:S(2)}) copy-start(bf16[1536,768]{1,0:T(8,128)(2,1)} %param.6) | copy-start | bytes 7077892
  1.6 6.2 %collective-permute-start.1 = (bf16[2,16,1536]{2,1,0:T(8,128)(2,1)S(1)}, bf16[2,16,1536]{2,1,0:T(8,128)(2,1)S(1)}, u32[]{:S(2)}, u32[]{:S(2)}) collective-permute-start(bf16[2,16,1536]{2,1,0:T(8,128)(2,1)S(1)} %get-tuple-element.89), channel_id=1, source_target_pairs={{0,32},{8,136},{16,48},{24,152},{32,0},{40,168},{48,16},{56,184},{... | collective-permute-start | bytes 294920 | tf_op jit(solution)/shard_map/ppermute | solution.py:59
  4.0 4.6 %collective-permute-start = (bf16[2,16,1536]{2,1,0:T(8,128)(2,1)S(1)}, bf16[2,16,1536]{2,1,0:T(8,128)(2,1)S(1)}, u32[]{:S(2)}, u32[]{:S(2)}) collective-permute-start(bf16[2,16,1536]{2,1,0:T(8,128)(2,1)S(1)} %get-tuple-element.89), channel_id=1, source_target_pairs={{0,16},{8,72},{16,0},{24,88},{32,48},{40,104},{48,32},{56,120},{64... | collective-permute-start | bytes 294920 | tf_op jit(solution)/shard_map/ppermute | solution.py:59
  4.3 4.6 %collective-permute-start.2 = (bf16[2,16,1536]{2,1,0:T(8,128)(2,1)S(1)}, bf16[2,16,1536]{2,1,0:T(8,128)(2,1)S(1)}, u32[]{:S(2)}, u32[]{:S(2)}) collective-permute-start(bf16[2,16,1536]{2,1,0:T(8,128)(2,1)S(1)} %get-tuple-element.89), channel_id=1, source_target_pairs={{0,48},{8,200},{16,32},{24,216},{32,16},{40,232},{48,0},{56,248},{... | collective-permute-start | bytes 294920 | tf_op jit(solution)/shard_map/ppermute | solution.py:59
  9.0 13.3 %collective-permute-start.5 = (bf16[2,4,16,1536]{3,2,1,0:T(8,128)(2,1)S(1)}, bf16[2,4,16,1536]{3,2,1,0:T(8,128)(2,1)S(1)}, u32[]{:S(2)}, u32[]{:S(2)}) collective-permute-start(bf16[2,4,16,1536]{3,2,1,0:T(8,128)(2,1)S(1)} %pad_maximum_fusion.3), channel_id=1, source_target_pairs={{0,192},{8,56},{16,208},{24,40},{32,224},{40,24},{48,240},{56,8},{... | collective-permute-start | bytes 1179656 | tf_op jit(solution)/shard_map/ppermute | solution.py:59
  12.1 10.2 %collective-permute-start.4 = (bf16[2,4,16,1536]{3,2,1,0:T(8,128)(2,1)S(1)}, bf16[2,4,16,1536]{3,2,1,0:T(8,128)(2,1)S(1)}, u32[]{:S(2)}, u32[]{:S(2)}) collective-permute-start(bf16[2,4,16,1536]{3,2,1,0:T(8,128)(2,1)S(1)} %pad_maximum_fusion.3), channel_id=1, source_target_pairs={{0,128},{8,40},{16,144},{24,56},{32,160},{40,8},{48,176},{56,24},{... | collective-permute-start | bytes 1179656 | tf_op jit(solution)/shard_map/ppermute | solution.py:59
  12.7 10.6 %collective-permute-start.3 = (bf16[2,4,16,1536]{3,2,1,0:T(8,128)(2,1)S(1)}, bf16[2,4,16,1536]{3,2,1,0:T(8,128)(2,1)}, u32[]{:S(2)}, u32[]{:S(2)}) collective-permute-start(bf16[2,4,16,1536]{3,2,1,0:T(8,128)(2,1)S(1)} %pad_maximum_fusion.3), channel_id=1, source_target_pairs={{0,64},{8,24},{16,80},{24,8},{32,96},{40,56},{48,112},{56,40},{64,... | collective-permute-start | bytes 1179656 | tf_op jit(solution)/shard_map/ppermute | solution.py:59
  24.5 1.7 %copy-start.1 = (bf16[768,1536]{1,0:T(8,128)(2,1)S(1)}, bf16[768,1536]{1,0:T(8,128)(2,1)}, u32[]{:S(2)}) copy-start(bf16[768,1536]{1,0:T(8,128)(2,1)} %param.8) | copy-start | bytes 7077892
  24.7 3.5 %collective-permute-start.6 = (bf16[2,256,1536]{2,1,0:T(8,128)(2,1)S(1)}, bf16[2,256,1536]{2,1,0:T(8,128)(2,1)S(1)}, u32[]{:S(2)}, u32[]{:S(2)}) collective-permute-start(bf16[2,256,1536]{2,1,0:T(8,128)(2,1)S(1)} %bitcast.261), channel_id=1, source_target_pairs={{0,8},{8,0},{16,24},{24,16},{32,40},{40,32},{48,56},{56,48},{64,72... | collective-permute-start | bytes 4718600 | tf_op jit(solution)/shard_map/ppermute | solution.py:63
  29.9 7.2 %collective-permute-start.11 = (bf16[1,2,32,768]{3,2,1,0:T(8,128)(2,1)S(1)}, bf16[1,2,32,768]{3,2,1,0:T(8,128)(2,1)S(1)}, u32[]{:S(2)}, u32[]{:S(2)}) collective-permute-start(bf16[1,2,32,768]{3,2,1,0:T(8,128)(2,1)S(1)} %pad_maximum_fusion.11), channel_id=1, source_target_pairs={{0,1},{1,0},{2,3},{3,2},{4,5},{5,4},{6,7},{7,6},{8,9},{9,8},{10,11... | collective-permute-start | bytes 294920 | tf_op jit(solution)/shard_map/ppermute | solution.py:67
  31.9 7.8 %collective-permute-start.7 = (bf16[1,2,32,768]{3,2,1,0:T(8,128)(2,1)S(1)}, bf16[1,2,32,768]{3,2,1,0:T(8,128)(2,1)S(1)}, u32[]{:S(2)}, u32[]{:S(2)}) collective-permute-start(bf16[1,2,32,768]{3,2,1,0:T(8,128)(2,1)S(1)} %pad_maximum_fusion.12), channel_id=1, source_target_pairs={{0,7},{1,2},{2,1},{3,4},{4,3},{5,6},{6,5},{7,0},{8,15},{9,10},{10,... | collective-permute-start | bytes 294920 | tf_op jit(solution)/shard_map/ppermute | solution.py:67
  39.8 6.2 %collective-permute-start.8 = (bf16[2,2,32,768]{3,2,1,0:T(8,128)(2,1)S(1)}, bf16[2,2,32,768]{3,2,1,0:T(8,128)(2,1)S(1)}, u32[]{:S(2)}, u32[]{:S(2)}) collective-permute-start(bf16[2,2,32,768]{3,2,1,0:T(8,128)(2,1)S(1)} %pad_maximum_fusion.7), channel_id=1, source_target_pairs={{0,1},{1,0},{2,3},{3,2},{4,5},{5,4},{6,7},{7,6},{8,9},{9,8},{10,11... | collective-permute-start | bytes 589832 | tf_op jit(solution)/shard_map/ppermute | solution.py:67
  40.0 8.7 %collective-permute-start.12 = (bf16[2,2,32,768]{3,2,1,0:T(8,128)(2,1)S(1)}, bf16[2,2,32,768]{3,2,1,0:T(8,128)(2,1)S(1)}, u32[]{:S(2)}, u32[]{:S(2)}) collective-permute-start(bf16[2,2,32,768]{3,2,1,0:T(8,128)(2,1)S(1)} %pad_maximum_fusion.8), channel_id=1, source_target_pairs={{0,7},{1,2},{2,1},{3,4},{4,3},{5,6},{6,5},{7,0},{8,15},{9,10},{10,... | collective-permute-start | bytes 589832 | tf_op jit(solution)/shard_map/ppermute | solution.py:67
  46.1 7.0 %collective-permute-start.9 = (bf16[2,2,32,768]{3,2,1,0:T(8,128)(2,1)S(1)}, bf16[2,2,32,768]{3,2,1,0:T(8,128)(2,1)S(1)}, u32[]{:S(2)}, u32[]{:S(2)}) collective-permute-start(bf16[2,2,32,768]{3,2,1,0:T(8,128)(2,1)S(1)} %fusion.12), channel_id=1, source_target_pairs={{0,7},{1,2},{2,1},{3,4},{4,3},{5,6},{6,5},{7,0},{8,15},{9,10},{10,... | collective-permute-start | bytes 589832 | tf_op jit(solution)/shard_map/ppermute | solution.py:67
  48.8 7.3 %collective-permute-start.13 = (bf16[2,2,32,768]{3,2,1,0:T(8,128)(2,1)S(1)}, bf16[2,2,32,768]{3,2,1,0:T(8,128)(2,1)S(1)}, u32[]{:S(2)}, u32[]{:S(2)}) collective-permute-start(bf16[2,2,32,768]{3,2,1,0:T(8,128)(2,1)S(1)} %fusion.14), channel_id=1, source_target_pairs={{0,1},{1,0},{2,3},{3,2},{4,5},{5,4},{6,7},{7,6},{8,9},{9,8},{10,11... | collective-permute-start | bytes 589832 | tf_op jit(solution)/shard_map/ppermute | solution.py:67
  53.1 5.8 %collective-permute-start.10 = (bf16[2,2,32,768]{3,2,1,0:T(8,128)(2,1)S(1)}, bf16[2,2,32,768]{3,2,1,0:T(8,128)(2,1)S(1)}, u32[]{:S(2)}, u32[]{:S(2)}) collective-permute-start(bf16[2,2,32,768]{3,2,1,0:T(8,128)(2,1)S(1)} %fusion.11), channel_id=1, source_target_pairs={{0,1},{1,0},{2,3},{3,2},{4,5},{5,4},{6,7},{7,6},{8,9},{9,8},{10,11... | collective-permute-start | bytes 589832 | tf_op jit(solution)/shard_map/ppermute | solution.py:67
  56.1 9.2 %collective-permute-start.14 = (bf16[2,2,32,768]{3,2,1,0:T(8,128)(2,1)S(1)}, bf16[2,2,32,768]{3,2,1,0:T(8,128)(2,1)S(1)}, u32[]{:S(2)}, u32[]{:S(2)}) collective-permute-start(bf16[2,2,32,768]{3,2,1,0:T(8,128)(2,1)S(1)} %fusion.13), channel_id=1, source_target_pairs={{0,7},{1,2},{2,1},{3,4},{4,3},{5,6},{6,5},{7,0},{8,15},{9,10},{10,... | collective-permute-start | bytes 589832 | tf_op jit(solution)/shard_map/ppermute | solution.py:67
  57.5 7.9 %copy-start.5 = (f32[768]{0:T(1024)S(1)}, f32[768]{0:T(1024)}, u32[]{:S(2)}) copy-start(f32[768]{0:T(1024)} %param.7) | copy-start | bytes 9220
  65.6 7.9 %collective-permute-start.15 = (bf16[2,2,32,768]{3,2,1,0:T(8,128)(2,1)S(1)}, bf16[2,2,32,768]{3,2,1,0:T(8,128)(2,1)S(1)}, u32[]{:S(2)}, u32[]{:S(2)}) collective-permute-start(bf16[2,2,32,768]{3,2,1,0:T(8,128)(2,1)S(1)} %pad_maximum_fusion.9), channel_id=1, source_target_pairs={{0,1},{1,0},{2,3},{3,2},{4,5},{5,4},{6,7},{7,6},{8,9},{9,8},{10,11... | collective-permute-start | bytes 589832 | tf_op jit(solution)/shard_map/ppermute | solution.py:67
  65.7 7.8 %collective-permute-start.16 = (bf16[2,2,32,768]{3,2,1,0:T(8,128)(2,1)S(1)}, bf16[2,2,32,768]{3,2,1,0:T(8,128)(2,1)S(1)}, u32[]{:S(2)}, u32[]{:S(2)}) collective-permute-start(bf16[2,2,32,768]{3,2,1,0:T(8,128)(2,1)S(1)} %pad_maximum_fusion.9), channel_id=1, source_target_pairs={{0,7},{1,2},{2,1},{3,4},{4,3},{5,6},{6,5},{7,0},{8,15},{9,10},{10,... | collective-permute-start | bytes 589832 | tf_op jit(solution)/shard_map/ppermute | solution.py:67
  73.5 7.8 %collective-permute-start.18 = (bf16[2,2,32,768]{3,2,1,0:T(8,128)(2,1)S(1)}, bf16[2,2,32,768]{3,2,1,0:T(8,128)(2,1)S(1)}, u32[]{:S(2)}, u32[]{:S(2)}) collective-permute-start(bf16[2,2,32,768]{3,2,1,0:T(8,128)(2,1)S(1)} %collective-permute-done.15), channel_id=1, source_target_pairs={{0,7},{1,2},{2,1},{3,4},{4,3},{5,6},{6,5},{7,0},{8,15},{9,10},{10,... | collective-permute-start | bytes 589832 | tf_op jit(solution)/shard_map/ppermute | solution.py:67
  73.5 7.8 %collective-permute-start.17 = (bf16[2,2,32,768]{3,2,1,0:T(8,128)(2,1)S(1)}, bf16[2,2,32,768]{3,2,1,0:T(8,128)(2,1)S(1)}, u32[]{:S(2)}, u32[]{:S(2)}) collective-permute-start(bf16[2,2,32,768]{3,2,1,0:T(8,128)(2,1)S(1)} %collective-permute-done.16), channel_id=1, source_target_pairs={{0,1},{1,0},{2,3},{3,2},{4,5},{5,4},{6,7},{7,6},{8,9},{9,8},{10,11... | collective-permute-start | bytes 589832 | tf_op jit(solution)/shard_map/ppermute | solution.py:67
  81.3 5.7 %collective-permute-start.19 = (bf16[2,2,32,768]{3,2,1,0:T(8,128)(2,1)S(1)}, bf16[2,2,32,768]{3,2,1,0:T(8,128)(2,1)S(1)}, u32[]{:S(2)}, u32[]{:S(2)}) collective-permute-start(bf16[2,2,32,768]{3,2,1,0:T(8,128)(2,1)S(1)} %collective-permute-done.18), channel_id=1, source_target_pairs={{0,1},{1,0},{2,3},{3,2},{4,5},{5,4},{6,7},{7,6},{8,9},{9,8},{10,11... | collective-permute-start | bytes 589832 | tf_op jit(solution)/shard_map/ppermute | solution.py:67
  81.3 6.9 %collective-permute-start.20 = (bf16[2,2,32,768]{3,2,1,0:T(8,128)(2,1)S(1)}, bf16[2,2,32,768]{3,2,1,0:T(8,128)(2,1)S(1)}, u32[]{:S(2)}, u32[]{:S(2)}) collective-permute-start(bf16[2,2,32,768]{3,2,1,0:T(8,128)(2,1)S(1)} %collective-permute-done.17), channel_id=1, source_target_pairs={{0,7},{1,2},{2,1},{3,4},{4,3},{5,6},{6,5},{7,0},{8,15},{9,10},{10,... | collective-permute-start | bytes 589832 | tf_op jit(solution)/shard_map/ppermute | solution.py:67
  86.9 5.9 %collective-permute-start.22 = (bf16[1,2,32,768]{3,2,1,0:T(8,128)(2,1)S(1)}, bf16[1,2,32,768]{3,2,1,0:T(8,128)(2,1)S(1)}, u32[]{:S(2)}, u32[]{:S(2)}) collective-permute-start(bf16[1,2,32,768]{3,2,1,0:T(8,128)(2,1)S(1)} %slice.174), channel_id=1, source_target_pairs={{0,7},{1,2},{2,1},{3,4},{4,3},{5,6},{6,5},{7,0},{8,15},{9,10},{10,... | collective-permute-start | bytes 294920 | tf_op jit(solution)/shard_map/ppermute | solution.py:67
  88.2 4.7 %collective-permute-start.21 = (bf16[1,2,32,768]{3,2,1,0:T(8,128)(2,1)S(1)}, bf16[1,2,32,768]{3,2,1,0:T(8,128)(2,1)S(1)}, u32[]{:S(2)}, u32[]{:S(2)}) collective-permute-start(bf16[1,2,32,768]{3,2,1,0:T(8,128)(2,1)S(1)} %slice.173), channel_id=1, source_target_pairs={{0,1},{1,0},{2,3},{3,2},{4,5},{5,4},{6,7},{7,6},{8,9},{9,8},{10,11... | collective-permute-start | bytes 294920 | tf_op jit(solution)/shard_map/ppermute | solution.py:67
  93.0 1.7 %copy-start.2 = (bf16[768,1536]{1,0:T(8,128)(2,1)S(1)}, bf16[768,1536]{1,0:T(8,128)(2,1)}, u32[]{:S(2)}) copy-start(bf16[768,1536]{1,0:T(8,128)(2,1)} %param.8) | copy-start | bytes 7077892
  93.8 2.4 %collective-permute-start.24 = (bf16[256,1536]{1,0:T(8,128)(2,1)S(1)}, bf16[256,1536]{1,0:T(8,128)(2,1)S(1)}, u32[]{:S(2)}, u32[]{:S(2)}) collective-permute-start(bf16[256,1536]{1,0:T(8,128)(2,1)S(1)} %convolution_convert_fusion), channel_id=1, source_target_pairs={{0,8},{8,0},{16,24},{24,16},{32,40},{40,32},{48,56},{56,48},{64,72... | collective-permute-start | bytes 2359304 | tf_op jit(solution)/shard_map/ppermute | solution.py:63
  95.4 2.4 %collective-permute-start.23 = (bf16[256,1536]{1,0:T(8,128)(2,1)S(1)}, bf16[256,1536]{1,0:T(8,128)(2,1)S(1)}, u32[]{:S(2)}, u32[]{:S(2)}) collective-permute-start(bf16[256,1536]{1,0:T(8,128)(2,1)S(1)} %convolution_convert_fusion.1), channel_id=1, source_target_pairs={{0,8},{8,0},{16,24},{24,16},{32,40},{40,32},{48,56},{56,48},{64,72... | collective-permute-start | bytes 2359304 | tf_op jit(solution)/shard_map/ppermute | solution.py:63
  98.8 4.9 %copy-start.3 = (bf16[512,1536]{1,0:T(8,128)(2,1)S(1)}, bf16[512,1536]{1,0:T(8,128)(2,1)}, u32[]{:S(2)}) copy-start(bf16[512,1536]{1,0:T(8,128)(2,1)} %pad_maximum_fusion.2) | copy-start | bytes 4718596
  98.9 11.9 %collective-permute-start.25 = (bf16[2,4,16,1536]{3,2,0,1:T(8,128)(2,1)S(1)}, bf16[2,4,16,1536]{3,2,0,1:T(8,128)(2,1)S(1)}, u32[]{:S(2)}, u32[]{:S(2)}) collective-permute-start(bf16[2,4,16,1536]{3,2,0,1:T(8,128)(2,1)S(1)} %pad_maximum_fusion.4), channel_id=1, source_target_pairs={{0,64},{8,24},{16,80},{24,8},{32,96},{40,56},{48,112},{56,40},{64,... | collective-permute-start | bytes 1179656 | tf_op jit(solution)/shard_map/ppermute | solution.py:59
  100.5 13.0 %collective-permute-start.26 = (bf16[2,4,16,1536]{3,2,0,1:T(8,128)(2,1)S(1)}, bf16[2,4,16,1536]{3,2,0,1:T(8,128)(2,1)S(1)}, u32[]{:S(2)}, u32[]{:S(2)}) collective-permute-start(bf16[2,4,16,1536]{3,2,0,1:T(8,128)(2,1)S(1)} %pad_maximum_fusion.5), channel_id=1, source_target_pairs={{0,128},{8,40},{16,144},{24,56},{32,160},{40,8},{48,176},{56,24},{... | collective-permute-start | bytes 1179656 | tf_op jit(solution)/shard_map/ppermute | solution.py:59
  103.4 13.2 %collective-permute-start.27 = (bf16[2,4,16,1536]{3,2,0,1:T(8,128)(2,1)S(1)}, bf16[2,4,16,1536]{3,2,0,1:T(8,128)(2,1)S(1)}, u32[]{:S(2)}, u32[]{:S(2)}) collective-permute-start(bf16[2,4,16,1536]{3,2,0,1:T(8,128)(2,1)S(1)} %pad_maximum_fusion.6), channel_id=1, source_target_pairs={{0,192},{8,56},{16,208},{24,40},{32,224},{40,24},{48,240},{56,8},{... | collective-permute-start | bytes 1179656 | tf_op jit(solution)/shard_map/ppermute | solution.py:59
  106.5 1.4 %copy-start.4 = (bf16[512,1536]{1,0:T(8,128)(2,1)S(1)}, bf16[512,1536]{1,0:T(8,128)(2,1)}, u32[]{:S(2)}) copy-start(bf16[512,1536]{1,0:T(8,128)(2,1)} %pad_maximum_fusion.1) | copy-start | bytes 4718596
  116.9 4.8 %collective-permute-start.28 = (bf16[2,16,1536]{2,1,0:T(8,128)(2,1)S(1)}, bf16[2,16,1536]{2,1,0:T(8,128)(2,1)S(1)}, u32[]{:S(2)}, u32[]{:S(2)}) collective-permute-start(bf16[2,16,1536]{2,1,0:T(8,128)(2,1)S(1)} %get-tuple-element.83), channel_id=1, source_target_pairs={{0,16},{8,72},{16,0},{24,88},{32,48},{40,104},{48,32},{56,120},{64... | collective-permute-start | bytes 294920 | tf_op jit(solution)/shard_map/ppermute | solution.py:59
  118.2 4.7 %collective-permute-start.30 = (bf16[2,16,1536]{2,1,0:T(8,128)(2,1)S(1)}, bf16[2,16,1536]{2,1,0:T(8,128)(2,1)S(1)}, u32[]{:S(2)}, u32[]{:S(2)}) collective-permute-start(bf16[2,16,1536]{2,1,0:T(8,128)(2,1)S(1)} %get-tuple-element.84), channel_id=1, source_target_pairs={{0,48},{8,200},{16,32},{24,216},{32,16},{40,232},{48,0},{56,248},{... | collective-permute-start | bytes 294920 | tf_op jit(solution)/shard_map/ppermute | solution.py:59
  120.3 6.1 %collective-permute-start.29 = (bf16[2,16,1536]{2,1,0:T(8,128)(2,1)S(1)}, bf16[2,16,1536]{2,1,0:T(8,128)(2,1)S(1)}, u32[]{:S(2)}, u32[]{:S(2)}) collective-permute-start(bf16[2,16,1536]{2,1,0:T(8,128)(2,1)S(1)} %get-tuple-element.85), channel_id=1, source_target_pairs={{0,32},{8,136},{16,48},{24,152},{32,0},{40,168},{48,16},{56,184},{... | collective-permute-start | bytes 294920 | tf_op jit(solution)/shard_map/ppermute | solution.py:59

commit v3 on v2

--- a/solution.py
+++ b/solution.py
@@ -78,11 +78,16 @@
     got = {k: plane_swap(mine, k, True) for k in (2, 1, 3)}
     line = lax.optimization_barrier(jnp.stack([mine, got[1], got[2], got[3]], axis=1))
     got = {k: plane_swap(line, k, False) for k in (2, 1, 3)}
-    own = jnp.stack([line, got[1], got[2], got[3]], axis=1).reshape(2, HALF, features)
+    own = jnp.zeros((2, 4, 4, 16, features), BF16)
+    for k, piece in ((0, line), (2, got[2]), (1, got[1]), (3, got[3])):
+        own = lax.dynamic_update_slice_in_dim(own, piece[:, None], k, 1)
+    own = own.reshape(2, HALF, features)
     other = swap_cores(own)
 
     def first_products(tokens):
-        return matmul(tokens[0], w_in), contract_cols(tokens[1], w_out)
+        pre = matmul(tokens[0], w_in)
+        pre, grads = lax.optimization_barrier((pre, tokens[1]))
+        return pre, contract_cols(grads, w_out)
 
     own_parts = first_products(own)
 

time: 127 us -> 125 us (0.984)
    ppermute x12, waiting for transfers between devices: 23.9 us -> 22.5 us  [plane_swap(): return lax.ppermute(values, 'row', pairs)]
  transfers between devices with their start and end apart: 31 -> 31, of which waited for: 23 -> 23; matrix products, arithmetic and copies ran while one was open for 10% -> 11% of each run, Pallas kernels for 0% -> 0%
where the time goes in v3:
time: 125 us
  waiting for transfers between devices  63.2 us (51%)
  starting transfers between devices  38.4 us (31%)
  matrix products  12 us (10%)
  other arithmetic  5.32 us (4%)
  local copies, waits for them, and re-layouts  5.1 us (4%)
    ppermute x16, waiting for transfers between devices, col_swap(): lax.ppermute(values, 'col', [(i, ring_partner(i, 8, odd_links)) for i in...  38.6 us
    ppermute x12, waiting for transfers between devices, plane_swap(): return lax.ppermute(values, 'row', pairs)  22.5 us
    ppermute x16, starting transfers between devices, col_swap(): lax.ppermute(values, 'col', [(i, ring_partner(i, 8, odd_links)) for i in...  20.6 us
    ppermute x12, starting transfers between devices, plane_swap(): return lax.ppermute(values, 'row', pairs)  17.5 us
    dot_general x2, matrix products, contract_rows(): lax.dot_general(left, right, (((0,), (0,)), ((), ())), preferred_element_...  5.66 us
    dot_general x4, matrix products, contract_cols(): lax.dot_general(left, right, (((1,), (1,)), ((), ())), preferred_element_...  3.23 us
    dot_general x4, matrix products, matmul(): return jnp.dot(left, right, preferred_element_type=F32)  3.09 us
    unnamed x12, local copies, waits for them, and re-layouts  2.83 us
  transfers between devices with their start and end apart: 31, of which 23 were waited for; matrix products, arithmetic and copies ran while one was open for 11% of the time, Pallas kernels for 0%

profile of v3, /device:TPU:4, one launch (start us, length us, event | category | flops | bytes accessed | tf_op | source)
XLA Modules:
  0.0 125.2 jit_solution(3627780014604495693)
XLA Ops:
  0.6 1.0 fusion.36
  1.6 2.3 %collective-permute-start.1 = (bf16[2,16,1536]{2,1,0:T(8,128)(2,1)S(1)}, bf16[2,16,1536]{2,1,0:T(8,128)(2,1)S(1)}, u32[]{:S(2)}, u32[]{:S(2)}) collective-permute-start(bf16[2,16,1536]{2,1,0:T(8,128)(2,1)S(1)} %get-tuple-element.97), channel_id=1, source_target_pairs={{0,32},{8,136},{16,48},{24,152},{32,0},{40,168},{48,16},{56,184},{... | collective-permute-start | bytes 294920 | tf_op jit(solution)/shard_map/ppermute | solution.py:59
  4.3 1.5 %collective-permute-start.2 = (bf16[2,16,1536]{2,1,0:T(8,128)(2,1)S(1)}, bf16[2,16,1536]{2,1,0:T(8,128)(2,1)S(1)}, u32[]{:S(2)}, u32[]{:S(2)}) collective-permute-start(bf16[2,16,1536]{2,1,0:T(8,128)(2,1)S(1)} %get-tuple-element.97), channel_id=1, source_target_pairs={{0,48},{8,200},{16,32},{24,216},{32,16},{40,232},{48,0},{56,248},{... | collective-permute-start | bytes 294920 | tf_op jit(solution)/shard_map/ppermute | solution.py:59
  5.8 2.0 %collective-permute-done.1 = bf16[2,16,1536]{2,1,0:T(8,128)(2,1)S(1)} collective-permute-done((bf16[2,16,1536]{2,1,0:T(8,128)(2,1)S(1)}, bf16[2,16,1536]{2,1,0:T(8,128)(2,1)S(1)}, u32[]{:S(2)}, u32[]{:S(2)}) %collective-permute-start.1) | collective-permute-done | bytes 98336 | tf_op jit(solution)/shard_map/ppermute | solution.py:59
  9.0 3.3 %collective-permute-start.3 = (bf16[2,4,16,1536]{3,2,1,0:T(8,128)(2,1)S(1)}, bf16[2,4,16,1536]{3,2,1,0:T(8,128)(2,1)S(1)}, u32[]{:S(2)}, u32[]{:S(2)}) collective-permute-start(bf16[2,4,16,1536]{3,2,1,0:T(8,128)(2,1)S(1)} %pad_maximum_fusion.2), channel_id=1, source_target_pairs={{0,128},{8,40},{16,144},{24,56},{32,160},{40,8},{48,176},{56,24},{... | collective-permute-start | bytes 1179656 | tf_op jit(solution)/shard_map/ppermute | solution.py:59
  12.3 1.1 collective-permute-start.5
  13.5 5.0 %collective-permute-done.3 = bf16[2,4,16,1536]{3,2,1,0:T(8,128)(2,1)S(1)} collective-permute-done((bf16[2,4,16,1536]{3,2,1,0:T(8,128)(2,1)S(1)}, bf16[2,4,16,1536]{3,2,1,0:T(8,128)(2,1)S(1)}, u32[]{:S(2)}, u32[]{:S(2)}) %collective-permute-start.3) | collective-permute-done | bytes 393248 | tf_op jit(solution)/shard_map/ppermute | solution.py:59
  18.5 4.5 %collective-permute-done.4 = bf16[2,4,16,1536]{3,2,1,0:T(8,128)(2,1)S(1)} collective-permute-done((bf16[2,4,16,1536]{3,2,1,0:T(8,128)(2,1)S(1)}, bf16[2,4,16,1536]{3,2,1,0:T(8,128)(2,1)S(1)}, u32[]{:S(2)}, u32[]{:S(2)}) %collective-permute-start.4) | collective-permute-done | bytes 393248 | tf_op jit(solution)/shard_map/ppermute | solution.py:59
  23.5 0.8 fusion.45
  24.2 0.9 copy-done.1
  25.1 0.8 fusion.46
  27.7 0.8 fusion.47
  28.6 2.0 %collective-permute-start.11 = (bf16[1,2,32,768]{3,2,1,0:T(8,128)(2,1)S(1)}, bf16[1,2,32,768]{3,2,1,0:T(8,128)(2,1)S(1)}, u32[]{:S(2)}, u32[]{:S(2)}) collective-permute-start(bf16[1,2,32,768]{3,2,1,0:T(8,128)(2,1)S(1)} %pad_maximum_fusion.10), channel_id=1, source_target_pairs={{0,1},{1,0},{2,3},{3,2},{4,5},{5,4},{6,7},{7,6},{8,9},{9,8},{10,11... | collective-permute-start | bytes 294920 | tf_op jit(solution)/shard_map/ppermute | solution.py:67
  30.7 5.0 %collective-permute-start.7 = (bf16[1,2,32,768]{3,2,1,0:T(8,128)(2,1)S(1)}, bf16[1,2,32,768]{3,2,1,0:T(8,128)(2,1)S(1)}, u32[]{:S(2)}, u32[]{:S(2)}) collective-permute-start(bf16[1,2,32,768]{3,2,1,0:T(8,128)(2,1)S(1)} %pad_maximum_fusion.11), channel_id=1, source_target_pairs={{0,7},{1,2},{2,1},{3,4},{4,3},{5,6},{6,5},{7,0},{8,15},{9,10},{10,... | collective-permute-start | bytes 294920 | tf_op jit(solution)/shard_map/ppermute | solution.py:67
  35.8 2.7 %collective-permute-done.7 = bf16[1,2,32,768]{3,2,1,0:T(8,128)(2,1)S(1)} collective-permute-done((bf16[1,2,32,768]{3,2,1,0:T(8,128)(2,1)S(1)}, bf16[1,2,32,768]{3,2,1,0:T(8,128)(2,1)S(1)}, u32[]{:S(2)}, u32[]{:S(2)}) %collective-permute-start.7) | collective-permute-done | bytes 98336 | tf_op jit(solution)/shard_map/ppermute | solution.py:67
  38.7 3.1 %collective-permute-start.12 = (bf16[2,2,32,768]{3,2,1,0:T(8,128)(2,1)S(1)}, bf16[2,2,32,768]{3,2,1,0:T(8,128)(2,1)S(1)}, u32[]{:S(2)}, u32[]{:S(2)}) collective-permute-start(bf16[2,2,32,768]{3,2,1,0:T(8,128)(2,1)S(1)} %pad_maximum_fusion.7), channel_id=1, source_target_pairs={{0,7},{1,2},{2,1},{3,4},{4,3},{5,6},{6,5},{7,0},{8,15},{9,10},{10,... | collective-permute-start | bytes 589832 | tf_op jit(solution)/shard_map/ppermute | solution.py:67
  42.0 1.2 pad_maximum_fusion.1
  43.3 1.5 %collective-permute-done.8 = bf16[2,2,32,768]{3,2,1,0:T(8,128)(2,1)S(1)} collective-permute-done((bf16[2,2,32,768]{3,2,1,0:T(8,128)(2,1)S(1)}, bf16[2,2,32,768]{3,2,1,0:T(8,128)(2,1)S(1)}, u32[]{:S(2)}, u32[]{:S(2)}) %collective-permute-start.8) | collective-permute-done | bytes 196640 | tf_op jit(solution)/shard_map/ppermute | solution.py:67
  44.8 2.7 %collective-permute-start.9 = (bf16[2,2,32,768]{3,2,1,0:T(8,128)(2,1)S(1)}, bf16[2,2,32,768]{3,2,1,0:T(8,128)(2,1)S(1)}, u32[]{:S(2)}, u32[]{:S(2)}) collective-permute-start(bf16[2,2,32,768]{3,2,1,0:T(8,128)(2,1)S(1)} %fusion.9), channel_id=1, source_target_pairs={{0,7},{1,2},{2,1},{3,4},{4,3},{5,6},{6,5},{7,0},{8,15},{9,10},{10,... | collective-permute-start | bytes 589832 | tf_op jit(solution)/shard_map/ppermute | solution.py:67
  47.6 4.2 %collective-permute-done.9 = bf16[2,2,32,768]{3,2,1,0:T(8,128)(2,1)S(1)} collective-permute-done((bf16[2,2,32,768]{3,2,1,0:T(8,128)(2,1)S(1)}, bf16[2,2,32,768]{3,2,1,0:T(8,128)(2,1)S(1)}, u32[]{:S(2)}, u32[]{:S(2)}) %collective-permute-start.9) | collective-permute-done | bytes 196640 | tf_op jit(solution)/shard_map/ppermute | solution.py:67
  51.9 3.0 %collective-permute-done.13 = bf16[2,2,32,768]{3,2,1,0:T(8,128)(2,1)S(1)} collective-permute-done((bf16[2,2,32,768]{3,2,1,0:T(8,128)(2,1)S(1)}, bf16[2,2,32,768]{3,2,1,0:T(8,128)(2,1)S(1)}, u32[]{:S(2)}, u32[]{:S(2)}) %collective-permute-start.13) | collective-permute-done | bytes 196640 | tf_op jit(solution)/shard_map/ppermute | solution.py:67
  54.9 1.3 %collective-permute-start.14 = (bf16[2,2,32,768]{3,2,1,0:T(8,128)(2,1)S(1)}, bf16[2,2,32,768]{3,2,1,0:T(8,128)(2,1)S(1)}, u32[]{:S(2)}, u32[]{:S(2)}) collective-permute-start(bf16[2,2,32,768]{3,2,1,0:T(8,128)(2,1)S(1)} %fusion.10), channel_id=1, source_target_pairs={{0,7},{1,2},{2,1},{3,4},{4,3},{5,6},{6,5},{7,0},{8,15},{9,10},{10,... | collective-permute-start | bytes 589832 | tf_op jit(solution)/shard_map/ppermute | solution.py:67
  56.2 1.2 pad_maximum_fusion
  57.6 6.6 %collective-permute-done.14 = bf16[2,2,32,768]{3,2,1,0:T(8,128)(2,1)S(1)} collective-permute-done((bf16[2,2,32,768]{3,2,1,0:T(8,128)(2,1)S(1)}, bf16[2,2,32,768]{3,2,1,0:T(8,128)(2,1)S(1)}, u32[]{:S(2)}, u32[]{:S(2)}) %collective-permute-start.14) | collective-permute-done | bytes 196640 | tf_op jit(solution)/shard_map/ppermute | solution.py:67
  64.5 2.1 %collective-permute-start.16 = (bf16[2,2,32,768]{3,2,1,0:T(8,128)(2,1)S(1)}, bf16[2,2,32,768]{3,2,1,0:T(8,128)(2,1)S(1)}, u32[]{:S(2)}, u32[]{:S(2)}) collective-permute-start(bf16[2,2,32,768]{3,2,1,0:T(8,128)(2,1)S(1)} %pad_maximum_fusion.8), channel_id=1, source_target_pairs={{0,7},{1,2},{2,1},{3,4},{4,3},{5,6},{6,5},{7,0},{8,15},{9,10},{10,... | collective-permute-start | bytes 589832 | tf_op jit(solution)/shard_map/ppermute | solution.py:67
  66.7 5.5 %collective-permute-done.15 = bf16[2,2,32,768]{3,2,1,0:T(8,128)(2,1)S(1)} collective-permute-done((bf16[2,2,32,768]{3,2,1,0:T(8,128)(2,1)S(1)}, bf16[2,2,32,768]{3,2,1,0:T(8,128)(2,1)S(1)}, u32[]{:S(2)}, u32[]{:S(2)}) %collective-permute-start.15) | collective-permute-done | bytes 196640 | tf_op jit(solution)/shard_map/ppermute | solution.py:67
  72.3 0.9 collective-permute-start.17
  73.2 6.8 %collective-permute-done.18 = bf16[2,2,32,768]{3,2,1,0:T(8,128)(2,1)S(1)} collective-permute-done((bf16[2,2,32,768]{3,2,1,0:T(8,128)(2,1)S(1)}, bf16[2,2,32,768]{3,2,1,0:T(8,128)(2,1)S(1)}, u32[]{:S(2)}, u32[]{:S(2)}) %collective-permute-start.18) | collective-permute-done | bytes 196640 | tf_op jit(solution)/shard_map/ppermute | solution.py:67
  80.0 1.5 %collective-permute-start.20 = (bf16[2,2,32,768]{3,2,1,0:T(8,128)(2,1)S(1)}, bf16[2,2,32,768]{3,2,1,0:T(8,128)(2,1)S(1)}, u32[]{:S(2)}, u32[]{:S(2)}) collective-permute-start(bf16[2,2,32,768]{3,2,1,0:T(8,128)(2,1)S(1)} %collective-permute-done.17), channel_id=1, source_target_pairs={{0,7},{1,2},{2,1},{3,4},{4,3},{5,6},{6,5},{7,0},{8,15},{9,10},{10,... | collective-permute-start | bytes 589832 | tf_op jit(solution)/shard_map/ppermute | solution.py:67
  81.5 4.2 %collective-permute-done.19 = bf16[2,2,32,768]{3,2,1,0:T(8,128)(2,1)S(1)} collective-permute-done((bf16[2,2,32,768]{3,2,1,0:T(8,128)(2,1)S(1)}, bf16[2,2,32,768]{3,2,1,0:T(8,128)(2,1)S(1)}, u32[]{:S(2)}, u32[]{:S(2)}) %collective-permute-start.19) | collective-permute-done | bytes 196640 | tf_op jit(solution)/shard_map/ppermute | solution.py:67
  86.9 0.9 collective-permute-start.21
  87.8 3.8 %collective-permute-done.22 = bf16[1,2,32,768]{3,2,1,0:T(8,128)(2,1)S(1)} collective-permute-done((bf16[1,2,32,768]{3,2,1,0:T(8,128)(2,1)S(1)}, bf16[1,2,32,768]{3,2,1,0:T(8,128)(2,1)S(1)}, u32[]{:S(2)}, u32[]{:S(2)}) %collective-permute-start.22) | collective-permute-done | bytes 98336 | tf_op jit(solution)/shard_map/ppermute | solution.py:67
  91.8 0.8 convolution_convert_fusion
  94.9 0.8 fusion.43
  96.6 0.8 fusion.44
  97.7 1.4 %collective-permute-start.25 = (bf16[2,4,16,1536]{3,2,0,1:T(8,128)(2,1)S(1)}, bf16[2,4,16,1536]{3,2,0,1:T(8,128)(2,1)S(1)}, u32[]{:S(2)}, u32[]{:S(2)}) collective-permute-start(bf16[2,4,16,1536]{3,2,0,1:T(8,128)(2,1)S(1)} %pad_maximum_fusion.3), channel_id=1, source_target_pairs={{0,64},{8,24},{16,80},{24,8},{32,96},{40,56},{48,112},{56,40},{64,... | collective-permute-start | bytes 1179656 | tf_op jit(solution)/shard_map/ppermute | solution.py:59
  99.1 2.5 %collective-permute-start.26 = (bf16[2,4,16,1536]{3,2,0,1:T(8,128)(2,1)S(1)}, bf16[2,4,16,1536]{3,2,0,1:T(8,128)(2,1)S(1)}, u32[]{:S(2)}, u32[]{:S(2)}) collective-permute-start(bf16[2,4,16,1536]{3,2,0,1:T(8,128)(2,1)S(1)} %pad_maximum_fusion.4), channel_id=1, source_target_pairs={{0,128},{8,40},{16,144},{24,56},{32,160},{40,8},{48,176},{56,24},{... | collective-permute-start | bytes 1179656 | tf_op jit(solution)/shard_map/ppermute | solution.py:59
  101.6 0.9 collective-permute-start.27
  102.4 2.8 %multiply_convert_fusion = bf16[768,1536]{1,0:T(8,128)(2,1)} fusion(bf16[512,768]{1,0:T(8,128)(2,1)S(1)} %bitcast.270, bf16[512,1536]{1,0:T(8,128)(2,1)S(1)} %copy-done.3), kind=kOutput, calls=%fused_computation | convolution fusion | flops 1210318848 | bytes 4718592 | tf_op jit(solution)/shard_map/dot_general | solution.py:31
  105.5 1.2 copy-done.4
  106.7 2.8 %multiply_convert_fusion.1 = bf16[1536,768]{1,0:T(8,128)(2,1)} fusion(bf16[512,1536]{1,0:T(8,128)(2,1)S(1)} %copy-done.4, bf16[512,768]{1,0:T(8,128)(2,1)S(1)} %bitcast.269), kind=kOutput, calls=%fused_computation.1 | convolution fusion | flops 1210318848 | bytes 4718592 | tf_op jit(solution)/shard_map/dot_general | solution.py:31
  109.5 2.1 %collective-permute-done.26 = bf16[2,4,16,1536]{3,2,0,1:T(8,128)(2,1)S(1)} collective-permute-done((bf16[2,4,16,1536]{3,2,0,1:T(8,128)(2,1)S(1)}, bf16[2,4,16,1536]{3,2,0,1:T(8,128)(2,1)S(1)}, u32[]{:S(2)}, u32[]{:S(2)}) %collective-permute-start.26) | collective-permute-done | bytes 393248 | tf_op jit(solution)/shard_map/ppermute | solution.py:59
  111.6 3.1 %collective-permute-done.27 = bf16[2,4,16,1536]{3,2,0,1:T(8,128)(2,1)S(1)} collective-permute-done((bf16[2,4,16,1536]{3,2,0,1:T(8,128)(2,1)S(1)}, bf16[2,4,16,1536]{3,2,0,1:T(8,128)(2,1)S(1)}, u32[]{:S(2)}, u32[]{:S(2)}) %collective-permute-start.27) | collective-permute-done | bytes 393248 | tf_op jit(solution)/shard_map/ppermute | solution.py:59
  115.0 1.4 %collective-permute-start.28 = (bf16[2,16,1536]{2,1,0:T(8,128)(2,1)S(1)}, bf16[2,16,1536]{2,1,0:T(8,128)(2,1)S(1)}, u32[]{:S(2)}, u32[]{:S(2)}) collective-permute-start(bf16[2,16,1536]{2,1,0:T(8,128)(2,1)S(1)} %get-tuple-element.91), channel_id=1, source_target_pairs={{0,16},{8,72},{16,0},{24,88},{32,48},{40,104},{48,32},{56,120},{64... | collective-permute-start | bytes 294920 | tf_op jit(solution)/shard_map/ppermute | solution.py:59
  116.4 2.0 %collective-permute-start.30 = (bf16[2,16,1536]{2,1,0:T(8,128)(2,1)S(1)}, bf16[2,16,1536]{2,1,0:T(8,128)(2,1)S(1)}, u32[]{:S(2)}, u32[]{:S(2)}) collective-permute-start(bf16[2,16,1536]{2,1,0:T(8,128)(2,1)S(1)} %get-tuple-element.92), channel_id=1, source_target_pairs={{0,48},{8,200},{16,32},{24,216},{32,16},{40,232},{48,0},{56,248},{... | collective-permute-start | bytes 294920 | tf_op jit(solution)/shard_map/ppermute | solution.py:59
  118.4 0.8 collective-permute-start.29
  119.8 1.2 collective-permute-done.30
  121.0 3.5 %collective-permute-done.29 = bf16[2,16,1536]{2,1,0:T(8,128)(2,1)S(1)} collective-permute-done((bf16[2,16,1536]{2,1,0:T(8,128)(2,1)S(1)}, bf16[2,16,1536]{2,1,0:T(8,128)(2,1)S(1)}, u32[]{:S(2)}, u32[]{:S(2)}) %collective-permute-start.29) | collective-permute-done | bytes 98336 | tf_op jit(solution)/shard_map/ppermute | solution.py:59
  (103 shorter events, 11.8 us)
Async XLA Ops:
  0.6 22.8 %copy-start = (bf16[1536,768]{1,0:T(8,128)(2,1)S(1)}, bf16[1536,768]{1,0:T(8,128)(2,1)}, u32[]{:S(2)}) copy-start(bf16[1536,768]{1,0:T(8,128)(2,1)} %param.6) | copy-start | bytes 7077892
  1.6 6.2 %collective-permute-start.1 = (bf16[2,16,1536]{2,1,0:T(8,128)(2,1)S(1)}, bf16[2,16,1536]{2,1,0:T(8,128)(2,1)S(1)}, u32[]{:S(2)}, u32[]{:S(2)}) collective-permute-start(bf16[2,16,1536]{2,1,0:T(8,128)(2,1)S(1)} %get-tuple-element.97), channel_id=1, source_target_pairs={{0,32},{8,136},{16,48},{24,152},{32,0},{40,168},{48,16},{56,184},{... | collective-permute-start | bytes 294920 | tf_op jit(solution)/shard_map/ppermute | solution.py:59
  4.0 4.6 %collective-permute-start = (bf16[2,16,1536]{2,1,0:T(8,128)(2,1)S(1)}, bf16[2,16,1536]{2,1,0:T(8,128)(2,1)S(1)}, u32[]{:S(2)}, u32[]{:S(2)}) collective-permute-start(bf16[2,16,1536]{2,1,0:T(8,128)(2,1)S(1)} %get-tuple-element.97), channel_id=1, source_target_pairs={{0,16},{8,72},{16,0},{24,88},{32,48},{40,104},{48,32},{56,120},{64... | collective-permute-start | bytes 294920 | tf_op jit(solution)/shard_map/ppermute | solution.py:59
  4.3 4.6 %collective-permute-start.2 = (bf16[2,16,1536]{2,1,0:T(8,128)(2,1)S(1)}, bf16[2,16,1536]{2,1,0:T(8,128)(2,1)S(1)}, u32[]{:S(2)}, u32[]{:S(2)}) collective-permute-start(bf16[2,16,1536]{2,1,0:T(8,128)(2,1)S(1)} %get-tuple-element.97), channel_id=1, source_target_pairs={{0,48},{8,200},{16,32},{24,216},{32,16},{40,232},{48,0},{56,248},{... | collective-permute-start | bytes 294920 | tf_op jit(solution)/shard_map/ppermute | solution.py:59
  9.0 9.5 %collective-permute-start.3 = (bf16[2,4,16,1536]{3,2,1,0:T(8,128)(2,1)S(1)}, bf16[2,4,16,1536]{3,2,1,0:T(8,128)(2,1)S(1)}, u32[]{:S(2)}, u32[]{:S(2)}) collective-permute-start(bf16[2,4,16,1536]{3,2,1,0:T(8,128)(2,1)S(1)} %pad_maximum_fusion.2), channel_id=1, source_target_pairs={{0,128},{8,40},{16,144},{24,56},{32,160},{40,8},{48,176},{56,24},{... | collective-permute-start | bytes 1179656 | tf_op jit(solution)/shard_map/ppermute | solution.py:59
  12.3 10.9 %collective-permute-start.5 = (bf16[2,4,16,1536]{3,2,1,0:T(8,128)(2,1)S(1)}, bf16[2,4,16,1536]{3,2,1,0:T(8,128)(2,1)S(1)}, u32[]{:S(2)}, u32[]{:S(2)}) collective-permute-start(bf16[2,4,16,1536]{3,2,1,0:T(8,128)(2,1)S(1)} %pad_maximum_fusion.2), channel_id=1, source_target_pairs={{0,192},{8,56},{16,208},{24,40},{32,224},{40,24},{48,240},{56,8},{... | collective-permute-start | bytes 1179656 | tf_op jit(solution)/shard_map/ppermute | solution.py:59
  13.3 9.6 %collective-permute-start.4 = (bf16[2,4,16,1536]{3,2,1,0:T(8,128)(2,1)S(1)}, bf16[2,4,16,1536]{3,2,1,0:T(8,128)(2,1)S(1)}, u32[]{:S(2)}, u32[]{:S(2)}) collective-permute-start(bf16[2,4,16,1536]{3,2,1,0:T(8,128)(2,1)S(1)} %pad_maximum_fusion.2), channel_id=1, source_target_pairs={{0,64},{8,24},{16,80},{24,8},{32,96},{40,56},{48,112},{56,40},{64,... | collective-permute-start | bytes 1179656 | tf_op jit(solution)/shard_map/ppermute | solution.py:59
  23.3 3.5 %collective-permute-start.6 = (bf16[2,256,1536]{2,1,0:T(8,128)(2,1)S(1)}, bf16[2,256,1536]{2,1,0:T(8,128)(2,1)S(1)}, u32[]{:S(2)}, u32[]{:S(2)}) collective-permute-start(bf16[2,256,1536]{2,1,0:T(8,128)(2,1)S(1)} %bitcast.258), channel_id=1, source_target_pairs={{0,8},{8,0},{16,24},{24,16},{32,40},{40,32},{48,56},{56,48},{64,72... | collective-permute-start | bytes 4718600 | tf_op jit(solution)/shard_map/ppermute | solution.py:63
  23.5 1.7 %copy-start.1 = (bf16[768,1536]{1,0:T(8,128)(2,1)S(1)}, bf16[768,1536]{1,0:T(8,128)(2,1)}, u32[]{:S(2)}) copy-start(bf16[768,1536]{1,0:T(8,128)(2,1)} %param.8) | copy-start | bytes 7077892
  28.6 7.2 %collective-permute-start.11 = (bf16[1,2,32,768]{3,2,1,0:T(8,128)(2,1)S(1)}, bf16[1,2,32,768]{3,2,1,0:T(8,128)(2,1)S(1)}, u32[]{:S(2)}, u32[]{:S(2)}) collective-permute-start(bf16[1,2,32,768]{3,2,1,0:T(8,128)(2,1)S(1)} %pad_maximum_fusion.10), channel_id=1, source_target_pairs={{0,1},{1,0},{2,3},{3,2},{4,5},{5,4},{6,7},{7,6},{8,9},{9,8},{10,11... | collective-permute-start | bytes 294920 | tf_op jit(solution)/shard_map/ppermute | solution.py:67
  30.7 7.9 %collective-permute-start.7 = (bf16[1,2,32,768]{3,2,1,0:T(8,128)(2,1)S(1)}, bf16[1,2,32,768]{3,2,1,0:T(8,128)(2,1)S(1)}, u32[]{:S(2)}, u32[]{:S(2)}) collective-permute-start(bf16[1,2,32,768]{3,2,1,0:T(8,128)(2,1)S(1)} %pad_maximum_fusion.11), channel_id=1, source_target_pairs={{0,7},{1,2},{2,1},{3,4},{4,3},{5,6},{6,5},{7,0},{8,15},{9,10},{10,... | collective-permute-start | bytes 294920 | tf_op jit(solution)/shard_map/ppermute | solution.py:67
  38.6 6.2 %collective-permute-start.8 = (bf16[2,2,32,768]{3,2,1,0:T(8,128)(2,1)S(1)}, bf16[2,2,32,768]{3,2,1,0:T(8,128)(2,1)S(1)}, u32[]{:S(2)}, u32[]{:S(2)}) collective-permute-start(bf16[2,2,32,768]{3,2,1,0:T(8,128)(2,1)S(1)} %pad_maximum_fusion.6), channel_id=1, source_target_pairs={{0,1},{1,0},{2,3},{3,2},{4,5},{5,4},{6,7},{7,6},{8,9},{9,8},{10,11... | collective-permute-start | bytes 589832 | tf_op jit(solution)/shard_map/ppermute | solution.py:67
  38.7 8.7 %collective-permute-start.12 = (bf16[2,2,32,768]{3,2,1,0:T(8,128)(2,1)S(1)}, bf16[2,2,32,768]{3,2,1,0:T(8,128)(2,1)S(1)}, u32[]{:S(2)}, u32[]{:S(2)}) collective-permute-start(bf16[2,2,32,768]{3,2,1,0:T(8,128)(2,1)S(1)} %pad_maximum_fusion.7), channel_id=1, source_target_pairs={{0,7},{1,2},{2,1},{3,4},{4,3},{5,6},{6,5},{7,0},{8,15},{9,10},{10,... | collective-permute-start | bytes 589832 | tf_op jit(solution)/shard_map/ppermute | solution.py:67
  44.8 7.0 %collective-permute-start.9 = (bf16[2,2,32,768]{3,2,1,0:T(8,128)(2,1)S(1)}, bf16[2,2,32,768]{3,2,1,0:T(8,128)(2,1)S(1)}, u32[]{:S(2)}, u32[]{:S(2)}) collective-permute-start(bf16[2,2,32,768]{3,2,1,0:T(8,128)(2,1)S(1)} %fusion.9), channel_id=1, source_target_pairs={{0,7},{1,2},{2,1},{3,4},{4,3},{5,6},{6,5},{7,0},{8,15},{9,10},{10,... | collective-permute-start | bytes 589832 | tf_op jit(solution)/shard_map/ppermute | solution.py:67
  47.5 7.4 %collective-permute-start.13 = (bf16[2,2,32,768]{3,2,1,0:T(8,128)(2,1)S(1)}, bf16[2,2,32,768]{3,2,1,0:T(8,128)(2,1)S(1)}, u32[]{:S(2)}, u32[]{:S(2)}) collective-permute-start(bf16[2,2,32,768]{3,2,1,0:T(8,128)(2,1)S(1)} %fusion.11), channel_id=1, source_target_pairs={{0,1},{1,0},{2,3},{3,2},{4,5},{5,4},{6,7},{7,6},{8,9},{9,8},{10,11... | collective-permute-start | bytes 589832 | tf_op jit(solution)/shard_map/ppermute | solution.py:67
  51.8 5.8 %collective-permute-start.10 = (bf16[2,2,32,768]{3,2,1,0:T(8,128)(2,1)S(1)}, bf16[2,2,32,768]{3,2,1,0:T(8,128)(2,1)S(1)}, u32[]{:S(2)}, u32[]{:S(2)}) collective-permute-start(bf16[2,2,32,768]{3,2,1,0:T(8,128)(2,1)S(1)} %fusion.8), channel_id=1, source_target_pairs={{0,1},{1,0},{2,3},{3,2},{4,5},{5,4},{6,7},{7,6},{8,9},{9,8},{10,11... | collective-permute-start | bytes 589832 | tf_op jit(solution)/shard_map/ppermute | solution.py:67
  54.9 9.2 %collective-permute-start.14 = (bf16[2,2,32,768]{3,2,1,0:T(8,128)(2,1)S(1)}, bf16[2,2,32,768]{3,2,1,0:T(8,128)(2,1)S(1)}, u32[]{:S(2)}, u32[]{:S(2)}) collective-permute-start(bf16[2,2,32,768]{3,2,1,0:T(8,128)(2,1)S(1)} %fusion.10), channel_id=1, source_target_pairs={{0,7},{1,2},{2,1},{3,4},{4,3},{5,6},{6,5},{7,0},{8,15},{9,10},{10,... | collective-permute-start | bytes 589832 | tf_op jit(solution)/shard_map/ppermute | solution.py:67
  56.2 7.9 %copy-start.5 = (f32[768]{0:T(1024)S(1)}, f32[768]{0:T(1024)}, u32[]{:S(2)}) copy-start(f32[768]{0:T(1024)} %param.7) | copy-start | bytes 9220
  64.4 7.9 %collective-permute-start.15 = (bf16[2,2,32,768]{3,2,1,0:T(8,128)(2,1)S(1)}, bf16[2,2,32,768]{3,2,1,0:T(8,128)(2,1)S(1)}, u32[]{:S(2)}, u32[]{:S(2)}) collective-permute-start(bf16[2,2,32,768]{3,2,1,0:T(8,128)(2,1)S(1)} %pad_maximum_fusion.8), channel_id=1, source_target_pairs={{0,1},{1,0},{2,3},{3,2},{4,5},{5,4},{6,7},{7,6},{8,9},{9,8},{10,11... | collective-permute-start | bytes 589832 | tf_op jit(solution)/shard_map/ppermute | solution.py:67
  64.5 7.8 %collective-permute-start.16 = (bf16[2,2,32,768]{3,2,1,0:T(8,128)(2,1)S(1)}, bf16[2,2,32,768]{3,2,1,0:T(8,128)(2,1)S(1)}, u32[]{:S(2)}, u32[]{:S(2)}) collective-permute-start(bf16[2,2,32,768]{3,2,1,0:T(8,128)(2,1)S(1)} %pad_maximum_fusion.8), channel_id=1, source_target_pairs={{0,7},{1,2},{2,1},{3,4},{4,3},{5,6},{6,5},{7,0},{8,15},{9,10},{10,... | collective-permute-start | bytes 589832 | tf_op jit(solution)/shard_map/ppermute | solution.py:67
  72.3 7.8 %collective-permute-start.18 = (bf16[2,2,32,768]{3,2,1,0:T(8,128)(2,1)S(1)}, bf16[2,2,32,768]{3,2,1,0:T(8,128)(2,1)S(1)}, u32[]{:S(2)}, u32[]{:S(2)}) collective-permute-start(bf16[2,2,32,768]{3,2,1,0:T(8,128)(2,1)S(1)} %collective-permute-done.15), channel_id=1, source_target_pairs={{0,7},{1,2},{2,1},{3,4},{4,3},{5,6},{6,5},{7,0},{8,15},{9,10},{10,... | collective-permute-start | bytes 589832 | tf_op jit(solution)/shard_map/ppermute | solution.py:67
  72.3 7.8 %collective-permute-start.17 = (bf16[2,2,32,768]{3,2,1,0:T(8,128)(2,1)S(1)}, bf16[2,2,32,768]{3,2,1,0:T(8,128)(2,1)S(1)}, u32[]{:S(2)}, u32[]{:S(2)}) collective-permute-start(bf16[2,2,32,768]{3,2,1,0:T(8,128)(2,1)S(1)} %collective-permute-done.16), channel_id=1, source_target_pairs={{0,1},{1,0},{2,3},{3,2},{4,5},{5,4},{6,7},{7,6},{8,9},{9,8},{10,11... | collective-permute-start | bytes 589832 | tf_op jit(solution)/shard_map/ppermute | solution.py:67
  80.0 5.7 %collective-permute-start.19 = (bf16[2,2,32,768]{3,2,1,0:T(8,128)(2,1)S(1)}, bf16[2,2,32,768]{3,2,1,0:T(8,128)(2,1)S(1)}, u32[]{:S(2)}, u32[]{:S(2)}) collective-permute-start(bf16[2,2,32,768]{3,2,1,0:T(8,128)(2,1)S(1)} %collective-permute-done.18), channel_id=1, source_target_pairs={{0,1},{1,0},{2,3},{3,2},{4,5},{5,4},{6,7},{7,6},{8,9},{9,8},{10,11... | collective-permute-start | bytes 589832 | tf_op jit(solution)/shard_map/ppermute | solution.py:67
  80.0 6.9 %collective-permute-start.20 = (bf16[2,2,32,768]{3,2,1,0:T(8,128)(2,1)S(1)}, bf16[2,2,32,768]{3,2,1,0:T(8,128)(2,1)S(1)}, u32[]{:S(2)}, u32[]{:S(2)}) collective-permute-start(bf16[2,2,32,768]{3,2,1,0:T(8,128)(2,1)S(1)} %collective-permute-done.17), channel_id=1, source_target_pairs={{0,7},{1,2},{2,1},{3,4},{4,3},{5,6},{6,5},{7,0},{8,15},{9,10},{10,... | collective-permute-start | bytes 589832 | tf_op jit(solution)/shard_map/ppermute | solution.py:67
  85.7 5.9 %collective-permute-start.22 = (bf16[1,2,32,768]{3,2,1,0:T(8,128)(2,1)S(1)}, bf16[1,2,32,768]{3,2,1,0:T(8,128)(2,1)S(1)}, u32[]{:S(2)}, u32[]{:S(2)}) collective-permute-start(bf16[1,2,32,768]{3,2,1,0:T(8,128)(2,1)S(1)} %slice.174), channel_id=1, source_target_pairs={{0,7},{1,2},{2,1},{3,4},{4,3},{5,6},{6,5},{7,0},{8,15},{9,10},{10,... | collective-permute-start | bytes 294920 | tf_op jit(solution)/shard_map/ppermute | solution.py:67
  86.9 4.7 %collective-permute-start.21 = (bf16[1,2,32,768]{3,2,1,0:T(8,128)(2,1)S(1)}, bf16[1,2,32,768]{3,2,1,0:T(8,128)(2,1)S(1)}, u32[]{:S(2)}, u32[]{:S(2)}) collective-permute-start(bf16[1,2,32,768]{3,2,1,0:T(8,128)(2,1)S(1)} %slice.173), channel_id=1, source_target_pairs={{0,1},{1,0},{2,3},{3,2},{4,5},{5,4},{6,7},{7,6},{8,9},{9,8},{10,11... | collective-permute-start | bytes 294920 | tf_op jit(solution)/shard_map/ppermute | solution.py:67
  91.7 1.7 %copy-start.2 = (bf16[768,1536]{1,0:T(8,128)(2,1)S(1)}, bf16[768,1536]{1,0:T(8,128)(2,1)}, u32[]{:S(2)}) copy-start(bf16[768,1536]{1,0:T(8,128)(2,1)} %param.8) | copy-start | bytes 7077892
  92.6 2.4 %collective-permute-start.24 = (bf16[256,1536]{1,0:T(8,128)(2,1)S(1)}, bf16[256,1536]{1,0:T(8,128)(2,1)S(1)}, u32[]{:S(2)}, u32[]{:S(2)}) collective-permute-start(bf16[256,1536]{1,0:T(8,128)(2,1)S(1)} %convolution_convert_fusion), channel_id=1, source_target_pairs={{0,8},{8,0},{16,24},{24,16},{32,40},{40,32},{48,56},{56,48},{64,72... | collective-permute-start | bytes 2359304 | tf_op jit(solution)/shard_map/ppermute | solution.py:63
  94.2 2.4 %collective-permute-start.23 = (bf16[256,1536]{1,0:T(8,128)(2,1)S(1)}, bf16[256,1536]{1,0:T(8,128)(2,1)S(1)}, u32[]{:S(2)}, u32[]{:S(2)}) collective-permute-start(bf16[256,1536]{1,0:T(8,128)(2,1)S(1)} %convolution_convert_fusion.1), channel_id=1, source_target_pairs={{0,8},{8,0},{16,24},{24,16},{32,40},{40,32},{48,56},{56,48},{64,72... | collective-permute-start | bytes 2359304 | tf_op jit(solution)/shard_map/ppermute | solution.py:63
  97.5 4.9 %copy-start.3 = (bf16[512,1536]{1,0:T(8,128)(2,1)S(1)}, bf16[512,1536]{1,0:T(8,128)(2,1)}, u32[]{:S(2)}) copy-start(bf16[512,1536]{1,0:T(8,128)(2,1)} %pad_maximum_fusion.1) | copy-start | bytes 4718596
  97.7 11.9 %collective-permute-start.25 = (bf16[2,4,16,1536]{3,2,0,1:T(8,128)(2,1)S(1)}, bf16[2,4,16,1536]{3,2,0,1:T(8,128)(2,1)S(1)}, u32[]{:S(2)}, u32[]{:S(2)}) collective-permute-start(bf16[2,4,16,1536]{3,2,0,1:T(8,128)(2,1)S(1)} %pad_maximum_fusion.3), channel_id=1, source_target_pairs={{0,64},{8,24},{16,80},{24,8},{32,96},{40,56},{48,112},{56,40},{64,... | collective-permute-start | bytes 1179656 | tf_op jit(solution)/shard_map/ppermute | solution.py:59
  99.1 12.6 %collective-permute-start.26 = (bf16[2,4,16,1536]{3,2,0,1:T(8,128)(2,1)S(1)}, bf16[2,4,16,1536]{3,2,0,1:T(8,128)(2,1)S(1)}, u32[]{:S(2)}, u32[]{:S(2)}) collective-permute-start(bf16[2,4,16,1536]{3,2,0,1:T(8,128)(2,1)S(1)} %pad_maximum_fusion.4), channel_id=1, source_target_pairs={{0,128},{8,40},{16,144},{24,56},{32,160},{40,8},{48,176},{56,24},{... | collective-permute-start | bytes 1179656 | tf_op jit(solution)/shard_map/ppermute | solution.py:59
  101.6 13.2 %collective-permute-start.27 = (bf16[2,4,16,1536]{3,2,0,1:T(8,128)(2,1)S(1)}, bf16[2,4,16,1536]{3,2,0,1:T(8,128)(2,1)S(1)}, u32[]{:S(2)}, u32[]{:S(2)}) collective-permute-start(bf16[2,4,16,1536]{3,2,0,1:T(8,128)(2,1)S(1)} %pad_maximum_fusion.5), channel_id=1, source_target_pairs={{0,192},{8,56},{16,208},{24,40},{32,224},{40,24},{48,240},{56,8},{... | collective-permute-start | bytes 1179656 | tf_op jit(solution)/shard_map/ppermute | solution.py:59
  105.3 1.4 %copy-start.4 = (bf16[512,1536]{1,0:T(8,128)(2,1)S(1)}, bf16[512,1536]{1,0:T(8,128)(2,1)}, u32[]{:S(2)}) copy-start(bf16[512,1536]{1,0:T(8,128)(2,1)} %pad_maximum_fusion) | copy-start | bytes 4718596
  115.0 4.8 %collective-permute-start.28 = (bf16[2,16,1536]{2,1,0:T(8,128)(2,1)S(1)}, bf16[2,16,1536]{2,1,0:T(8,128)(2,1)S(1)}, u32[]{:S(2)}, u32[]{:S(2)}) collective-permute-start(bf16[2,16,1536]{2,1,0:T(8,128)(2,1)S(1)} %get-tuple-element.91), channel_id=1, source_target_pairs={{0,16},{8,72},{16,0},{24,88},{32,48},{40,104},{48,32},{56,120},{64... | collective-permute-start | bytes 294920 | tf_op jit(solution)/shard_map/ppermute | solution.py:59
  116.4 4.6 %collective-permute-start.30 = (bf16[2,16,1536]{2,1,0:T(8,128)(2,1)S(1)}, bf16[2,16,1536]{2,1,0:T(8,128)(2,1)S(1)}, u32[]{:S(2)}, u32[]{:S(2)}) collective-permute-start(bf16[2,16,1536]{2,1,0:T(8,128)(2,1)S(1)} %get-tuple-element.92), channel_id=1, source_target_pairs={{0,48},{8,200},{16,32},{24,216},{32,16},{40,232},{48,0},{56,248},{... | collective-permute-start | bytes 294920 | tf_op jit(solution)/shard_map/ppermute | solution.py:59
  118.4 6.1 %collective-permute-start.29 = (bf16[2,16,1536]{2,1,0:T(8,128)(2,1)S(1)}, bf16[2,16,1536]{2,1,0:T(8,128)(2,1)S(1)}, u32[]{:S(2)}, u32[]{:S(2)}) collective-permute-start(bf16[2,16,1536]{2,1,0:T(8,128)(2,1)S(1)} %get-tuple-element.93), channel_id=1, source_target_pairs={{0,32},{8,136},{16,48},{24,152},{32,0},{40,168},{48,16},{56,184},{... | collective-permute-start | bytes 294920 | tf_op jit(solution)/shard_map/ppermute | solution.py:59

commit v4 on v3

--- a/solution.py
+++ b/solution.py
@@ -82,14 +82,12 @@
     for k, piece in ((0, line), (2, got[2]), (1, got[1]), (3, got[3])):
         own = lax.dynamic_update_slice_in_dim(own, piece[:, None], k, 1)
     own = own.reshape(2, HALF, features)
-    other = swap_cores(own)
+    other = [swap_cores(own[0]), swap_cores(own[1])]
 
-    def first_products(tokens):
-        pre = matmul(tokens[0], w_in)
-        pre, grads = lax.optimization_barrier((pre, tokens[1]))
-        return pre, contract_cols(grads, w_out)
-
-    own_parts = first_products(own)
+    own_pre = matmul(own[0], w_in)
+    other_pre = matmul(other[0], w_in)
+    other_pre, grads = lax.optimization_barrier((other_pre, own[1]))
+    own_parts = own_pre, contract_cols(grads, w_out)
 
     def part(halves, j):
         at = ((me + way * j) % 8) * 32
@@ -98,9 +96,9 @@
         )
 
     far_own = part([own_parts], 4).astype(BF16)
-    far_own, other = lax.optimization_barrier((far_own, other))
+    far_own, other[1] = lax.optimization_barrier((far_own, other[1]))
     from_even = col_swap(far_own, False)
-    other_parts = first_products(other)
+    other_parts = other_pre, contract_cols(other[1], w_out)
     from_odd = col_swap(part([other_parts], 4).astype(BF16), True)
     halves = [own_parts, other_parts]
     from_even, own, other = lax.optimization_barrier((from_even, own, other))

time: 125 us -> 123 us (0.984); the launches traced: 125 us -> 122 us
  waiting for transfers between devices: 63.2 us -> 57.1 us
  local copies, waits for them, and re-layouts: 5.1 us -> 6.6 us
    ppermute x12, waiting for transfers between devices: 22.5 us -> 19.1 us  [plane_swap(): return lax.ppermute(values, 'row', pairs)]
    ppermute x16, waiting for transfers between devices: 38.6 us -> 36.6 us  [col_swap(): lax.ppermute(values, 'col', [(i, ring_partner(i, 8, odd_links)) for i in...]
    slice x1, local copies, waits for them, and re-layouts: 0.13 us -> 1.47 us  [local(): other_pre, grads = lax.optimization_barrier((other_pre, own[1]))]
    unnamed x12 -> x18, local copies, waits for them, and re-layouts: 2.83 us -> 3.18 us
  transfers between devices with their start and end apart: 31 -> 32, of which waited for: 23 -> 23; matrix products, arithmetic and copies ran while one was open for 11% -> 12% of each run, Pallas kernels for 0% -> 0%
where the time goes in v4:
time: 123 us; the launch traced here: 122 us
  waiting for transfers between devices  57.1 us (46%)
  starting transfers between devices  39 us (32%)
  matrix products  13.1 us (11%)
  local copies, waits for them, and re-layouts  6.6 us (5%)
  other arithmetic  4.7 us (4%)
  between operations  1.27 us (1%)
    ppermute x16, waiting for transfers between devices, col_swap(): lax.ppermute(values, 'col', [(i, ring_partner(i, 8, odd_links)) for i in...  36.6 us
    ppermute x16, starting transfers between devices, col_swap(): lax.ppermute(values, 'col', [(i, ring_partner(i, 8, odd_links)) for i in...  21.4 us
    ppermute x12, waiting for transfers between devices, plane_swap(): return lax.ppermute(values, 'row', pairs)  19.1 us
    ppermute x12, starting transfers between devices, plane_swap(): return lax.ppermute(values, 'row', pairs)  16.9 us
    dot_general x2, matrix products, contract_rows(): lax.dot_general(left, right, (((0,), (0,)), ((), ())), preferred_element_...  5.65 us
    dot_general x4, matrix products, matmul(): return jnp.dot(left, right, preferred_element_type=F32)  4.22 us
    dot_general x4, matrix products, contract_cols(): lax.dot_general(left, right, (((1,), (1,)), ((), ())), preferred_element_...  3.24 us
    unnamed x18, local copies, waits for them, and re-layouts  3.18 us
  transfers between devices with their start and end apart: 32, of which 23 were waited for; matrix products, arithmetic and copies ran while one was open for 12% of the time, Pallas kernels for 0%

profile of v4, /device:TPU:4, one launch (start us, length us, event | category | flops | bytes accessed | tf_op | source)
XLA Modules:
  0.0 121.8 jit_solution(3793733561813847787)
XLA Ops:
  0.6 1.0 fusion.33
  2.3 2.7 %collective-permute-start.1 = (bf16[2,16,1536]{2,1,0:T(8,128)(2,1)S(1)}, bf16[2,16,1536]{2,1,0:T(8,128)(2,1)S(1)}, u32[]{:S(2)}, u32[]{:S(2)}) collective-permute-start(bf16[2,16,1536]{2,1,0:T(8,128)(2,1)S(1)} %get-tuple-element.93), channel_id=1, source_target_pairs={{0,32},{8,136},{16,48},{24,152},{32,0},{40,168},{48,16},{56,184},{... | collective-permute-start | bytes 294920 | tf_op jit(solution)/shard_map/ppermute | solution.py:59
  5.0 0.8 collective-permute-start
  6.3 2.0 %collective-permute-done.1 = bf16[2,16,1536]{2,1,0:T(8,128)(2,1)S(1)} collective-permute-done((bf16[2,16,1536]{2,1,0:T(8,128)(2,1)S(1)}, bf16[2,16,1536]{2,1,0:T(8,128)(2,1)S(1)}, u32[]{:S(2)}, u32[]{:S(2)}) %collective-permute-start.1) | collective-permute-done | bytes 98336 | tf_op jit(solution)/shard_map/ppermute | solution.py:59
  8.4 1.2 %collective-permute-done = bf16[2,16,1536]{2,1,0:T(8,128)(2,1)S(1)} collective-permute-done((bf16[2,16,1536]{2,1,0:T(8,128)(2,1)S(1)}, bf16[2,16,1536]{2,1,0:T(8,128)(2,1)S(1)}, u32[]{:S(2)}, u32[]{:S(2)}) %collective-permute-start) | collective-permute-done | bytes 98336 | tf_op jit(solution)/shard_map/ppermute | solution.py:59
  9.7 3.3 %collective-permute-start.3 = (bf16[2,4,16,1536]{3,2,1,0:T(8,128)(2,1)S(1)}, bf16[2,4,16,1536]{3,2,1,0:T(8,128)(2,1)S(1)}, u32[]{:S(2)}, u32[]{:S(2)}) collective-permute-start(bf16[2,4,16,1536]{3,2,1,0:T(8,128)(2,1)S(1)} %pad_maximum_fusion.2), channel_id=1, source_target_pairs={{0,128},{8,40},{16,144},{24,56},{32,160},{40,8},{48,176},{56,24},{... | collective-permute-start | bytes 1179656 | tf_op jit(solution)/shard_map/ppermute | solution.py:59
  14.2 4.9 %collective-permute-done.3 = bf16[2,4,16,1536]{3,2,1,0:T(8,128)(2,1)S(1)} collective-permute-done((bf16[2,4,16,1536]{3,2,1,0:T(8,128)(2,1)S(1)}, bf16[2,4,16,1536]{3,2,1,0:T(8,128)(2,1)S(1)}, u32[]{:S(2)}, u32[]{:S(2)}) %collective-permute-start.3) | collective-permute-done | bytes 393248 | tf_op jit(solution)/shard_map/ppermute | solution.py:59
  19.1 4.5 %collective-permute-done.4 = bf16[2,4,16,1536]{3,2,1,0:T(8,128)(2,1)S(1)} collective-permute-done((bf16[2,4,16,1536]{3,2,1,0:T(8,128)(2,1)S(1)}, bf16[2,4,16,1536]{3,2,1,0:T(8,128)(2,1)S(1)}, u32[]{:S(2)}, u32[]{:S(2)}) %collective-permute-start.4) | collective-permute-done | bytes 393248 | tf_op jit(solution)/shard_map/ppermute | solution.py:59
  23.8 1.5 %fusion.37 = (bf16[1,4,4,16,1536]{4,3,2,1,0:T(8,128)(2,1)}, bf16[1,4,4,16,1536]{4,3,2,1,0:T(8,128)(2,1)}) fusion(bf16[2,4,4,16,1536]{4,3,2,1,0:T(8,128)(2,1)S(1)} %bitcast_dynamic-update-slice_fusion), kind=kLoop, calls=%fused_computation.135 | loop fusion | bytes 3145728 | tf_op jit(solution)/shard_map/slice | solution.py:89
  26.0 1.9 %fusion.42 = f32[256,768]{1,0:T(8,128)S(1)} fusion(bf16[256,1536]{1,0:T(8,128)(2,1)} %bitcast.13, bf16[1536,768]{1,0:T(8,128)(2,1)S(1)} %copy-done), kind=kOutput, calls=%fused_computation.140 | convolution fusion | flops 603979776 | bytes 3932160 | tf_op jit(solution)/shard_map/dot_general | solution.py:27
  28.0 0.8 fusion.43
  28.8 0.9 copy-done.3
  29.8 0.8 fusion.44
  30.8 0.8 fusion.45
  31.8 2.0 %collective-permute-start.12 = (bf16[1,2,32,768]{3,2,1,0:T(8,128)(2,1)S(1)}, bf16[1,2,32,768]{3,2,1,0:T(8,128)(2,1)S(1)}, u32[]{:S(2)}, u32[]{:S(2)}) collective-permute-start(bf16[1,2,32,768]{3,2,1,0:T(8,128)(2,1)S(1)} %pad_maximum_fusion.10), channel_id=1, source_target_pairs={{0,1},{1,0},{2,3},{3,2},{4,5},{5,4},{6,7},{7,6},{8,9},{9,8},{10,11... | collective-permute-start | bytes 294920 | tf_op jit(solution)/shard_map/ppermute | solution.py:67
  33.8 5.0 %collective-permute-start.8 = (bf16[1,2,32,768]{3,2,1,0:T(8,128)(2,1)S(1)}, bf16[1,2,32,768]{3,2,1,0:T(8,128)(2,1)S(1)}, u32[]{:S(2)}, u32[]{:S(2)}) collective-permute-start(bf16[1,2,32,768]{3,2,1,0:T(8,128)(2,1)S(1)} %pad_maximum_fusion.11), channel_id=1, source_target_pairs={{0,7},{1,2},{2,1},{3,4},{4,3},{5,6},{6,5},{7,0},{8,15},{9,10},{10,... | collective-permute-start | bytes 294920 | tf_op jit(solution)/shard_map/ppermute | solution.py:67
  39.2 3.4 %collective-permute-start.13 = (bf16[2,2,32,768]{3,2,1,0:T(8,128)(2,1)S(1)}, bf16[2,2,32,768]{3,2,1,0:T(8,128)(2,1)S(1)}, u32[]{:S(2)}, u32[]{:S(2)}) collective-permute-start(bf16[2,2,32,768]{3,2,1,0:T(8,128)(2,1)S(1)} %pad_maximum_fusion.7), channel_id=1, source_target_pairs={{0,7},{1,2},{2,1},{3,4},{4,3},{5,6},{6,5},{7,0},{8,15},{9,10},{10,... | collective-permute-start | bytes 589832 | tf_op jit(solution)/shard_map/ppermute | solution.py:67
  42.8 3.9 %collective-permute-done.13 = bf16[2,2,32,768]{3,2,1,0:T(8,128)(2,1)S(1)} collective-permute-done((bf16[2,2,32,768]{3,2,1,0:T(8,128)(2,1)S(1)}, bf16[2,2,32,768]{3,2,1,0:T(8,128)(2,1)S(1)}, u32[]{:S(2)}, u32[]{:S(2)}) %collective-permute-start.13) | collective-permute-done | bytes 196640 | tf_op jit(solution)/shard_map/ppermute | solution.py:67
  46.9 1.8 %collective-permute-done.9 = bf16[2,2,32,768]{3,2,1,0:T(8,128)(2,1)S(1)} collective-permute-done((bf16[2,2,32,768]{3,2,1,0:T(8,128)(2,1)S(1)}, bf16[2,2,32,768]{3,2,1,0:T(8,128)(2,1)S(1)}, u32[]{:S(2)}, u32[]{:S(2)}) %collective-permute-start.9) | collective-permute-done | bytes 196640 | tf_op jit(solution)/shard_map/ppermute | solution.py:67
  48.7 1.9 %collective-permute-start.10 = (bf16[2,2,32,768]{3,2,1,0:T(8,128)(2,1)S(1)}, bf16[2,2,32,768]{3,2,1,0:T(8,128)(2,1)S(1)}, u32[]{:S(2)}, u32[]{:S(2)}) collective-permute-start(bf16[2,2,32,768]{3,2,1,0:T(8,128)(2,1)S(1)} %fusion.6), channel_id=1, source_target_pairs={{0,7},{1,2},{2,1},{3,4},{4,3},{5,6},{6,5},{7,0},{8,15},{9,10},{10,... | collective-permute-start | bytes 589832 | tf_op jit(solution)/shard_map/ppermute | solution.py:67
  50.6 2.0 %collective-permute-done.14 = bf16[2,2,32,768]{3,2,1,0:T(8,128)(2,1)S(1)} collective-permute-done((bf16[2,2,32,768]{3,2,1,0:T(8,128)(2,1)S(1)}, bf16[2,2,32,768]{3,2,1,0:T(8,128)(2,1)S(1)}, u32[]{:S(2)}, u32[]{:S(2)}) %collective-permute-start.14) | collective-permute-done | bytes 196640 | tf_op jit(solution)/shard_map/ppermute | solution.py:67
  52.6 3.0 %collective-permute-start.15 = (bf16[2,2,32,768]{3,2,1,0:T(8,128)(2,1)S(1)}, bf16[2,2,32,768]{3,2,1,0:T(8,128)(2,1)S(1)}, u32[]{:S(2)}, u32[]{:S(2)}) collective-permute-start(bf16[2,2,32,768]{3,2,1,0:T(8,128)(2,1)S(1)} %fusion.7), channel_id=1, source_target_pairs={{0,7},{1,2},{2,1},{3,4},{4,3},{5,6},{6,5},{7,0},{8,15},{9,10},{10,... | collective-permute-start | bytes 589832 | tf_op jit(solution)/shard_map/ppermute | solution.py:67
  55.6 1.5 %collective-permute-done.10 = bf16[2,2,32,768]{3,2,1,0:T(8,128)(2,1)S(1)} collective-permute-done((bf16[2,2,32,768]{3,2,1,0:T(8,128)(2,1)S(1)}, bf16[2,2,32,768]{3,2,1,0:T(8,128)(2,1)S(1)}, u32[]{:S(2)}, u32[]{:S(2)}) %collective-permute-start.10) | collective-permute-done | bytes 196640 | tf_op jit(solution)/shard_map/ppermute | solution.py:67
  57.5 1.9 %pad_maximum_fusion = (bf16[512,1536]{1,0:T(8,128)(2,1)}, bf16[512,1536]{1,0:T(8,128)(2,1)}) fusion(bf16[256,1536]{1,0:T(8,128)(2,1)S(1)} %collective-permute-done.6, bf16[256,1536]{1,0:T(8,128)(2,1)S(1)} %get-tuple-element.44, bf16[256,1536]{1,0:T(8,128)(2,1)S(1)} %collective-permute-done.7, bf16[256,1536]{1,0:T(8,128)(2,1)S(1)} %get-tuple-element.43), kind=kLoop, calls=%fused_computation.4 | loop fusion | flops 6291456 | bytes 6291456 | tf_op jit(solution)/shard_map/concatenate | solution.py:105
  59.9 4.4 %collective-permute-done.11 = bf16[2,2,32,768]{3,2,1,0:T(8,128)(2,1)S(1)} collective-permute-done((bf16[2,2,32,768]{3,2,1,0:T(8,128)(2,1)S(1)}, bf16[2,2,32,768]{3,2,1,0:T(8,128)(2,1)S(1)}, u32[]{:S(2)}, u32[]{:S(2)}) %collective-permute-start.11) | collective-permute-done | bytes 196640 | tf_op jit(solution)/shard_map/ppermute | solution.py:67
  66.0 7.2 %collective-permute-done.17 = bf16[2,2,32,768]{3,2,1,0:T(8,128)(2,1)S(1)} collective-permute-done((bf16[2,2,32,768]{3,2,1,0:T(8,128)(2,1)S(1)}, bf16[2,2,32,768]{3,2,1,0:T(8,128)(2,1)S(1)}, u32[]{:S(2)}, u32[]{:S(2)}) %collective-permute-start.17) | collective-permute-done | bytes 196640 | tf_op jit(solution)/shard_map/ppermute | solution.py:67
  73.1 1.3 %collective-permute-start.19 = (bf16[2,2,32,768]{3,2,1,0:T(8,128)(2,1)S(1)}, bf16[2,2,32,768]{3,2,1,0:T(8,128)(2,1)S(1)}, u32[]{:S(2)}, u32[]{:S(2)}) collective-permute-start(bf16[2,2,32,768]{3,2,1,0:T(8,128)(2,1)S(1)} %collective-permute-done.16), channel_id=1, source_target_pairs={{0,7},{1,2},{2,1},{3,4},{4,3},{5,6},{6,5},{7,0},{8,15},{9,10},{10,... | collective-permute-start | bytes 589832 | tf_op jit(solution)/shard_map/ppermute | solution.py:67
  74.5 6.3 %collective-permute-done.19 = bf16[2,2,32,768]{3,2,1,0:T(8,128)(2,1)S(1)} collective-permute-done((bf16[2,2,32,768]{3,2,1,0:T(8,128)(2,1)S(1)}, bf16[2,2,32,768]{3,2,1,0:T(8,128)(2,1)S(1)}, u32[]{:S(2)}, u32[]{:S(2)}) %collective-permute-start.19) | collective-permute-done | bytes 196640 | tf_op jit(solution)/shard_map/ppermute | solution.py:67
  81.3 1.1 collective-permute-start.21
  82.4 4.0 %collective-permute-done.20 = bf16[2,2,32,768]{3,2,1,0:T(8,128)(2,1)S(1)} collective-permute-done((bf16[2,2,32,768]{3,2,1,0:T(8,128)(2,1)S(1)}, bf16[2,2,32,768]{3,2,1,0:T(8,128)(2,1)S(1)}, u32[]{:S(2)}, u32[]{:S(2)}) %collective-permute-start.20) | collective-permute-done | bytes 196640 | tf_op jit(solution)/shard_map/ppermute | solution.py:67
  86.5 1.2 collective-permute-start.23
  88.6 3.8 %collective-permute-done.23 = bf16[1,2,32,768]{3,2,1,0:T(8,128)(2,1)S(1)} collective-permute-done((bf16[1,2,32,768]{3,2,1,0:T(8,128)(2,1)S(1)}, bf16[1,2,32,768]{3,2,1,0:T(8,128)(2,1)S(1)}, u32[]{:S(2)}, u32[]{:S(2)}) %collective-permute-start.23) | collective-permute-done | bytes 98336 | tf_op jit(solution)/shard_map/ppermute | solution.py:67
  93.1 0.8 convolution_convert_fusion
  94.0 0.7 copy-done.4
  94.7 0.8 convolution_convert_fusion.1
  96.3 0.8 fusion.40
  97.9 0.8 fusion.41
  98.9 2.6 %collective-permute-start.28 = (bf16[2,4,16,1536]{3,2,0,1:T(8,128)(2,1)S(1)}, bf16[2,4,16,1536]{3,2,0,1:T(8,128)(2,1)S(1)}, u32[]{:S(2)}, u32[]{:S(2)}) collective-permute-start(bf16[2,4,16,1536]{3,2,0,1:T(8,128)(2,1)S(1)} %pad_maximum_fusion.5), channel_id=1, source_target_pairs={{0,192},{8,56},{16,208},{24,40},{32,224},{40,24},{48,240},{56,8},{... | collective-permute-start | bytes 1179656 | tf_op jit(solution)/shard_map/ppermute | solution.py:59
  101.4 1.0 collective-permute-start.27
  103.2 2.8 %multiply_convert_fusion = bf16[768,1536]{1,0:T(8,128)(2,1)} fusion(bf16[512,768]{1,0:T(8,128)(2,1)S(1)} %bitcast.263, bf16[512,1536]{1,0:T(8,128)(2,1)S(1)} %copy-done.6), kind=kOutput, calls=%fused_computation | convolution fusion | flops 1210318848 | bytes 4718592 | tf_op jit(solution)/shard_map/dot_general | solution.py:31
  106.2 1.2 copy-done.5
  107.4 2.8 %multiply_convert_fusion.1 = bf16[1536,768]{1,0:T(8,128)(2,1)} fusion(bf16[512,1536]{1,0:T(8,128)(2,1)S(1)} %copy-done.5, bf16[512,768]{1,0:T(8,128)(2,1)S(1)} %bitcast.262), kind=kOutput, calls=%fused_computation.1 | convolution fusion | flops 1210318848 | bytes 4718592 | tf_op jit(solution)/shard_map/dot_general | solution.py:31
  110.2 1.9 %collective-permute-done.28 = bf16[2,4,16,1536]{3,2,0,1:T(8,128)(2,1)S(1)} collective-permute-done((bf16[2,4,16,1536]{3,2,0,1:T(8,128)(2,1)S(1)}, bf16[2,4,16,1536]{3,2,0,1:T(8,128)(2,1)S(1)}, u32[]{:S(2)}, u32[]{:S(2)}) %collective-permute-start.28) | collective-permute-done | bytes 393248 | tf_op jit(solution)/shard_map/ppermute | solution.py:59
  112.2 0.9 collective-permute-done.26
  113.8 2.7 %collective-permute-start.30 = (bf16[2,16,1536]{2,1,0:T(8,128)(2,1)S(1)}, bf16[2,16,1536]{2,1,0:T(8,128)(2,1)S(1)}, u32[]{:S(2)}, u32[]{:S(2)}) collective-permute-start(bf16[2,16,1536]{2,1,0:T(8,128)(2,1)S(1)} %get-tuple-element.89), channel_id=1, source_target_pairs={{0,32},{8,136},{16,48},{24,152},{32,0},{40,168},{48,16},{56,184},{... | collective-permute-start | bytes 294920 | tf_op jit(solution)/shard_map/ppermute | solution.py:59
  116.5 1.0 collective-permute-start.29
  118.1 1.8 %collective-permute-done.30 = bf16[2,16,1536]{2,1,0:T(8,128)(2,1)S(1)} collective-permute-done((bf16[2,16,1536]{2,1,0:T(8,128)(2,1)S(1)}, bf16[2,16,1536]{2,1,0:T(8,128)(2,1)S(1)}, u32[]{:S(2)}, u32[]{:S(2)}) %collective-permute-start.30) | collective-permute-done | bytes 98336 | tf_op jit(solution)/shard_map/ppermute | solution.py:59
  119.9 1.2 %collective-permute-done.29 = bf16[2,16,1536]{2,1,0:T(8,128)(2,1)S(1)} collective-permute-done((bf16[2,16,1536]{2,1,0:T(8,128)(2,1)S(1)}, bf16[2,16,1536]{2,1,0:T(8,128)(2,1)S(1)}, u32[]{:S(2)}, u32[]{:S(2)}) %collective-permute-start.29) | collective-permute-done | bytes 98336 | tf_op jit(solution)/shard_map/ppermute | solution.py:59
  (110 shorter events, 13.9 us)
Async XLA Ops:
  0.6 25.4 %copy-start = (bf16[1536,768]{1,0:T(8,128)(2,1)S(1)}, bf16[1536,768]{1,0:T(8,128)(2,1)}, u32[]{:S(2)}) copy-start(bf16[1536,768]{1,0:T(8,128)(2,1)} %param.6) | copy-start | bytes 7077892
  1.6 4.7 %collective-permute-start.2 = (bf16[2,16,1536]{2,1,0:T(8,128)(2,1)S(1)}, bf16[2,16,1536]{2,1,0:T(8,128)(2,1)S(1)}, u32[]{:S(2)}, u32[]{:S(2)}) collective-permute-start(bf16[2,16,1536]{2,1,0:T(8,128)(2,1)S(1)} %get-tuple-element.93), channel_id=1, source_target_pairs={{0,48},{8,200},{16,32},{24,216},{32,16},{40,232},{48,0},{56,248},{... | collective-permute-start | bytes 294920 | tf_op jit(solution)/shard_map/ppermute | solution.py:59
  2.3 6.1 %collective-permute-start.1 = (bf16[2,16,1536]{2,1,0:T(8,128)(2,1)S(1)}, bf16[2,16,1536]{2,1,0:T(8,128)(2,1)S(1)}, u32[]{:S(2)}, u32[]{:S(2)}) collective-permute-start(bf16[2,16,1536]{2,1,0:T(8,128)(2,1)S(1)} %get-tuple-element.93), channel_id=1, source_target_pairs={{0,32},{8,136},{16,48},{24,152},{32,0},{40,168},{48,16},{56,184},{... | collective-permute-start | bytes 294920 | tf_op jit(solution)/shard_map/ppermute | solution.py:59
  5.0 4.6 %collective-permute-start = (bf16[2,16,1536]{2,1,0:T(8,128)(2,1)S(1)}, bf16[2,16,1536]{2,1,0:T(8,128)(2,1)S(1)}, u32[]{:S(2)}, u32[]{:S(2)}) collective-permute-start(bf16[2,16,1536]{2,1,0:T(8,128)(2,1)S(1)} %get-tuple-element.93), channel_id=1, source_target_pairs={{0,16},{8,72},{16,0},{24,88},{32,48},{40,104},{48,32},{56,120},{64... | collective-permute-start | bytes 294920 | tf_op jit(solution)/shard_map/ppermute | solution.py:59
  9.7 9.4 %collective-permute-start.3 = (bf16[2,4,16,1536]{3,2,1,0:T(8,128)(2,1)S(1)}, bf16[2,4,16,1536]{3,2,1,0:T(8,128)(2,1)S(1)}, u32[]{:S(2)}, u32[]{:S(2)}) collective-permute-start(bf16[2,4,16,1536]{3,2,1,0:T(8,128)(2,1)S(1)} %pad_maximum_fusion.2), channel_id=1, source_target_pairs={{0,128},{8,40},{16,144},{24,56},{32,160},{40,8},{48,176},{56,24},{... | collective-permute-start | bytes 1179656 | tf_op jit(solution)/shard_map/ppermute | solution.py:59
  12.9 10.7 %collective-permute-start.4 = (bf16[2,4,16,1536]{3,2,1,0:T(8,128)(2,1)S(1)}, bf16[2,4,16,1536]{3,2,1,0:T(8,128)(2,1)S(1)}, u32[]{:S(2)}, u32[]{:S(2)}) collective-permute-start(bf16[2,4,16,1536]{3,2,1,0:T(8,128)(2,1)S(1)} %pad_maximum_fusion.2), channel_id=1, source_target_pairs={{0,64},{8,24},{16,80},{24,8},{32,96},{40,56},{48,112},{56,40},{64,... | collective-permute-start | bytes 1179656 | tf_op jit(solution)/shard_map/ppermute | solution.py:59
  13.6 10.2 %collective-permute-start.5 = (bf16[2,4,16,1536]{3,2,1,0:T(8,128)(2,1)S(1)}, bf16[2,4,16,1536]{3,2,1,0:T(8,128)(2,1)S(1)}, u32[]{:S(2)}, u32[]{:S(2)}) collective-permute-start(bf16[2,4,16,1536]{3,2,1,0:T(8,128)(2,1)S(1)} %pad_maximum_fusion.2), channel_id=1, source_target_pairs={{0,192},{8,56},{16,208},{24,40},{32,224},{40,24},{48,240},{56,8},{... | collective-permute-start | bytes 1179656 | tf_op jit(solution)/shard_map/ppermute | solution.py:59
  23.8 1.7 %copy-start.1 = (bf16[2,4,4,16,1536]{4,3,2,1,0:T(8,128)(2,1)}, bf16[2,4,4,16,1536]{4,3,2,1,0:T(8,128)(2,1)S(1)}, u32[]{:S(2)}) copy-start(bf16[2,4,4,16,1536]{4,3,2,1,0:T(8,128)(2,1)S(1)} %bitcast_dynamic-update-slice_fusion) | copy-start | bytes 4718596
  25.5 2.5 %collective-permute-start.6 = (bf16[256,1536]{1,0:T(8,128)(2,1)}, bf16[256,1536]{1,0:T(8,128)(2,1)S(1)}, u32[]{:S(2)}, u32[]{:S(2)}) collective-permute-start(bf16[256,1536]{1,0:T(8,128)(2,1)} %bitcast.13), channel_id=1, source_target_pairs={{0,8},{8,0},{16,24},{24,16},{32,40},{40,32},{48,56},{56,48},{64,72... | collective-permute-start | bytes 2359304 | tf_op jit(solution)/shard_map/ppermute | solution.py:63
  25.5 5.3 %collective-permute-start.7 = (bf16[256,1536]{1,0:T(8,128)(2,1)}, bf16[256,1536]{1,0:T(8,128)(2,1)S(1)}, u32[]{:S(2)}, u32[]{:S(2)}) collective-permute-start(bf16[256,1536]{1,0:T(8,128)(2,1)} %bitcast.260), channel_id=1, source_target_pairs={{0,8},{8,0},{16,24},{24,16},{32,40},{40,32},{48,56},{56,48},{64,72... | collective-permute-start | bytes 2359304 | tf_op jit(solution)/shard_map/ppermute | solution.py:63
  28.0 1.7 %copy-start.3 = (bf16[768,1536]{1,0:T(8,128)(2,1)S(1)}, bf16[768,1536]{1,0:T(8,128)(2,1)}, u32[]{:S(2)}) copy-start(bf16[768,1536]{1,0:T(8,128)(2,1)} %param.8) | copy-start | bytes 7077892
  28.0 1.8 %copy-start.7 = (bf16[1,4,4,16,1536]{4,3,2,1,0:T(8,128)(2,1)S(1)}, bf16[1,4,4,16,1536]{4,3,2,1,0:T(8,128)(2,1)}, u32[]{:S(2)}) copy-start(bf16[1,4,4,16,1536]{4,3,2,1,0:T(8,128)(2,1)} %get-tuple-element.45) | copy-start | bytes 2359300
  31.8 7.3 %collective-permute-start.12 = (bf16[1,2,32,768]{3,2,1,0:T(8,128)(2,1)S(1)}, bf16[1,2,32,768]{3,2,1,0:T(8,128)(2,1)S(1)}, u32[]{:S(2)}, u32[]{:S(2)}) collective-permute-start(bf16[1,2,32,768]{3,2,1,0:T(8,128)(2,1)S(1)} %pad_maximum_fusion.10), channel_id=1, source_target_pairs={{0,1},{1,0},{2,3},{3,2},{4,5},{5,4},{6,7},{7,6},{8,9},{9,8},{10,11... | collective-permute-start | bytes 294920 | tf_op jit(solution)/shard_map/ppermute | solution.py:67
  33.8 8.8 %collective-permute-start.8 = (bf16[1,2,32,768]{3,2,1,0:T(8,128)(2,1)S(1)}, bf16[1,2,32,768]{3,2,1,0:T(8,128)(2,1)S(1)}, u32[]{:S(2)}, u32[]{:S(2)}) collective-permute-start(bf16[1,2,32,768]{3,2,1,0:T(8,128)(2,1)S(1)} %pad_maximum_fusion.11), channel_id=1, source_target_pairs={{0,7},{1,2},{2,1},{3,4},{4,3},{5,6},{6,5},{7,0},{8,15},{9,10},{10,... | collective-permute-start | bytes 294920 | tf_op jit(solution)/shard_map/ppermute | solution.py:67
  39.0 3.7 %copy-start.2 = (bf16[2,4,4,16,1536]{4,3,2,1,0:T(8,128)(2,1)S(1)}, bf16[2,4,4,16,1536]{4,3,2,1,0:T(8,128)(2,1)}, u32[]{:S(2)}) copy-start(bf16[2,4,4,16,1536]{4,3,2,1,0:T(8,128)(2,1)} %copy-done.1) | copy-start | bytes 4718596
  39.2 7.6 %collective-permute-start.13 = (bf16[2,2,32,768]{3,2,1,0:T(8,128)(2,1)S(1)}, bf16[2,2,32,768]{3,2,1,0:T(8,128)(2,1)S(1)}, u32[]{:S(2)}, u32[]{:S(2)}) collective-permute-start(bf16[2,2,32,768]{3,2,1,0:T(8,128)(2,1)S(1)} %pad_maximum_fusion.7), channel_id=1, source_target_pairs={{0,7},{1,2},{2,1},{3,4},{4,3},{5,6},{6,5},{7,0},{8,15},{9,10},{10,... | collective-permute-start | bytes 589832 | tf_op jit(solution)/shard_map/ppermute | solution.py:67
  42.6 6.1 %collective-permute-start.9 = (bf16[2,2,32,768]{3,2,1,0:T(8,128)(2,1)S(1)}, bf16[2,2,32,768]{3,2,1,0:T(8,128)(2,1)S(1)}, u32[]{:S(2)}, u32[]{:S(2)}) collective-permute-start(bf16[2,2,32,768]{3,2,1,0:T(8,128)(2,1)S(1)} %pad_maximum_fusion.6), channel_id=1, source_target_pairs={{0,1},{1,0},{2,3},{3,2},{4,5},{5,4},{6,7},{7,6},{8,9},{9,8},{10,11... | collective-permute-start | bytes 589832 | tf_op jit(solution)/shard_map/ppermute | solution.py:67
  46.8 5.8 %collective-permute-start.14 = (bf16[2,2,32,768]{3,2,1,0:T(8,128)(2,1)S(1)}, bf16[2,2,32,768]{3,2,1,0:T(8,128)(2,1)S(1)}, u32[]{:S(2)}, u32[]{:S(2)}) collective-permute-start(bf16[2,2,32,768]{3,2,1,0:T(8,128)(2,1)S(1)} %fusion.8), channel_id=1, source_target_pairs={{0,1},{1,0},{2,3},{3,2},{4,5},{5,4},{6,7},{7,6},{8,9},{9,8},{10,11... | collective-permute-start | bytes 589832 | tf_op jit(solution)/shard_map/ppermute | solution.py:67
  48.7 8.5 %collective-permute-start.10 = (bf16[2,2,32,768]{3,2,1,0:T(8,128)(2,1)S(1)}, bf16[2,2,32,768]{3,2,1,0:T(8,128)(2,1)S(1)}, u32[]{:S(2)}, u32[]{:S(2)}) collective-permute-start(bf16[2,2,32,768]{3,2,1,0:T(8,128)(2,1)S(1)} %fusion.6), channel_id=1, source_target_pairs={{0,7},{1,2},{2,1},{3,4},{4,3},{5,6},{6,5},{7,0},{8,15},{9,10},{10,... | collective-permute-start | bytes 589832 | tf_op jit(solution)/shard_map/ppermute | solution.py:67
  52.6 7.3 %collective-permute-start.15 = (bf16[2,2,32,768]{3,2,1,0:T(8,128)(2,1)S(1)}, bf16[2,2,32,768]{3,2,1,0:T(8,128)(2,1)S(1)}, u32[]{:S(2)}, u32[]{:S(2)}) collective-permute-start(bf16[2,2,32,768]{3,2,1,0:T(8,128)(2,1)S(1)} %fusion.7), channel_id=1, source_target_pairs={{0,7},{1,2},{2,1},{3,4},{4,3},{5,6},{6,5},{7,0},{8,15},{9,10},{10,... | collective-permute-start | bytes 589832 | tf_op jit(solution)/shard_map/ppermute | solution.py:67
  57.2 7.1 %collective-permute-start.11 = (bf16[2,2,32,768]{3,2,1,0:T(8,128)(2,1)S(1)}, bf16[2,2,32,768]{3,2,1,0:T(8,128)(2,1)S(1)}, u32[]{:S(2)}, u32[]{:S(2)}) collective-permute-start(bf16[2,2,32,768]{3,2,1,0:T(8,128)(2,1)S(1)} %fusion.5), channel_id=1, source_target_pairs={{0,1},{1,0},{2,3},{3,2},{4,5},{5,4},{6,7},{7,6},{8,9},{9,8},{10,11... | collective-permute-start | bytes 589832 | tf_op jit(solution)/shard_map/ppermute | solution.py:67
  57.5 6.8 %copy-start.8 = (f32[768]{0:T(1024)S(1)}, f32[768]{0:T(1024)}, u32[]{:S(2)}) copy-start(f32[768]{0:T(1024)} %param.7) | copy-start | bytes 9220
  64.5 8.6 %collective-permute-start.17 = (bf16[2,2,32,768]{3,2,1,0:T(8,128)(2,1)S(1)}, bf16[2,2,32,768]{3,2,1,0:T(8,128)(2,1)S(1)}, u32[]{:S(2)}, u32[]{:S(2)}) collective-permute-start(bf16[2,2,32,768]{3,2,1,0:T(8,128)(2,1)S(1)} %pad_maximum_fusion.8), channel_id=1, source_target_pairs={{0,7},{1,2},{2,1},{3,4},{4,3},{5,6},{6,5},{7,0},{8,15},{9,10},{10,... | collective-permute-start | bytes 589832 | tf_op jit(solution)/shard_map/ppermute | solution.py:67
  65.0 8.1 %collective-permute-start.16 = (bf16[2,2,32,768]{3,2,1,0:T(8,128)(2,1)S(1)}, bf16[2,2,32,768]{3,2,1,0:T(8,128)(2,1)S(1)}, u32[]{:S(2)}, u32[]{:S(2)}) collective-permute-start(bf16[2,2,32,768]{3,2,1,0:T(8,128)(2,1)S(1)} %pad_maximum_fusion.8), channel_id=1, source_target_pairs={{0,1},{1,0},{2,3},{3,2},{4,5},{5,4},{6,7},{7,6},{8,9},{9,8},{10,11... | collective-permute-start | bytes 589832 | tf_op jit(solution)/shard_map/ppermute | solution.py:67
  73.1 8.2 %collective-permute-start.18 = (bf16[2,2,32,768]{3,2,1,0:T(8,128)(2,1)S(1)}, bf16[2,2,32,768]{3,2,1,0:T(8,128)(2,1)S(1)}, u32[]{:S(2)}, u32[]{:S(2)}) collective-permute-start(bf16[2,2,32,768]{3,2,1,0:T(8,128)(2,1)S(1)} %collective-permute-done.17), channel_id=1, source_target_pairs={{0,1},{1,0},{2,3},{3,2},{4,5},{5,4},{6,7},{7,6},{8,9},{9,8},{10,11... | collective-permute-start | bytes 589832 | tf_op jit(solution)/shard_map/ppermute | solution.py:67
  73.1 7.7 %collective-permute-start.19 = (bf16[2,2,32,768]{3,2,1,0:T(8,128)(2,1)S(1)}, bf16[2,2,32,768]{3,2,1,0:T(8,128)(2,1)S(1)}, u32[]{:S(2)}, u32[]{:S(2)}) collective-permute-start(bf16[2,2,32,768]{3,2,1,0:T(8,128)(2,1)S(1)} %collective-permute-done.16), channel_id=1, source_target_pairs={{0,7},{1,2},{2,1},{3,4},{4,3},{5,6},{6,5},{7,0},{8,15},{9,10},{10,... | collective-permute-start | bytes 589832 | tf_op jit(solution)/shard_map/ppermute | solution.py:67
  80.8 5.7 %collective-permute-start.20 = (bf16[2,2,32,768]{3,2,1,0:T(8,128)(2,1)S(1)}, bf16[2,2,32,768]{3,2,1,0:T(8,128)(2,1)S(1)}, u32[]{:S(2)}, u32[]{:S(2)}) collective-permute-start(bf16[2,2,32,768]{3,2,1,0:T(8,128)(2,1)S(1)} %collective-permute-done.19), channel_id=1, source_target_pairs={{0,1},{1,0},{2,3},{3,2},{4,5},{5,4},{6,7},{7,6},{8,9},{9,8},{10,11... | collective-permute-start | bytes 589832 | tf_op jit(solution)/shard_map/ppermute | solution.py:67
  81.3 6.9 %collective-permute-start.21 = (bf16[2,2,32,768]{3,2,1,0:T(8,128)(2,1)S(1)}, bf16[2,2,32,768]{3,2,1,0:T(8,128)(2,1)S(1)}, u32[]{:S(2)}, u32[]{:S(2)}) collective-permute-start(bf16[2,2,32,768]{3,2,1,0:T(8,128)(2,1)S(1)} %collective-permute-done.18), channel_id=1, source_target_pairs={{0,7},{1,2},{2,1},{3,4},{4,3},{5,6},{6,5},{7,0},{8,15},{9,10},{10,... | collective-permute-start | bytes 589832 | tf_op jit(solution)/shard_map/ppermute | solution.py:67
  86.5 5.9 %collective-permute-start.23 = (bf16[1,2,32,768]{3,2,1,0:T(8,128)(2,1)S(1)}, bf16[1,2,32,768]{3,2,1,0:T(8,128)(2,1)S(1)}, u32[]{:S(2)}, u32[]{:S(2)}) collective-permute-start(bf16[1,2,32,768]{3,2,1,0:T(8,128)(2,1)S(1)} %slice.160), channel_id=1, source_target_pairs={{0,7},{1,2},{2,1},{3,4},{4,3},{5,6},{6,5},{7,0},{8,15},{9,10},{10,... | collective-permute-start | bytes 294920 | tf_op jit(solution)/shard_map/ppermute | solution.py:67
  88.2 4.7 %collective-permute-start.22 = (bf16[1,2,32,768]{3,2,1,0:T(8,128)(2,1)S(1)}, bf16[1,2,32,768]{3,2,1,0:T(8,128)(2,1)S(1)}, u32[]{:S(2)}, u32[]{:S(2)}) collective-permute-start(bf16[1,2,32,768]{3,2,1,0:T(8,128)(2,1)S(1)} %slice.159), channel_id=1, source_target_pairs={{0,1},{1,0},{2,3},{3,2},{4,5},{5,4},{6,7},{7,6},{8,9},{9,8},{10,11... | collective-permute-start | bytes 294920 | tf_op jit(solution)/shard_map/ppermute | solution.py:67
  93.1 1.7 %copy-start.4 = (bf16[768,1536]{1,0:T(8,128)(2,1)S(1)}, bf16[768,1536]{1,0:T(8,128)(2,1)}, u32[]{:S(2)}) copy-start(bf16[768,1536]{1,0:T(8,128)(2,1)} %param.8) | copy-start | bytes 7077892
  93.9 2.4 %collective-permute-start.25 = (bf16[256,1536]{1,0:T(8,128)(2,1)S(1)}, bf16[256,1536]{1,0:T(8,128)(2,1)S(1)}, u32[]{:S(2)}, u32[]{:S(2)}) collective-permute-start(bf16[256,1536]{1,0:T(8,128)(2,1)S(1)} %convolution_convert_fusion), channel_id=1, source_target_pairs={{0,8},{8,0},{16,24},{24,16},{32,40},{40,32},{48,56},{56,48},{64,72... | collective-permute-start | bytes 2359304 | tf_op jit(solution)/shard_map/ppermute | solution.py:63
  95.5 2.4 %collective-permute-start.24 = (bf16[256,1536]{1,0:T(8,128)(2,1)S(1)}, bf16[256,1536]{1,0:T(8,128)(2,1)S(1)}, u32[]{:S(2)}, u32[]{:S(2)}) collective-permute-start(bf16[256,1536]{1,0:T(8,128)(2,1)S(1)} %convolution_convert_fusion.1), channel_id=1, source_target_pairs={{0,8},{8,0},{16,24},{24,16},{32,40},{40,32},{48,56},{56,48},{64,72... | collective-permute-start | bytes 2359304 | tf_op jit(solution)/shard_map/ppermute | solution.py:63
  98.8 4.3 %copy-start.6 = (bf16[512,1536]{1,0:T(8,128)(2,1)S(1)}, bf16[512,1536]{1,0:T(8,128)(2,1)}, u32[]{:S(2)}) copy-start(bf16[512,1536]{1,0:T(8,128)(2,1)} %get-tuple-element.38) | copy-start | bytes 4718596
  98.9 13.3 %collective-permute-start.28 = (bf16[2,4,16,1536]{3,2,0,1:T(8,128)(2,1)S(1)}, bf16[2,4,16,1536]{3,2,0,1:T(8,128)(2,1)S(1)}, u32[]{:S(2)}, u32[]{:S(2)}) collective-permute-start(bf16[2,4,16,1536]{3,2,0,1:T(8,128)(2,1)S(1)} %pad_maximum_fusion.5), channel_id=1, source_target_pairs={{0,192},{8,56},{16,208},{24,40},{32,224},{40,24},{48,240},{56,8},{... | collective-permute-start | bytes 1179656 | tf_op jit(solution)/shard_map/ppermute | solution.py:59
  101.4 10.7 %collective-permute-start.27 = (bf16[2,4,16,1536]{3,2,0,1:T(8,128)(2,1)S(1)}, bf16[2,4,16,1536]{3,2,0,1:T(8,128)(2,1)S(1)}, u32[]{:S(2)}, u32[]{:S(2)}) collective-permute-start(bf16[2,4,16,1536]{3,2,0,1:T(8,128)(2,1)S(1)} %pad_maximum_fusion.4), channel_id=1, source_target_pairs={{0,128},{8,40},{16,144},{24,56},{32,160},{40,8},{48,176},{56,24},{... | collective-permute-start | bytes 1179656 | tf_op jit(solution)/shard_map/ppermute | solution.py:59
  102.4 10.7 %collective-permute-start.26 = (bf16[2,4,16,1536]{3,2,0,1:T(8,128)(2,1)S(1)}, bf16[2,4,16,1536]{3,2,0,1:T(8,128)(2,1)S(1)}, u32[]{:S(2)}, u32[]{:S(2)}) collective-permute-start(bf16[2,4,16,1536]{3,2,0,1:T(8,128)(2,1)S(1)} %pad_maximum_fusion.3), channel_id=1, source_target_pairs={{0,64},{8,24},{16,80},{24,8},{32,96},{40,56},{48,112},{56,40},{64,... | collective-permute-start | bytes 1179656 | tf_op jit(solution)/shard_map/ppermute | solution.py:59
  106.0 1.4 %copy-start.5 = (bf16[512,1536]{1,0:T(8,128)(2,1)S(1)}, bf16[512,1536]{1,0:T(8,128)(2,1)}, u32[]{:S(2)}) copy-start(bf16[512,1536]{1,0:T(8,128)(2,1)} %get-tuple-element.36) | copy-start | bytes 4718596
  113.3 4.8 %collective-permute-start.31 = (bf16[2,16,1536]{2,1,0:T(8,128)(2,1)S(1)}, bf16[2,16,1536]{2,1,0:T(8,128)(2,1)S(1)}, u32[]{:S(2)}, u32[]{:S(2)}) collective-permute-start(bf16[2,16,1536]{2,1,0:T(8,128)(2,1)S(1)} %get-tuple-element.88), channel_id=1, source_target_pairs={{0,48},{8,200},{16,32},{24,216},{32,16},{40,232},{48,0},{56,248},{... | collective-permute-start | bytes 294920 | tf_op jit(solution)/shard_map/ppermute | solution.py:59
  113.8 6.1 %collective-permute-start.30 = (bf16[2,16,1536]{2,1,0:T(8,128)(2,1)S(1)}, bf16[2,16,1536]{2,1,0:T(8,128)(2,1)S(1)}, u32[]{:S(2)}, u32[]{:S(2)}) collective-permute-start(bf16[2,16,1536]{2,1,0:T(8,128)(2,1)S(1)} %get-tuple-element.89), channel_id=1, source_target_pairs={{0,32},{8,136},{16,48},{24,152},{32,0},{40,168},{48,16},{56,184},{... | collective-permute-start | bytes 294920 | tf_op jit(solution)/shard_map/ppermute | solution.py:59
  116.5 4.6 %collective-permute-start.29 = (bf16[2,16,1536]{2,1,0:T(8,128)(2,1)S(1)}, bf16[2,16,1536]{2,1,0:T(8,128)(2,1)S(1)}, u32[]{:S(2)}, u32[]{:S(2)}) collective-permute-start(bf16[2,16,1536]{2,1,0:T(8,128)(2,1)S(1)} %get-tuple-element.87), channel_id=1, source_target_pairs={{0,16},{8,72},{16,0},{24,88},{32,48},{40,104},{48,32},{56,120},{64... | collective-permute-start | bytes 294920 | tf_op jit(solution)/shard_map/ppermute | solution.py:59

commit v5 on v4

--- a/solution.py
+++ b/solution.py
@@ -78,10 +78,12 @@
     got = {k: plane_swap(mine, k, True) for k in (2, 1, 3)}
     line = lax.optimization_barrier(jnp.stack([mine, got[1], got[2], got[3]], axis=1))
     got = {k: plane_swap(line, k, False) for k in (2, 1, 3)}
-    own = jnp.zeros((2, 4, 4, 16, features), BF16)
-    for k, piece in ((0, line), (2, got[2]), (1, got[1]), (3, got[3])):
-        own = lax.dynamic_update_slice_in_dim(own, piece[:, None], k, 1)
-    own = own.reshape(2, HALF, features)
+    own = []
+    for which in range(2):
+        held = jnp.zeros((4, 4, 16, features), BF16)
+        for k, piece in ((0, line), (2, got[2]), (1, got[1]), (3, got[3])):
+            held = lax.dynamic_update_slice_in_dim(held, piece[which][None], k, 0)
+        own.append(held.reshape(HALF, features))
     other = [swap_cores(own[0]), swap_cores(own[1])]
 
     own_pre = matmul(own[0], w_in)

time: 123 us -> 124 us (level)
  waiting for transfers between devices: 57.1 us -> 55.5 us
  other arithmetic: 4.7 us -> 6.1 us
    dynamic_update_slice x5, local copies, waits for them, and re-layouts: 0.34 us -> 3.15 us  [local(): held = lax.dynamic_update_slice_in_dim(held, piece[which][None], k, 0)]
    ppermute x12, waiting for transfers between devices: 19.1 us -> 17.5 us  [plane_swap(): return lax.ppermute(values, 'row', pairs)]
    slice x1, local copies, waits for them, and re-layouts: 1.47 us -> 0.03 us  [local(): held = lax.dynamic_update_slice_in_dim(held, piece[which][None], k, 0)]
    concatenate x1, other arithmetic: 1.86 us -> 3.24 us  [local(): all_inputs = jnp.concatenate([own[0], other[0]])]
    unnamed x18 -> x12, local copies, waits for them, and re-layouts: 3.18 us -> 1.96 us
  transfers between devices with their start and end apart: 32 -> 32, of which waited for: 23 -> 23; matrix products, arithmetic and copies ran while one was open for 12% -> 16% of each run, Pallas kernels for 0% -> 0%
where the time goes in v5:
time: 124 us; the launch traced here: 123 us
  waiting for transfers between devices  55.5 us (45%)
  starting transfers between devices  38.9 us (31%)
  matrix products  14.3 us (12%)
  local copies, waits for them, and re-layouts  6.63 us (5%)
  other arithmetic  6.1 us (5%)
    ppermute x16, waiting for transfers between devices, col_swap(): lax.ppermute(values, 'col', [(i, ring_partner(i, 8, odd_links)) for i in...  35.4 us
    ppermute x16, starting transfers between devices, col_swap(): lax.ppermute(values, 'col', [(i, ring_partner(i, 8, odd_links)) for i in...  21.4 us
    ppermute x12, waiting for transfers between devices, plane_swap(): return lax.ppermute(values, 'row', pairs)  17.5 us
    ppermute x12, starting transfers between devices, plane_swap(): return lax.ppermute(values, 'row', pairs)  16.9 us
    dot_general x2, matrix products, contract_rows(): lax.dot_general(left, right, (((0,), (0,)), ((), ())), preferred_element_...  5.66 us
    dot_general x4, matrix products, matmul(): return jnp.dot(left, right, preferred_element_type=F32)  5.35 us
    dot_general x4, matrix products, contract_cols(): lax.dot_general(left, right, (((1,), (1,)), ((), ())), preferred_element_...  3.26 us
    concatenate x1, other arithmetic, local(): all_inputs = jnp.concatenate([own[0], other[0]])  3.24 us
  transfers between devices with their start and end apart: 32, of which 23 were waited for; matrix products, arithmetic and copies ran while one was open for 16% of the time, Pallas kernels for 0%

profile of v5, /device:TPU:4, one launch (start us, length us, event | category | flops | bytes accessed | tf_op | source)
XLA Modules:
  0.0 122.7 jit_solution(6487271641013693838)
XLA Ops:
  0.6 1.0 fusion.33
  2.3 2.7 %collective-permute-start.1 = (bf16[2,16,1536]{2,1,0:T(8,128)(2,1)S(1)}, bf16[2,16,1536]{2,1,0:T(8,128)(2,1)S(1)}, u32[]{:S(2)}, u32[]{:S(2)}) collective-permute-start(bf16[2,16,1536]{2,1,0:T(8,128)(2,1)S(1)} %get-tuple-element.99), channel_id=1, source_target_pairs={{0,32},{8,136},{16,48},{24,152},{32,0},{40,168},{48,16},{56,184},{... | collective-permute-start | bytes 294920 | tf_op jit(solution)/shard_map/ppermute | solution.py:59
  5.0 0.8 collective-permute-start
  6.3 2.0 %collective-permute-done.1 = bf16[2,16,1536]{2,1,0:T(8,128)(2,1)S(1)} collective-permute-done((bf16[2,16,1536]{2,1,0:T(8,128)(2,1)S(1)}, bf16[2,16,1536]{2,1,0:T(8,128)(2,1)S(1)}, u32[]{:S(2)}, u32[]{:S(2)}) %collective-permute-start.1) | collective-permute-done | bytes 98336 | tf_op jit(solution)/shard_map/ppermute | solution.py:59
  8.4 1.2 collective-permute-done
  9.7 3.3 %collective-permute-start.3 = (bf16[2,4,16,1536]{3,2,1,0:T(8,128)(2,1)S(1)}, bf16[2,4,16,1536]{3,2,1,0:T(8,128)(2,1)S(1)}, u32[]{:S(2)}, u32[]{:S(2)}) collective-permute-start(bf16[2,4,16,1536]{3,2,1,0:T(8,128)(2,1)S(1)} %pad_maximum_fusion.2), channel_id=1, source_target_pairs={{0,128},{8,40},{16,144},{24,56},{32,160},{40,8},{48,176},{56,24},{... | collective-permute-start | bytes 1179656 | tf_op jit(solution)/shard_map/ppermute | solution.py:59
  14.1 1.0 dynamic_update_slice.48
  15.1 4.0 %collective-permute-done.3 = bf16[2,4,16,1536]{3,2,1,0:T(8,128)(2,1)S(1)} collective-permute-done((bf16[2,4,16,1536]{3,2,1,0:T(8,128)(2,1)S(1)}, bf16[2,4,16,1536]{3,2,1,0:T(8,128)(2,1)S(1)}, u32[]{:S(2)}, u32[]{:S(2)}) %collective-permute-start.3) | collective-permute-done | bytes 393248 | tf_op jit(solution)/shard_map/ppermute | solution.py:59
  19.8 3.8 %collective-permute-done.4 = bf16[2,4,16,1536]{3,2,1,0:T(8,128)(2,1)S(1)} collective-permute-done((bf16[2,4,16,1536]{3,2,1,0:T(8,128)(2,1)S(1)}, bf16[2,4,16,1536]{3,2,1,0:T(8,128)(2,1)S(1)}, u32[]{:S(2)}, u32[]{:S(2)}) %collective-permute-start.4) | collective-permute-done | bytes 393248 | tf_op jit(solution)/shard_map/ppermute | solution.py:59
  25.5 1.9 %fusion.42 = f32[256,768]{1,0:T(8,128)S(1)} fusion(bf16[256,1536]{1,0:T(8,128)(2,1)} %bitcast.9, bf16[1536,768]{1,0:T(8,128)(2,1)S(1)} %copy-done), kind=kOutput, calls=%fused_computation.141 | convolution fusion | flops 603979776 | bytes 3932160 | tf_op jit(solution)/shard_map/dot_general | solution.py:27
  27.6 1.2 collective-permute-done.6
  28.8 1.9 %fusion.43 = f32[256,768]{1,0:T(8,128)S(1)} fusion(bf16[256,1536]{1,0:T(8,128)(2,1)} %collective-permute-done.6, bf16[1536,768]{1,0:T(8,128)(2,1)S(1)} %copy-done), kind=kOutput, calls=%fused_computation.142 | convolution fusion | flops 603979776 | bytes 3932160 | tf_op jit(solution)/shard_map/dot_general | solution.py:27
  30.7 0.8 fusion.44
  31.6 0.8 fusion.45
  32.6 2.0 %collective-permute-start.12 = (bf16[1,2,32,768]{3,2,1,0:T(8,128)(2,1)S(1)}, bf16[1,2,32,768]{3,2,1,0:T(8,128)(2,1)S(1)}, u32[]{:S(2)}, u32[]{:S(2)}) collective-permute-start(bf16[1,2,32,768]{3,2,1,0:T(8,128)(2,1)S(1)} %pad_maximum_fusion.10), channel_id=1, source_target_pairs={{0,1},{1,0},{2,3},{3,2},{4,5},{5,4},{6,7},{7,6},{8,9},{9,8},{10,11... | collective-permute-start | bytes 294920 | tf_op jit(solution)/shard_map/ppermute | solution.py:67
  34.6 5.0 %collective-permute-start.8 = (bf16[1,2,32,768]{3,2,1,0:T(8,128)(2,1)S(1)}, bf16[1,2,32,768]{3,2,1,0:T(8,128)(2,1)S(1)}, u32[]{:S(2)}, u32[]{:S(2)}) collective-permute-start(bf16[1,2,32,768]{3,2,1,0:T(8,128)(2,1)S(1)} %pad_maximum_fusion.11), channel_id=1, source_target_pairs={{0,7},{1,2},{2,1},{3,4},{4,3},{5,6},{6,5},{7,0},{8,15},{9,10},{10,... | collective-permute-start | bytes 294920 | tf_op jit(solution)/shard_map/ppermute | solution.py:67
  40.0 3.5 %collective-permute-start.13 = (bf16[2,2,32,768]{3,2,1,0:T(8,128)(2,1)S(1)}, bf16[2,2,32,768]{3,2,1,0:T(8,128)(2,1)S(1)}, u32[]{:S(2)}, u32[]{:S(2)}) collective-permute-start(bf16[2,2,32,768]{3,2,1,0:T(8,128)(2,1)S(1)} %pad_maximum_fusion.7), channel_id=1, source_target_pairs={{0,7},{1,2},{2,1},{3,4},{4,3},{5,6},{6,5},{7,0},{8,15},{9,10},{10,... | collective-permute-start | bytes 589832 | tf_op jit(solution)/shard_map/ppermute | solution.py:67
  43.7 4.2 %collective-permute-done.13 = bf16[2,2,32,768]{3,2,1,0:T(8,128)(2,1)S(1)} collective-permute-done((bf16[2,2,32,768]{3,2,1,0:T(8,128)(2,1)S(1)}, bf16[2,2,32,768]{3,2,1,0:T(8,128)(2,1)S(1)}, u32[]{:S(2)}, u32[]{:S(2)}) %collective-permute-start.13) | collective-permute-done | bytes 196640 | tf_op jit(solution)/shard_map/ppermute | solution.py:67
  48.0 1.6 %collective-permute-done.9 = bf16[2,2,32,768]{3,2,1,0:T(8,128)(2,1)S(1)} collective-permute-done((bf16[2,2,32,768]{3,2,1,0:T(8,128)(2,1)S(1)}, bf16[2,2,32,768]{3,2,1,0:T(8,128)(2,1)S(1)}, u32[]{:S(2)}, u32[]{:S(2)}) %collective-permute-start.9) | collective-permute-done | bytes 196640 | tf_op jit(solution)/shard_map/ppermute | solution.py:67
  49.7 1.8 %collective-permute-start.10 = (bf16[2,2,32,768]{3,2,1,0:T(8,128)(2,1)S(1)}, bf16[2,2,32,768]{3,2,1,0:T(8,128)(2,1)S(1)}, u32[]{:S(2)}, u32[]{:S(2)}) collective-permute-start(bf16[2,2,32,768]{3,2,1,0:T(8,128)(2,1)S(1)} %fusion.6), channel_id=1, source_target_pairs={{0,7},{1,2},{2,1},{3,4},{4,3},{5,6},{6,5},{7,0},{8,15},{9,10},{10,... | collective-permute-start | bytes 589832 | tf_op jit(solution)/shard_map/ppermute | solution.py:67
  51.4 2.3 %collective-permute-done.14 = bf16[2,2,32,768]{3,2,1,0:T(8,128)(2,1)S(1)} collective-permute-done((bf16[2,2,32,768]{3,2,1,0:T(8,128)(2,1)S(1)}, bf16[2,2,32,768]{3,2,1,0:T(8,128)(2,1)S(1)}, u32[]{:S(2)}, u32[]{:S(2)}) %collective-permute-start.14) | collective-permute-done | bytes 196640 | tf_op jit(solution)/shard_map/ppermute | solution.py:67
  53.7 3.0 %collective-permute-start.15 = (bf16[2,2,32,768]{3,2,1,0:T(8,128)(2,1)S(1)}, bf16[2,2,32,768]{3,2,1,0:T(8,128)(2,1)S(1)}, u32[]{:S(2)}, u32[]{:S(2)}) collective-permute-start(bf16[2,2,32,768]{3,2,1,0:T(8,128)(2,1)S(1)} %fusion.7), channel_id=1, source_target_pairs={{0,7},{1,2},{2,1},{3,4},{4,3},{5,6},{6,5},{7,0},{8,15},{9,10},{10,... | collective-permute-start | bytes 589832 | tf_op jit(solution)/shard_map/ppermute | solution.py:67
  56.8 1.2 collective-permute-done.10
  58.3 3.2 %pad_maximum_fusion = (bf16[512,1536]{1,0:T(8,128)(2,1)}, bf16[512,1536]{1,0:T(8,128)(2,1)}) fusion(bf16[256,1536]{1,0:T(8,128)(2,1)} %collective-permute-done.6, bf16[256,1536]{1,0:T(8,128)(2,1)} %bitcast.9, bf16[256,1536]{1,0:T(8,128)(2,1)S(1)} %collective-permute-done.7, bf16[256,1536]{1,0:T(8,128)(2,1)S(1)} %bitcast.240), kind=kLoop, calls=%fused_computation.4 | loop fusion | flops 6291456 | bytes 6291456 | tf_op jit(solution)/shard_map/concatenate | solution.py:107
  61.5 3.5 %collective-permute-done.11 = bf16[2,2,32,768]{3,2,1,0:T(8,128)(2,1)S(1)} collective-permute-done((bf16[2,2,32,768]{3,2,1,0:T(8,128)(2,1)S(1)}, bf16[2,2,32,768]{3,2,1,0:T(8,128)(2,1)S(1)}, u32[]{:S(2)}, u32[]{:S(2)}) %collective-permute-start.11) | collective-permute-done | bytes 196640 | tf_op jit(solution)/shard_map/ppermute | solution.py:67
  65.3 1.0 collective-permute-start.17
  66.8 7.1 %collective-permute-done.17 = bf16[2,2,32,768]{3,2,1,0:T(8,128)(2,1)S(1)} collective-permute-done((bf16[2,2,32,768]{3,2,1,0:T(8,128)(2,1)S(1)}, bf16[2,2,32,768]{3,2,1,0:T(8,128)(2,1)S(1)}, u32[]{:S(2)}, u32[]{:S(2)}) %collective-permute-start.17) | collective-permute-done | bytes 196640 | tf_op jit(solution)/shard_map/ppermute | solution.py:67
  73.9 1.6 %collective-permute-start.19 = (bf16[2,2,32,768]{3,2,1,0:T(8,128)(2,1)S(1)}, bf16[2,2,32,768]{3,2,1,0:T(8,128)(2,1)S(1)}, u32[]{:S(2)}, u32[]{:S(2)}) collective-permute-start(bf16[2,2,32,768]{3,2,1,0:T(8,128)(2,1)S(1)} %collective-permute-done.16), channel_id=1, source_target_pairs={{0,7},{1,2},{2,1},{3,4},{4,3},{5,6},{6,5},{7,0},{8,15},{9,10},{10,... | collective-permute-start | bytes 589832 | tf_op jit(solution)/shard_map/ppermute | solution.py:67
  75.5 6.2 %collective-permute-done.19 = bf16[2,2,32,768]{3,2,1,0:T(8,128)(2,1)S(1)} collective-permute-done((bf16[2,2,32,768]{3,2,1,0:T(8,128)(2,1)S(1)}, bf16[2,2,32,768]{3,2,1,0:T(8,128)(2,1)S(1)}, u32[]{:S(2)}, u32[]{:S(2)}) %collective-permute-start.19) | collective-permute-done | bytes 196640 | tf_op jit(solution)/shard_map/ppermute | solution.py:67
  82.2 0.8 collective-permute-start.21
  83.0 4.3 %collective-permute-done.20 = bf16[2,2,32,768]{3,2,1,0:T(8,128)(2,1)S(1)} collective-permute-done((bf16[2,2,32,768]{3,2,1,0:T(8,128)(2,1)S(1)}, bf16[2,2,32,768]{3,2,1,0:T(8,128)(2,1)S(1)}, u32[]{:S(2)}, u32[]{:S(2)}) %collective-permute-start.20) | collective-permute-done | bytes 196640 | tf_op jit(solution)/shard_map/ppermute | solution.py:67
  87.4 1.0 collective-permute-start.23
  89.5 3.8 %collective-permute-done.23 = bf16[1,2,32,768]{3,2,1,0:T(8,128)(2,1)S(1)} collective-permute-done((bf16[1,2,32,768]{3,2,1,0:T(8,128)(2,1)S(1)}, bf16[1,2,32,768]{3,2,1,0:T(8,128)(2,1)S(1)}, u32[]{:S(2)}, u32[]{:S(2)}) %collective-permute-start.23) | collective-permute-done | bytes 98336 | tf_op jit(solution)/shard_map/ppermute | solution.py:67
  93.9 0.8 convolution_convert_fusion
  95.6 0.8 convolution_convert_fusion.1
  97.1 0.8 fusion.40
  98.7 0.8 fusion.41
  99.7 2.0 %collective-permute-start.28 = (bf16[2,4,16,1536]{3,2,0,1:T(8,128)(2,1)S(1)}, bf16[2,4,16,1536]{3,2,0,1:T(8,128)(2,1)S(1)}, u32[]{:S(2)}, u32[]{:S(2)}) collective-permute-start(bf16[2,4,16,1536]{3,2,0,1:T(8,128)(2,1)S(1)} %pad_maximum_fusion.5), channel_id=1, source_target_pairs={{0,192},{8,56},{16,208},{24,40},{32,224},{40,24},{48,240},{56,8},{... | collective-permute-start | bytes 1179656 | tf_op jit(solution)/shard_map/ppermute | solution.py:59
  101.7 1.5 %collective-permute-start.27 = (bf16[2,4,16,1536]{3,2,0,1:T(8,128)(2,1)S(1)}, bf16[2,4,16,1536]{3,2,0,1:T(8,128)(2,1)S(1)}, u32[]{:S(2)}, u32[]{:S(2)}) collective-permute-start(bf16[2,4,16,1536]{3,2,0,1:T(8,128)(2,1)S(1)} %pad_maximum_fusion.4), channel_id=1, source_target_pairs={{0,128},{8,40},{16,144},{24,56},{32,160},{40,8},{48,176},{56,24},{... | collective-permute-start | bytes 1179656 | tf_op jit(solution)/shard_map/ppermute | solution.py:59
  104.0 2.8 %multiply_convert_fusion = bf16[768,1536]{1,0:T(8,128)(2,1)} fusion(bf16[512,768]{1,0:T(8,128)(2,1)S(1)} %bitcast.250, bf16[512,1536]{1,0:T(8,128)(2,1)S(1)} %copy-done.4), kind=kOutput, calls=%fused_computation | convolution fusion | flops 1210318848 | bytes 4718592 | tf_op jit(solution)/shard_map/dot_general | solution.py:31
  107.1 1.2 copy-done.3
  108.3 2.8 %multiply_convert_fusion.1 = bf16[1536,768]{1,0:T(8,128)(2,1)} fusion(bf16[512,1536]{1,0:T(8,128)(2,1)S(1)} %copy-done.3, bf16[512,768]{1,0:T(8,128)(2,1)S(1)} %bitcast.249), kind=kOutput, calls=%fused_computation.1 | convolution fusion | flops 1210318848 | bytes 4718592 | tf_op jit(solution)/shard_map/dot_general | solution.py:31
  111.1 1.9 %collective-permute-done.28 = bf16[2,4,16,1536]{3,2,0,1:T(8,128)(2,1)S(1)} collective-permute-done((bf16[2,4,16,1536]{3,2,0,1:T(8,128)(2,1)S(1)}, bf16[2,4,16,1536]{3,2,0,1:T(8,128)(2,1)S(1)}, u32[]{:S(2)}, u32[]{:S(2)}) %collective-permute-start.28) | collective-permute-done | bytes 393248 | tf_op jit(solution)/shard_map/ppermute | solution.py:59
  113.0 0.9 collective-permute-done.26
  114.6 2.7 %collective-permute-start.30 = (bf16[2,16,1536]{2,1,0:T(8,128)(2,1)S(1)}, bf16[2,16,1536]{2,1,0:T(8,128)(2,1)S(1)}, u32[]{:S(2)}, u32[]{:S(2)}) collective-permute-start(bf16[2,16,1536]{2,1,0:T(8,128)(2,1)S(1)} %get-tuple-element.87), channel_id=1, source_target_pairs={{0,32},{8,136},{16,48},{24,152},{32,0},{40,168},{48,16},{56,184},{... | collective-permute-start | bytes 294920 | tf_op jit(solution)/shard_map/ppermute | solution.py:59
  117.3 1.0 collective-permute-start.29
  118.9 1.8 %collective-permute-done.30 = bf16[2,16,1536]{2,1,0:T(8,128)(2,1)S(1)} collective-permute-done((bf16[2,16,1536]{2,1,0:T(8,128)(2,1)S(1)}, bf16[2,16,1536]{2,1,0:T(8,128)(2,1)S(1)}, u32[]{:S(2)}, u32[]{:S(2)}) %collective-permute-start.30) | collective-permute-done | bytes 98336 | tf_op jit(solution)/shard_map/ppermute | solution.py:59
  120.7 1.2 %collective-permute-done.29 = bf16[2,16,1536]{2,1,0:T(8,128)(2,1)S(1)} collective-permute-done((bf16[2,16,1536]{2,1,0:T(8,128)(2,1)S(1)}, bf16[2,16,1536]{2,1,0:T(8,128)(2,1)S(1)}, u32[]{:S(2)}, u32[]{:S(2)}) %collective-permute-start.29) | collective-permute-done | bytes 98336 | tf_op jit(solution)/shard_map/ppermute | solution.py:59
  (103 shorter events, 14.7 us)
Async XLA Ops:
  0.6 24.9 %copy-start = (bf16[1536,768]{1,0:T(8,128)(2,1)S(1)}, bf16[1536,768]{1,0:T(8,128)(2,1)}, u32[]{:S(2)}) copy-start(bf16[1536,768]{1,0:T(8,128)(2,1)} %param.6) | copy-start | bytes 7077892
  1.6 4.7 %collective-permute-start.2 = (bf16[2,16,1536]{2,1,0:T(8,128)(2,1)S(1)}, bf16[2,16,1536]{2,1,0:T(8,128)(2,1)S(1)}, u32[]{:S(2)}, u32[]{:S(2)}) collective-permute-start(bf16[2,16,1536]{2,1,0:T(8,128)(2,1)S(1)} %get-tuple-element.99), channel_id=1, source_target_pairs={{0,48},{8,200},{16,32},{24,216},{32,16},{40,232},{48,0},{56,248},{... | collective-permute-start | bytes 294920 | tf_op jit(solution)/shard_map/ppermute | solution.py:59
  2.3 6.1 %collective-permute-start.1 = (bf16[2,16,1536]{2,1,0:T(8,128)(2,1)S(1)}, bf16[2,16,1536]{2,1,0:T(8,128)(2,1)S(1)}, u32[]{:S(2)}, u32[]{:S(2)}) collective-permute-start(bf16[2,16,1536]{2,1,0:T(8,128)(2,1)S(1)} %get-tuple-element.99), channel_id=1, source_target_pairs={{0,32},{8,136},{16,48},{24,152},{32,0},{40,168},{48,16},{56,184},{... | collective-permute-start | bytes 294920 | tf_op jit(solution)/shard_map/ppermute | solution.py:59
  5.0 4.6 %collective-permute-start = (bf16[2,16,1536]{2,1,0:T(8,128)(2,1)S(1)}, bf16[2,16,1536]{2,1,0:T(8,128)(2,1)S(1)}, u32[]{:S(2)}, u32[]{:S(2)}) collective-permute-start(bf16[2,16,1536]{2,1,0:T(8,128)(2,1)S(1)} %get-tuple-element.99), channel_id=1, source_target_pairs={{0,16},{8,72},{16,0},{24,88},{32,48},{40,104},{48,32},{56,120},{64... | collective-permute-start | bytes 294920 | tf_op jit(solution)/shard_map/ppermute | solution.py:59
  9.7 9.4 %collective-permute-start.3 = (bf16[2,4,16,1536]{3,2,1,0:T(8,128)(2,1)S(1)}, bf16[2,4,16,1536]{3,2,1,0:T(8,128)(2,1)S(1)}, u32[]{:S(2)}, u32[]{:S(2)}) collective-permute-start(bf16[2,4,16,1536]{3,2,1,0:T(8,128)(2,1)S(1)} %pad_maximum_fusion.2), channel_id=1, source_target_pairs={{0,128},{8,40},{16,144},{24,56},{32,160},{40,8},{48,176},{56,24},{... | collective-permute-start | bytes 1179656 | tf_op jit(solution)/shard_map/ppermute | solution.py:59
  12.9 10.7 %collective-permute-start.4 = (bf16[2,4,16,1536]{3,2,1,0:T(8,128)(2,1)S(1)}, bf16[2,4,16,1536]{3,2,1,0:T(8,128)(2,1)S(1)}, u32[]{:S(2)}, u32[]{:S(2)}) collective-permute-start(bf16[2,4,16,1536]{3,2,1,0:T(8,128)(2,1)S(1)} %pad_maximum_fusion.2), channel_id=1, source_target_pairs={{0,64},{8,24},{16,80},{24,8},{32,96},{40,56},{48,112},{56,40},{64,... | collective-permute-start | bytes 1179656 | tf_op jit(solution)/shard_map/ppermute | solution.py:59
  13.6 10.7 %collective-permute-start.5 = (bf16[2,4,16,1536]{3,2,1,0:T(8,128)(2,1)S(1)}, bf16[2,4,16,1536]{3,2,1,0:T(8,128)(2,1)S(1)}, u32[]{:S(2)}, u32[]{:S(2)}) collective-permute-start(bf16[2,4,16,1536]{3,2,1,0:T(8,128)(2,1)S(1)} %pad_maximum_fusion.2), channel_id=1, source_target_pairs={{0,192},{8,56},{16,208},{24,40},{32,224},{40,24},{48,240},{56,8},{... | collective-permute-start | bytes 1179656 | tf_op jit(solution)/shard_map/ppermute | solution.py:59
  25.0 3.7 %collective-permute-start.6 = (bf16[256,1536]{1,0:T(8,128)(2,1)}, bf16[256,1536]{1,0:T(8,128)(2,1)}, u32[]{:S(2)}, u32[]{:S(2)}) collective-permute-start(bf16[256,1536]{1,0:T(8,128)(2,1)} %bitcast.9), channel_id=1, source_target_pairs={{0,8},{8,0},{16,24},{24,16},{32,40},{40,32},{48,56},{56,48},{64,72... | collective-permute-start | bytes 2359304 | tf_op jit(solution)/shard_map/ppermute | solution.py:63
  25.0 6.6 %collective-permute-start.7 = (bf16[256,1536]{1,0:T(8,128)(2,1)S(1)}, bf16[256,1536]{1,0:T(8,128)(2,1)S(1)}, u32[]{:S(2)}, u32[]{:S(2)}) collective-permute-start(bf16[256,1536]{1,0:T(8,128)(2,1)S(1)} %bitcast.238), channel_id=1, source_target_pairs={{0,8},{8,0},{16,24},{24,16},{32,40},{40,32},{48,56},{56,48},{64,72... | collective-permute-start | bytes 2359304 | tf_op jit(solution)/shard_map/ppermute | solution.py:63
  27.6 3.1 %copy-start.1 = (bf16[768,1536]{1,0:T(8,128)(2,1)S(1)}, bf16[768,1536]{1,0:T(8,128)(2,1)}, u32[]{:S(2)}) copy-start(bf16[768,1536]{1,0:T(8,128)(2,1)} %param.8) | copy-start | bytes 7077892
  32.6 7.3 %collective-permute-start.12 = (bf16[1,2,32,768]{3,2,1,0:T(8,128)(2,1)S(1)}, bf16[1,2,32,768]{3,2,1,0:T(8,128)(2,1)S(1)}, u32[]{:S(2)}, u32[]{:S(2)}) collective-permute-start(bf16[1,2,32,768]{3,2,1,0:T(8,128)(2,1)S(1)} %pad_maximum_fusion.10), channel_id=1, source_target_pairs={{0,1},{1,0},{2,3},{3,2},{4,5},{5,4},{6,7},{7,6},{8,9},{9,8},{10,11... | collective-permute-start | bytes 294920 | tf_op jit(solution)/shard_map/ppermute | solution.py:67
  34.6 8.9 %collective-permute-start.8 = (bf16[1,2,32,768]{3,2,1,0:T(8,128)(2,1)S(1)}, bf16[1,2,32,768]{3,2,1,0:T(8,128)(2,1)S(1)}, u32[]{:S(2)}, u32[]{:S(2)}) collective-permute-start(bf16[1,2,32,768]{3,2,1,0:T(8,128)(2,1)S(1)} %pad_maximum_fusion.11), channel_id=1, source_target_pairs={{0,7},{1,2},{2,1},{3,4},{4,3},{5,6},{6,5},{7,0},{8,15},{9,10},{10,... | collective-permute-start | bytes 294920 | tf_op jit(solution)/shard_map/ppermute | solution.py:67
  40.0 7.9 %collective-permute-start.13 = (bf16[2,2,32,768]{3,2,1,0:T(8,128)(2,1)S(1)}, bf16[2,2,32,768]{3,2,1,0:T(8,128)(2,1)S(1)}, u32[]{:S(2)}, u32[]{:S(2)}) collective-permute-start(bf16[2,2,32,768]{3,2,1,0:T(8,128)(2,1)S(1)} %pad_maximum_fusion.7), channel_id=1, source_target_pairs={{0,7},{1,2},{2,1},{3,4},{4,3},{5,6},{6,5},{7,0},{8,15},{9,10},{10,... | collective-permute-start | bytes 589832 | tf_op jit(solution)/shard_map/ppermute | solution.py:67
  43.6 6.0 %collective-permute-start.9 = (bf16[2,2,32,768]{3,2,1,0:T(8,128)(2,1)S(1)}, bf16[2,2,32,768]{3,2,1,0:T(8,128)(2,1)S(1)}, u32[]{:S(2)}, u32[]{:S(2)}) collective-permute-start(bf16[2,2,32,768]{3,2,1,0:T(8,128)(2,1)S(1)} %pad_maximum_fusion.6), channel_id=1, source_target_pairs={{0,1},{1,0},{2,3},{3,2},{4,5},{5,4},{6,7},{7,6},{8,9},{9,8},{10,11... | collective-permute-start | bytes 589832 | tf_op jit(solution)/shard_map/ppermute | solution.py:67
  47.9 5.8 %collective-permute-start.14 = (bf16[2,2,32,768]{3,2,1,0:T(8,128)(2,1)S(1)}, bf16[2,2,32,768]{3,2,1,0:T(8,128)(2,1)S(1)}, u32[]{:S(2)}, u32[]{:S(2)}) collective-permute-start(bf16[2,2,32,768]{3,2,1,0:T(8,128)(2,1)S(1)} %fusion.8), channel_id=1, source_target_pairs={{0,1},{1,0},{2,3},{3,2},{4,5},{5,4},{6,7},{7,6},{8,9},{9,8},{10,11... | collective-permute-start | bytes 589832 | tf_op jit(solution)/shard_map/ppermute | solution.py:67
  49.7 8.3 %collective-permute-start.10 = (bf16[2,2,32,768]{3,2,1,0:T(8,128)(2,1)S(1)}, bf16[2,2,32,768]{3,2,1,0:T(8,128)(2,1)S(1)}, u32[]{:S(2)}, u32[]{:S(2)}) collective-permute-start(bf16[2,2,32,768]{3,2,1,0:T(8,128)(2,1)S(1)} %fusion.6), channel_id=1, source_target_pairs={{0,7},{1,2},{2,1},{3,4},{4,3},{5,6},{6,5},{7,0},{8,15},{9,10},{10,... | collective-permute-start | bytes 589832 | tf_op jit(solution)/shard_map/ppermute | solution.py:67
  53.7 7.8 %collective-permute-start.15 = (bf16[2,2,32,768]{3,2,1,0:T(8,128)(2,1)S(1)}, bf16[2,2,32,768]{3,2,1,0:T(8,128)(2,1)S(1)}, u32[]{:S(2)}, u32[]{:S(2)}) collective-permute-start(bf16[2,2,32,768]{3,2,1,0:T(8,128)(2,1)S(1)} %fusion.7), channel_id=1, source_target_pairs={{0,7},{1,2},{2,1},{3,4},{4,3},{5,6},{6,5},{7,0},{8,15},{9,10},{10,... | collective-permute-start | bytes 589832 | tf_op jit(solution)/shard_map/ppermute | solution.py:67
  58.0 7.1 %copy-start.5 = (f32[768]{0:T(1024)S(1)}, f32[768]{0:T(1024)}, u32[]{:S(2)}) copy-start(f32[768]{0:T(1024)} %param.7) | copy-start | bytes 9220
  58.0 7.0 %collective-permute-start.11 = (bf16[2,2,32,768]{3,2,1,0:T(8,128)(2,1)S(1)}, bf16[2,2,32,768]{3,2,1,0:T(8,128)(2,1)S(1)}, u32[]{:S(2)}, u32[]{:S(2)}) collective-permute-start(bf16[2,2,32,768]{3,2,1,0:T(8,128)(2,1)S(1)} %fusion.5), channel_id=1, source_target_pairs={{0,1},{1,0},{2,3},{3,2},{4,5},{5,4},{6,7},{7,6},{8,9},{9,8},{10,11... | collective-permute-start | bytes 589832 | tf_op jit(solution)/shard_map/ppermute | solution.py:67
  65.3 8.6 %collective-permute-start.17 = (bf16[2,2,32,768]{3,2,1,0:T(8,128)(2,1)S(1)}, bf16[2,2,32,768]{3,2,1,0:T(8,128)(2,1)S(1)}, u32[]{:S(2)}, u32[]{:S(2)}) collective-permute-start(bf16[2,2,32,768]{3,2,1,0:T(8,128)(2,1)S(1)} %pad_maximum_fusion.8), channel_id=1, source_target_pairs={{0,7},{1,2},{2,1},{3,4},{4,3},{5,6},{6,5},{7,0},{8,15},{9,10},{10,... | collective-permute-start | bytes 589832 | tf_op jit(solution)/shard_map/ppermute | solution.py:67
  66.3 7.6 %collective-permute-start.16 = (bf16[2,2,32,768]{3,2,1,0:T(8,128)(2,1)S(1)}, bf16[2,2,32,768]{3,2,1,0:T(8,128)(2,1)S(1)}, u32[]{:S(2)}, u32[]{:S(2)}) collective-permute-start(bf16[2,2,32,768]{3,2,1,0:T(8,128)(2,1)S(1)} %pad_maximum_fusion.8), channel_id=1, source_target_pairs={{0,1},{1,0},{2,3},{3,2},{4,5},{5,4},{6,7},{7,6},{8,9},{9,8},{10,11... | collective-permute-start | bytes 589832 | tf_op jit(solution)/shard_map/ppermute | solution.py:67
  73.9 8.3 %collective-permute-start.18 = (bf16[2,2,32,768]{3,2,1,0:T(8,128)(2,1)S(1)}, bf16[2,2,32,768]{3,2,1,0:T(8,128)(2,1)S(1)}, u32[]{:S(2)}, u32[]{:S(2)}) collective-permute-start(bf16[2,2,32,768]{3,2,1,0:T(8,128)(2,1)S(1)} %collective-permute-done.17), channel_id=1, source_target_pairs={{0,1},{1,0},{2,3},{3,2},{4,5},{5,4},{6,7},{7,6},{8,9},{9,8},{10,11... | collective-permute-start | bytes 589832 | tf_op jit(solution)/shard_map/ppermute | solution.py:67
  73.9 7.8 %collective-permute-start.19 = (bf16[2,2,32,768]{3,2,1,0:T(8,128)(2,1)S(1)}, bf16[2,2,32,768]{3,2,1,0:T(8,128)(2,1)S(1)}, u32[]{:S(2)}, u32[]{:S(2)}) collective-permute-start(bf16[2,2,32,768]{3,2,1,0:T(8,128)(2,1)S(1)} %collective-permute-done.16), channel_id=1, source_target_pairs={{0,7},{1,2},{2,1},{3,4},{4,3},{5,6},{6,5},{7,0},{8,15},{9,10},{10,... | collective-permute-start | bytes 589832 | tf_op jit(solution)/shard_map/ppermute | solution.py:67
  81.7 5.7 %collective-permute-start.20 = (bf16[2,2,32,768]{3,2,1,0:T(8,128)(2,1)S(1)}, bf16[2,2,32,768]{3,2,1,0:T(8,128)(2,1)S(1)}, u32[]{:S(2)}, u32[]{:S(2)}) collective-permute-start(bf16[2,2,32,768]{3,2,1,0:T(8,128)(2,1)S(1)} %collective-permute-done.19), channel_id=1, source_target_pairs={{0,1},{1,0},{2,3},{3,2},{4,5},{5,4},{6,7},{7,6},{8,9},{9,8},{10,11... | collective-permute-start | bytes 589832 | tf_op jit(solution)/shard_map/ppermute | solution.py:67
  82.2 6.9 %collective-permute-start.21 = (bf16[2,2,32,768]{3,2,1,0:T(8,128)(2,1)S(1)}, bf16[2,2,32,768]{3,2,1,0:T(8,128)(2,1)S(1)}, u32[]{:S(2)}, u32[]{:S(2)}) collective-permute-start(bf16[2,2,32,768]{3,2,1,0:T(8,128)(2,1)S(1)} %collective-permute-done.18), channel_id=1, source_target_pairs={{0,7},{1,2},{2,1},{3,4},{4,3},{5,6},{6,5},{7,0},{8,15},{9,10},{10,... | collective-permute-start | bytes 589832 | tf_op jit(solution)/shard_map/ppermute | solution.py:67
  87.4 5.9 %collective-permute-start.23 = (bf16[1,2,32,768]{3,2,1,0:T(8,128)(2,1)S(1)}, bf16[1,2,32,768]{3,2,1,0:T(8,128)(2,1)S(1)}, u32[]{:S(2)}, u32[]{:S(2)}) collective-permute-start(bf16[1,2,32,768]{3,2,1,0:T(8,128)(2,1)S(1)} %slice.178), channel_id=1, source_target_pairs={{0,7},{1,2},{2,1},{3,4},{4,3},{5,6},{6,5},{7,0},{8,15},{9,10},{10,... | collective-permute-start | bytes 294920 | tf_op jit(solution)/shard_map/ppermute | solution.py:67
  89.1 4.7 %collective-permute-start.22 = (bf16[1,2,32,768]{3,2,1,0:T(8,128)(2,1)S(1)}, bf16[1,2,32,768]{3,2,1,0:T(8,128)(2,1)S(1)}, u32[]{:S(2)}, u32[]{:S(2)}) collective-permute-start(bf16[1,2,32,768]{3,2,1,0:T(8,128)(2,1)S(1)} %slice.177), channel_id=1, source_target_pairs={{0,1},{1,0},{2,3},{3,2},{4,5},{5,4},{6,7},{7,6},{8,9},{9,8},{10,11... | collective-permute-start | bytes 294920 | tf_op jit(solution)/shard_map/ppermute | solution.py:67
  93.9 1.7 %copy-start.2 = (bf16[768,1536]{1,0:T(8,128)(2,1)S(1)}, bf16[768,1536]{1,0:T(8,128)(2,1)}, u32[]{:S(2)}) copy-start(bf16[768,1536]{1,0:T(8,128)(2,1)} %param.8) | copy-start | bytes 7077892
  94.7 2.4 %collective-permute-start.25 = (bf16[256,1536]{1,0:T(8,128)(2,1)S(1)}, bf16[256,1536]{1,0:T(8,128)(2,1)S(1)}, u32[]{:S(2)}, u32[]{:S(2)}) collective-permute-start(bf16[256,1536]{1,0:T(8,128)(2,1)S(1)} %convolution_convert_fusion), channel_id=1, source_target_pairs={{0,8},{8,0},{16,24},{24,16},{32,40},{40,32},{48,56},{56,48},{64,72... | collective-permute-start | bytes 2359304 | tf_op jit(solution)/shard_map/ppermute | solution.py:63
  96.4 2.4 %collective-permute-start.24 = (bf16[256,1536]{1,0:T(8,128)(2,1)S(1)}, bf16[256,1536]{1,0:T(8,128)(2,1)S(1)}, u32[]{:S(2)}, u32[]{:S(2)}) collective-permute-start(bf16[256,1536]{1,0:T(8,128)(2,1)S(1)} %convolution_convert_fusion.1), channel_id=1, source_target_pairs={{0,8},{8,0},{16,24},{24,16},{32,40},{40,32},{48,56},{56,48},{64,72... | collective-permute-start | bytes 2359304 | tf_op jit(solution)/shard_map/ppermute | solution.py:63
  99.7 4.3 %copy-start.4 = (bf16[512,1536]{1,0:T(8,128)(2,1)S(1)}, bf16[512,1536]{1,0:T(8,128)(2,1)}, u32[]{:S(2)}) copy-start(bf16[512,1536]{1,0:T(8,128)(2,1)} %get-tuple-element.40) | copy-start | bytes 4718596
  99.7 13.3 %collective-permute-start.28 = (bf16[2,4,16,1536]{3,2,0,1:T(8,128)(2,1)S(1)}, bf16[2,4,16,1536]{3,2,0,1:T(8,128)(2,1)S(1)}, u32[]{:S(2)}, u32[]{:S(2)}) collective-permute-start(bf16[2,4,16,1536]{3,2,0,1:T(8,128)(2,1)S(1)} %pad_maximum_fusion.5), channel_id=1, source_target_pairs={{0,192},{8,56},{16,208},{24,40},{32,224},{40,24},{48,240},{56,8},{... | collective-permute-start | bytes 1179656 | tf_op jit(solution)/shard_map/ppermute | solution.py:59
  101.7 11.3 %collective-permute-start.27 = (bf16[2,4,16,1536]{3,2,0,1:T(8,128)(2,1)S(1)}, bf16[2,4,16,1536]{3,2,0,1:T(8,128)(2,1)S(1)}, u32[]{:S(2)}, u32[]{:S(2)}) collective-permute-start(bf16[2,4,16,1536]{3,2,0,1:T(8,128)(2,1)S(1)} %pad_maximum_fusion.4), channel_id=1, source_target_pairs={{0,128},{8,40},{16,144},{24,56},{32,160},{40,8},{48,176},{56,24},{... | collective-permute-start | bytes 1179656 | tf_op jit(solution)/shard_map/ppermute | solution.py:59
  103.2 10.7 %collective-permute-start.26 = (bf16[2,4,16,1536]{3,2,0,1:T(8,128)(2,1)S(1)}, bf16[2,4,16,1536]{3,2,0,1:T(8,128)(2,1)S(1)}, u32[]{:S(2)}, u32[]{:S(2)}) collective-permute-start(bf16[2,4,16,1536]{3,2,0,1:T(8,128)(2,1)S(1)} %pad_maximum_fusion.3), channel_id=1, source_target_pairs={{0,64},{8,24},{16,80},{24,8},{32,96},{40,56},{48,112},{56,40},{64,... | collective-permute-start | bytes 1179656 | tf_op jit(solution)/shard_map/ppermute | solution.py:59
  106.8 1.4 %copy-start.3 = (bf16[512,1536]{1,0:T(8,128)(2,1)S(1)}, bf16[512,1536]{1,0:T(8,128)(2,1)}, u32[]{:S(2)}) copy-start(bf16[512,1536]{1,0:T(8,128)(2,1)} %get-tuple-element.38) | copy-start | bytes 4718596
  114.1 4.8 %collective-permute-start.31 = (bf16[2,16,1536]{2,1,0:T(8,128)(2,1)S(1)}, bf16[2,16,1536]{2,1,0:T(8,128)(2,1)S(1)}, u32[]{:S(2)}, u32[]{:S(2)}) collective-permute-start(bf16[2,16,1536]{2,1,0:T(8,128)(2,1)S(1)} %get-tuple-element.86), channel_id=1, source_target_pairs={{0,48},{8,200},{16,32},{24,216},{32,16},{40,232},{48,0},{56,248},{... | collective-permute-start | bytes 294920 | tf_op jit(solution)/shard_map/ppermute | solution.py:59
  114.6 6.1 %collective-permute-start.30 = (bf16[2,16,1536]{2,1,0:T(8,128)(2,1)S(1)}, bf16[2,16,1536]{2,1,0:T(8,128)(2,1)S(1)}, u32[]{:S(2)}, u32[]{:S(2)}) collective-permute-start(bf16[2,16,1536]{2,1,0:T(8,128)(2,1)S(1)} %get-tuple-element.87), channel_id=1, source_target_pairs={{0,32},{8,136},{16,48},{24,152},{32,0},{40,168},{48,16},{56,184},{... | collective-permute-start | bytes 294920 | tf_op jit(solution)/shard_map/ppermute | solution.py:59
  117.3 4.6 %collective-permute-start.29 = (bf16[2,16,1536]{2,1,0:T(8,128)(2,1)S(1)}, bf16[2,16,1536]{2,1,0:T(8,128)(2,1)S(1)}, u32[]{:S(2)}, u32[]{:S(2)}) collective-permute-start(bf16[2,16,1536]{2,1,0:T(8,128)(2,1)S(1)} %get-tuple-element.85), channel_id=1, source_target_pairs={{0,16},{8,72},{16,0},{24,88},{32,48},{40,104},{48,32},{56,120},{64... | collective-permute-start | bytes 294920 | tf_op jit(solution)/shard_map/ppermute | solution.py:59

commit v6 on v3

--- a/solution.py
+++ b/solution.py
@@ -141,11 +141,11 @@
     ]
     sent = [x.astype(BF16) for x in kept[1:]]
     everything, all_inputs, all_grads, *sent = lax.optimization_barrier((everything, all_inputs, all_grads, *sent))
-    came = {k: plane_swap(sent[k - 1], k, False) for k in (2, 1, 3)}
+    came = {k: plane_swap(sent[k - 1], k, False) for k in (3, 1, 2)}
     plane_sum = kept[0]
     for k in (1, 2, 3):
         plane_sum = plane_sum + came[k].astype(F32)
-    came = {k: plane_swap(plane_sum[:, k].astype(BF16), k, True) for k in (2, 1, 3)}
+    came = {k: plane_swap(plane_sum[:, k].astype(BF16), k, True) for k in (3, 1, 2)}
     line_sum = plane_sum[:, 0]
     for k in (1, 2, 3):
         line_sum = line_sum + came[k].astype(F32)

time: 125 us -> 125 us (level)
  no operation moved by 1% of the time
where the time goes in v6:
time: 125 us
  waiting for transfers between devices  63.2 us (51%)
  starting transfers between devices  38.4 us (31%)
  matrix products  12 us (10%)
  other arithmetic  5.32 us (4%)
  local copies, waits for them, and re-layouts  5.1 us (4%)
    ppermute x16, waiting for transfers between devices, col_swap(): lax.ppermute(values, 'col', [(i, ring_partner(i, 8, odd_links)) for i in...  38.6 us
    ppermute x12, waiting for transfers between devices, plane_swap(): return lax.ppermute(values, 'row', pairs)  22.5 us
    ppermute x16, starting transfers between devices, col_swap(): lax.ppermute(values, 'col', [(i, ring_partner(i, 8, odd_links)) for i in...  20.6 us
    ppermute x12, starting transfers between devices, plane_swap(): return lax.ppermute(values, 'row', pairs)  17.5 us
    dot_general x2, matrix products, contract_rows(): lax.dot_general(left, right, (((0,), (0,)), ((), ())), preferred_element_...  5.66 us
    dot_general x4, matrix products, contract_cols(): lax.dot_general(left, right, (((1,), (1,)), ((), ())), preferred_element_...  3.23 us
    dot_general x4, matrix products, matmul(): return jnp.dot(left, right, preferred_element_type=F32)  3.09 us
    unnamed x12, local copies, waits for them, and re-layouts  2.83 us
  transfers between devices with their start and end apart: 31, of which 23 were waited for; matrix products, arithmetic and copies ran while one was open for 11% of the time, Pallas kernels for 0%

profile of v6, /device:TPU:4, one launch (start us, length us, event | category | flops | bytes accessed | tf_op | source)
XLA Modules:
  0.0 125.2 jit_solution(3627780014604495693)
XLA Ops:
  0.6 1.0 fusion.36
  1.6 2.3 %collective-permute-start.1 = (bf16[2,16,1536]{2,1,0:T(8,128)(2,1)S(1)}, bf16[2,16,1536]{2,1,0:T(8,128)(2,1)S(1)}, u32[]{:S(2)}, u32[]{:S(2)}) collective-permute-start(bf16[2,16,1536]{2,1,0:T(8,128)(2,1)S(1)} %get-tuple-element.97), channel_id=1, source_target_pairs={{0,32},{8,136},{16,48},{24,152},{32,0},{40,168},{48,16},{56,184},{... | collective-permute-start | bytes 294920 | tf_op jit(solution)/shard_map/ppermute | solution.py:59
  4.3 1.5 %collective-permute-start.2 = (bf16[2,16,1536]{2,1,0:T(8,128)(2,1)S(1)}, bf16[2,16,1536]{2,1,0:T(8,128)(2,1)S(1)}, u32[]{:S(2)}, u32[]{:S(2)}) collective-permute-start(bf16[2,16,1536]{2,1,0:T(8,128)(2,1)S(1)} %get-tuple-element.97), channel_id=1, source_target_pairs={{0,48},{8,200},{16,32},{24,216},{32,16},{40,232},{48,0},{56,248},{... | collective-permute-start | bytes 294920 | tf_op jit(solution)/shard_map/ppermute | solution.py:59
  5.8 2.0 %collective-permute-done.1 = bf16[2,16,1536]{2,1,0:T(8,128)(2,1)S(1)} collective-permute-done((bf16[2,16,1536]{2,1,0:T(8,128)(2,1)S(1)}, bf16[2,16,1536]{2,1,0:T(8,128)(2,1)S(1)}, u32[]{:S(2)}, u32[]{:S(2)}) %collective-permute-start.1) | collective-permute-done | bytes 98336 | tf_op jit(solution)/shard_map/ppermute | solution.py:59
  9.0 3.3 %collective-permute-start.3 = (bf16[2,4,16,1536]{3,2,1,0:T(8,128)(2,1)S(1)}, bf16[2,4,16,1536]{3,2,1,0:T(8,128)(2,1)S(1)}, u32[]{:S(2)}, u32[]{:S(2)}) collective-permute-start(bf16[2,4,16,1536]{3,2,1,0:T(8,128)(2,1)S(1)} %pad_maximum_fusion.2), channel_id=1, source_target_pairs={{0,128},{8,40},{16,144},{24,56},{32,160},{40,8},{48,176},{56,24},{... | collective-permute-start | bytes 1179656 | tf_op jit(solution)/shard_map/ppermute | solution.py:59
  12.3 1.1 collective-permute-start.5
  13.5 5.0 %collective-permute-done.3 = bf16[2,4,16,1536]{3,2,1,0:T(8,128)(2,1)S(1)} collective-permute-done((bf16[2,4,16,1536]{3,2,1,0:T(8,128)(2,1)S(1)}, bf16[2,4,16,1536]{3,2,1,0:T(8,128)(2,1)S(1)}, u32[]{:S(2)}, u32[]{:S(2)}) %collective-permute-start.3) | collective-permute-done | bytes 393248 | tf_op jit(solution)/shard_map/ppermute | solution.py:59
  18.5 4.5 %collective-permute-done.4 = bf16[2,4,16,1536]{3,2,1,0:T(8,128)(2,1)S(1)} collective-permute-done((bf16[2,4,16,1536]{3,2,1,0:T(8,128)(2,1)S(1)}, bf16[2,4,16,1536]{3,2,1,0:T(8,128)(2,1)S(1)}, u32[]{:S(2)}, u32[]{:S(2)}) %collective-permute-start.4) | collective-permute-done | bytes 393248 | tf_op jit(solution)/shard_map/ppermute | solution.py:59
  23.5 0.8 fusion.45
  24.2 0.9 copy-done.1
  25.1 0.8 fusion.46
  27.7 0.8 fusion.47
  28.6 2.0 %collective-permute-start.11 = (bf16[1,2,32,768]{3,2,1,0:T(8,128)(2,1)S(1)}, bf16[1,2,32,768]{3,2,1,0:T(8,128)(2,1)S(1)}, u32[]{:S(2)}, u32[]{:S(2)}) collective-permute-start(bf16[1,2,32,768]{3,2,1,0:T(8,128)(2,1)S(1)} %pad_maximum_fusion.10), channel_id=1, source_target_pairs={{0,1},{1,0},{2,3},{3,2},{4,5},{5,4},{6,7},{7,6},{8,9},{9,8},{10,11... | collective-permute-start | bytes 294920 | tf_op jit(solution)/shard_map/ppermute | solution.py:67
  30.7 5.0 %collective-permute-start.7 = (bf16[1,2,32,768]{3,2,1,0:T(8,128)(2,1)S(1)}, bf16[1,2,32,768]{3,2,1,0:T(8,128)(2,1)S(1)}, u32[]{:S(2)}, u32[]{:S(2)}) collective-permute-start(bf16[1,2,32,768]{3,2,1,0:T(8,128)(2,1)S(1)} %pad_maximum_fusion.11), channel_id=1, source_target_pairs={{0,7},{1,2},{2,1},{3,4},{4,3},{5,6},{6,5},{7,0},{8,15},{9,10},{10,... | collective-permute-start | bytes 294920 | tf_op jit(solution)/shard_map/ppermute | solution.py:67
  35.8 2.7 %collective-permute-done.7 = bf16[1,2,32,768]{3,2,1,0:T(8,128)(2,1)S(1)} collective-permute-done((bf16[1,2,32,768]{3,2,1,0:T(8,128)(2,1)S(1)}, bf16[1,2,32,768]{3,2,1,0:T(8,128)(2,1)S(1)}, u32[]{:S(2)}, u32[]{:S(2)}) %collective-permute-start.7) | collective-permute-done | bytes 98336 | tf_op jit(solution)/shard_map/ppermute | solution.py:67
  38.7 3.1 %collective-permute-start.12 = (bf16[2,2,32,768]{3,2,1,0:T(8,128)(2,1)S(1)}, bf16[2,2,32,768]{3,2,1,0:T(8,128)(2,1)S(1)}, u32[]{:S(2)}, u32[]{:S(2)}) collective-permute-start(bf16[2,2,32,768]{3,2,1,0:T(8,128)(2,1)S(1)} %pad_maximum_fusion.7), channel_id=1, source_target_pairs={{0,7},{1,2},{2,1},{3,4},{4,3},{5,6},{6,5},{7,0},{8,15},{9,10},{10,... | collective-permute-start | bytes 589832 | tf_op jit(solution)/shard_map/ppermute | solution.py:67
  42.0 1.2 pad_maximum_fusion.1
  43.3 1.5 %collective-permute-done.8 = bf16[2,2,32,768]{3,2,1,0:T(8,128)(2,1)S(1)} collective-permute-done((bf16[2,2,32,768]{3,2,1,0:T(8,128)(2,1)S(1)}, bf16[2,2,32,768]{3,2,1,0:T(8,128)(2,1)S(1)}, u32[]{:S(2)}, u32[]{:S(2)}) %collective-permute-start.8) | collective-permute-done | bytes 196640 | tf_op jit(solution)/shard_map/ppermute | solution.py:67
  44.8 2.7 %collective-permute-start.9 = (bf16[2,2,32,768]{3,2,1,0:T(8,128)(2,1)S(1)}, bf16[2,2,32,768]{3,2,1,0:T(8,128)(2,1)S(1)}, u32[]{:S(2)}, u32[]{:S(2)}) collective-permute-start(bf16[2,2,32,768]{3,2,1,0:T(8,128)(2,1)S(1)} %fusion.9), channel_id=1, source_target_pairs={{0,7},{1,2},{2,1},{3,4},{4,3},{5,6},{6,5},{7,0},{8,15},{9,10},{10,... | collective-permute-start | bytes 589832 | tf_op jit(solution)/shard_map/ppermute | solution.py:67
  47.6 4.2 %collective-permute-done.9 = bf16[2,2,32,768]{3,2,1,0:T(8,128)(2,1)S(1)} collective-permute-done((bf16[2,2,32,768]{3,2,1,0:T(8,128)(2,1)S(1)}, bf16[2,2,32,768]{3,2,1,0:T(8,128)(2,1)S(1)}, u32[]{:S(2)}, u32[]{:S(2)}) %collective-permute-start.9) | collective-permute-done | bytes 196640 | tf_op jit(solution)/shard_map/ppermute | solution.py:67
  51.9 3.0 %collective-permute-done.13 = bf16[2,2,32,768]{3,2,1,0:T(8,128)(2,1)S(1)} collective-permute-done((bf16[2,2,32,768]{3,2,1,0:T(8,128)(2,1)S(1)}, bf16[2,2,32,768]{3,2,1,0:T(8,128)(2,1)S(1)}, u32[]{:S(2)}, u32[]{:S(2)}) %collective-permute-start.13) | collective-permute-done | bytes 196640 | tf_op jit(solution)/shard_map/ppermute | solution.py:67
  54.9 1.3 %collective-permute-start.14 = (bf16[2,2,32,768]{3,2,1,0:T(8,128)(2,1)S(1)}, bf16[2,2,32,768]{3,2,1,0:T(8,128)(2,1)S(1)}, u32[]{:S(2)}, u32[]{:S(2)}) collective-permute-start(bf16[2,2,32,768]{3,2,1,0:T(8,128)(2,1)S(1)} %fusion.10), channel_id=1, source_target_pairs={{0,7},{1,2},{2,1},{3,4},{4,3},{5,6},{6,5},{7,0},{8,15},{9,10},{10,... | collective-permute-start | bytes 589832 | tf_op jit(solution)/shard_map/ppermute | solution.py:67
  56.2 1.2 pad_maximum_fusion
  57.6 6.6 %collective-permute-done.14 = bf16[2,2,32,768]{3,2,1,0:T(8,128)(2,1)S(1)} collective-permute-done((bf16[2,2,32,768]{3,2,1,0:T(8,128)(2,1)S(1)}, bf16[2,2,32,768]{3,2,1,0:T(8,128)(2,1)S(1)}, u32[]{:S(2)}, u32[]{:S(2)}) %collective-permute-start.14) | collective-permute-done | bytes 196640 | tf_op jit(solution)/shard_map/ppermute | solution.py:67
  64.5 2.1 %collective-permute-start.16 = (bf16[2,2,32,768]{3,2,1,0:T(8,128)(2,1)S(1)}, bf16[2,2,32,768]{3,2,1,0:T(8,128)(2,1)S(1)}, u32[]{:S(2)}, u32[]{:S(2)}) collective-permute-start(bf16[2,2,32,768]{3,2,1,0:T(8,128)(2,1)S(1)} %pad_maximum_fusion.8), channel_id=1, source_target_pairs={{0,7},{1,2},{2,1},{3,4},{4,3},{5,6},{6,5},{7,0},{8,15},{9,10},{10,... | collective-permute-start | bytes 589832 | tf_op jit(solution)/shard_map/ppermute | solution.py:67
  66.7 5.5 %collective-permute-done.15 = bf16[2,2,32,768]{3,2,1,0:T(8,128)(2,1)S(1)} collective-permute-done((bf16[2,2,32,768]{3,2,1,0:T(8,128)(2,1)S(1)}, bf16[2,2,32,768]{3,2,1,0:T(8,128)(2,1)S(1)}, u32[]{:S(2)}, u32[]{:S(2)}) %collective-permute-start.15) | collective-permute-done | bytes 196640 | tf_op jit(solution)/shard_map/ppermute | solution.py:67
  72.3 0.9 collective-permute-start.17
  73.2 6.8 %collective-permute-done.18 = bf16[2,2,32,768]{3,2,1,0:T(8,128)(2,1)S(1)} collective-permute-done((bf16[2,2,32,768]{3,2,1,0:T(8,128)(2,1)S(1)}, bf16[2,2,32,768]{3,2,1,0:T(8,128)(2,1)S(1)}, u32[]{:S(2)}, u32[]{:S(2)}) %collective-permute-start.18) | collective-permute-done | bytes 196640 | tf_op jit(solution)/shard_map/ppermute | solution.py:67
  80.0 1.5 %collective-permute-start.20 = (bf16[2,2,32,768]{3,2,1,0:T(8,128)(2,1)S(1)}, bf16[2,2,32,768]{3,2,1,0:T(8,128)(2,1)S(1)}, u32[]{:S(2)}, u32[]{:S(2)}) collective-permute-start(bf16[2,2,32,768]{3,2,1,0:T(8,128)(2,1)S(1)} %collective-permute-done.17), channel_id=1, source_target_pairs={{0,7},{1,2},{2,1},{3,4},{4,3},{5,6},{6,5},{7,0},{8,15},{9,10},{10,... | collective-permute-start | bytes 589832 | tf_op jit(solution)/shard_map/ppermute | solution.py:67
  81.5 4.2 %collective-permute-done.19 = bf16[2,2,32,768]{3,2,1,0:T(8,128)(2,1)S(1)} collective-permute-done((bf16[2,2,32,768]{3,2,1,0:T(8,128)(2,1)S(1)}, bf16[2,2,32,768]{3,2,1,0:T(8,128)(2,1)S(1)}, u32[]{:S(2)}, u32[]{:S(2)}) %collective-permute-start.19) | collective-permute-done | bytes 196640 | tf_op jit(solution)/shard_map/ppermute | solution.py:67
  86.9 0.9 collective-permute-start.21
  87.8 3.8 %collective-permute-done.22 = bf16[1,2,32,768]{3,2,1,0:T(8,128)(2,1)S(1)} collective-permute-done((bf16[1,2,32,768]{3,2,1,0:T(8,128)(2,1)S(1)}, bf16[1,2,32,768]{3,2,1,0:T(8,128)(2,1)S(1)}, u32[]{:S(2)}, u32[]{:S(2)}) %collective-permute-start.22) | collective-permute-done | bytes 98336 | tf_op jit(solution)/shard_map/ppermute | solution.py:67
  91.8 0.8 convolution_convert_fusion
  94.9 0.8 fusion.43
  96.6 0.8 fusion.44
  97.7 1.4 %collective-permute-start.25 = (bf16[2,4,16,1536]{3,2,0,1:T(8,128)(2,1)S(1)}, bf16[2,4,16,1536]{3,2,0,1:T(8,128)(2,1)S(1)}, u32[]{:S(2)}, u32[]{:S(2)}) collective-permute-start(bf16[2,4,16,1536]{3,2,0,1:T(8,128)(2,1)S(1)} %pad_maximum_fusion.3), channel_id=1, source_target_pairs={{0,64},{8,24},{16,80},{24,8},{32,96},{40,56},{48,112},{56,40},{64,... | collective-permute-start | bytes 1179656 | tf_op jit(solution)/shard_map/ppermute | solution.py:59
  99.1 2.5 %collective-permute-start.26 = (bf16[2,4,16,1536]{3,2,0,1:T(8,128)(2,1)S(1)}, bf16[2,4,16,1536]{3,2,0,1:T(8,128)(2,1)S(1)}, u32[]{:S(2)}, u32[]{:S(2)}) collective-permute-start(bf16[2,4,16,1536]{3,2,0,1:T(8,128)(2,1)S(1)} %pad_maximum_fusion.4), channel_id=1, source_target_pairs={{0,128},{8,40},{16,144},{24,56},{32,160},{40,8},{48,176},{56,24},{... | collective-permute-start | bytes 1179656 | tf_op jit(solution)/shard_map/ppermute | solution.py:59
  101.6 0.9 collective-permute-start.27
  102.4 2.8 %multiply_convert_fusion = bf16[768,1536]{1,0:T(8,128)(2,1)} fusion(bf16[512,768]{1,0:T(8,128)(2,1)S(1)} %bitcast.270, bf16[512,1536]{1,0:T(8,128)(2,1)S(1)} %copy-done.3), kind=kOutput, calls=%fused_computation | convolution fusion | flops 1210318848 | bytes 4718592 | tf_op jit(solution)/shard_map/dot_general | solution.py:31
  105.5 1.2 copy-done.4
  106.7 2.8 %multiply_convert_fusion.1 = bf16[1536,768]{1,0:T(8,128)(2,1)} fusion(bf16[512,1536]{1,0:T(8,128)(2,1)S(1)} %copy-done.4, bf16[512,768]{1,0:T(8,128)(2,1)S(1)} %bitcast.269), kind=kOutput, calls=%fused_computation.1 | convolution fusion | flops 1210318848 | bytes 4718592 | tf_op jit(solution)/shard_map/dot_general | solution.py:31
  109.5 2.1 %collective-permute-done.26 = bf16[2,4,16,1536]{3,2,0,1:T(8,128)(2,1)S(1)} collective-permute-done((bf16[2,4,16,1536]{3,2,0,1:T(8,128)(2,1)S(1)}, bf16[2,4,16,1536]{3,2,0,1:T(8,128)(2,1)S(1)}, u32[]{:S(2)}, u32[]{:S(2)}) %collective-permute-start.26) | collective-permute-done | bytes 393248 | tf_op jit(solution)/shard_map/ppermute | solution.py:59
  111.6 3.1 %collective-permute-done.27 = bf16[2,4,16,1536]{3,2,0,1:T(8,128)(2,1)S(1)} collective-permute-done((bf16[2,4,16,1536]{3,2,0,1:T(8,128)(2,1)S(1)}, bf16[2,4,16,1536]{3,2,0,1:T(8,128)(2,1)S(1)}, u32[]{:S(2)}, u32[]{:S(2)}) %collective-permute-start.27) | collective-permute-done | bytes 393248 | tf_op jit(solution)/shard_map/ppermute | solution.py:59
  115.0 1.4 %collective-permute-start.28 = (bf16[2,16,1536]{2,1,0:T(8,128)(2,1)S(1)}, bf16[2,16,1536]{2,1,0:T(8,128)(2,1)S(1)}, u32[]{:S(2)}, u32[]{:S(2)}) collective-permute-start(bf16[2,16,1536]{2,1,0:T(8,128)(2,1)S(1)} %get-tuple-element.91), channel_id=1, source_target_pairs={{0,16},{8,72},{16,0},{24,88},{32,48},{40,104},{48,32},{56,120},{64... | collective-permute-start | bytes 294920 | tf_op jit(solution)/shard_map/ppermute | solution.py:59
  116.4 2.0 %collective-permute-start.30 = (bf16[2,16,1536]{2,1,0:T(8,128)(2,1)S(1)}, bf16[2,16,1536]{2,1,0:T(8,128)(2,1)S(1)}, u32[]{:S(2)}, u32[]{:S(2)}) collective-permute-start(bf16[2,16,1536]{2,1,0:T(8,128)(2,1)S(1)} %get-tuple-element.92), channel_id=1, source_target_pairs={{0,48},{8,200},{16,32},{24,216},{32,16},{40,232},{48,0},{56,248},{... | collective-permute-start | bytes 294920 | tf_op jit(solution)/shard_map/ppermute | solution.py:59
  118.4 0.8 collective-permute-start.29
  119.8 1.2 collective-permute-done.30
  121.0 3.5 %collective-permute-done.29 = bf16[2,16,1536]{2,1,0:T(8,128)(2,1)S(1)} collective-permute-done((bf16[2,16,1536]{2,1,0:T(8,128)(2,1)S(1)}, bf16[2,16,1536]{2,1,0:T(8,128)(2,1)S(1)}, u32[]{:S(2)}, u32[]{:S(2)}) %collective-permute-start.29) | collective-permute-done | bytes 98336 | tf_op jit(solution)/shard_map/ppermute | solution.py:59
  (103 shorter events, 11.8 us)
Async XLA Ops:
  0.6 22.8 %copy-start = (bf16[1536,768]{1,0:T(8,128)(2,1)S(1)}, bf16[1536,768]{1,0:T(8,128)(2,1)}, u32[]{:S(2)}) copy-start(bf16[1536,768]{1,0:T(8,128)(2,1)} %param.6) | copy-start | bytes 7077892
  1.6 6.2 %collective-permute-start.1 = (bf16[2,16,1536]{2,1,0:T(8,128)(2,1)S(1)}, bf16[2,16,1536]{2,1,0:T(8,128)(2,1)S(1)}, u32[]{:S(2)}, u32[]{:S(2)}) collective-permute-start(bf16[2,16,1536]{2,1,0:T(8,128)(2,1)S(1)} %get-tuple-element.97), channel_id=1, source_target_pairs={{0,32},{8,136},{16,48},{24,152},{32,0},{40,168},{48,16},{56,184},{... | collective-permute-start | bytes 294920 | tf_op jit(solution)/shard_map/ppermute | solution.py:59
  4.0 4.6 %collective-permute-start = (bf16[2,16,1536]{2,1,0:T(8,128)(2,1)S(1)}, bf16[2,16,1536]{2,1,0:T(8,128)(2,1)S(1)}, u32[]{:S(2)}, u32[]{:S(2)}) collective-permute-start(bf16[2,16,1536]{2,1,0:T(8,128)(2,1)S(1)} %get-tuple-element.97), channel_id=1, source_target_pairs={{0,16},{8,72},{16,0},{24,88},{32,48},{40,104},{48,32},{56,120},{64... | collective-permute-start | bytes 294920 | tf_op jit(solution)/shard_map/ppermute | solution.py:59
  4.3 4.6 %collective-permute-start.2 = (bf16[2,16,1536]{2,1,0:T(8,128)(2,1)S(1)}, bf16[2,16,1536]{2,1,0:T(8,128)(2,1)S(1)}, u32[]{:S(2)}, u32[]{:S(2)}) collective-permute-start(bf16[2,16,1536]{2,1,0:T(8,128)(2,1)S(1)} %get-tuple-element.97), channel_id=1, source_target_pairs={{0,48},{8,200},{16,32},{24,216},{32,16},{40,232},{48,0},{56,248},{... | collective-permute-start | bytes 294920 | tf_op jit(solution)/shard_map/ppermute | solution.py:59
  9.0 9.5 %collective-permute-start.3 = (bf16[2,4,16,1536]{3,2,1,0:T(8,128)(2,1)S(1)}, bf16[2,4,16,1536]{3,2,1,0:T(8,128)(2,1)S(1)}, u32[]{:S(2)}, u32[]{:S(2)}) collective-permute-start(bf16[2,4,16,1536]{3,2,1,0:T(8,128)(2,1)S(1)} %pad_maximum_fusion.2), channel_id=1, source_target_pairs={{0,128},{8,40},{16,144},{24,56},{32,160},{40,8},{48,176},{56,24},{... | collective-permute-start | bytes 1179656 | tf_op jit(solution)/shard_map/ppermute | solution.py:59
  12.3 10.9 %collective-permute-start.5 = (bf16[2,4,16,1536]{3,2,1,0:T(8,128)(2,1)S(1)}, bf16[2,4,16,1536]{3,2,1,0:T(8,128)(2,1)S(1)}, u32[]{:S(2)}, u32[]{:S(2)}) collective-permute-start(bf16[2,4,16,1536]{3,2,1,0:T(8,128)(2,1)S(1)} %pad_maximum_fusion.2), channel_id=1, source_target_pairs={{0,192},{8,56},{16,208},{24,40},{32,224},{40,24},{48,240},{56,8},{... | collective-permute-start | bytes 1179656 | tf_op jit(solution)/shard_map/ppermute | solution.py:59
  13.3 9.6 %collective-permute-start.4 = (bf16[2,4,16,1536]{3,2,1,0:T(8,128)(2,1)S(1)}, bf16[2,4,16,1536]{3,2,1,0:T(8,128)(2,1)S(1)}, u32[]{:S(2)}, u32[]{:S(2)}) collective-permute-start(bf16[2,4,16,1536]{3,2,1,0:T(8,128)(2,1)S(1)} %pad_maximum_fusion.2), channel_id=1, source_target_pairs={{0,64},{8,24},{16,80},{24,8},{32,96},{40,56},{48,112},{56,40},{64,... | collective-permute-start | bytes 1179656 | tf_op jit(solution)/shard_map/ppermute | solution.py:59
  23.3 3.5 %collective-permute-start.6 = (bf16[2,256,1536]{2,1,0:T(8,128)(2,1)S(1)}, bf16[2,256,1536]{2,1,0:T(8,128)(2,1)S(1)}, u32[]{:S(2)}, u32[]{:S(2)}) collective-permute-start(bf16[2,256,1536]{2,1,0:T(8,128)(2,1)S(1)} %bitcast.258), channel_id=1, source_target_pairs={{0,8},{8,0},{16,24},{24,16},{32,40},{40,32},{48,56},{56,48},{64,72... | collective-permute-start | bytes 4718600 | tf_op jit(solution)/shard_map/ppermute | solution.py:63
  23.5 1.7 %copy-start.1 = (bf16[768,1536]{1,0:T(8,128)(2,1)S(1)}, bf16[768,1536]{1,0:T(8,128)(2,1)}, u32[]{:S(2)}) copy-start(bf16[768,1536]{1,0:T(8,128)(2,1)} %param.8) | copy-start | bytes 7077892
  28.6 7.2 %collective-permute-start.11 = (bf16[1,2,32,768]{3,2,1,0:T(8,128)(2,1)S(1)}, bf16[1,2,32,768]{3,2,1,0:T(8,128)(2,1)S(1)}, u32[]{:S(2)}, u32[]{:S(2)}) collective-permute-start(bf16[1,2,32,768]{3,2,1,0:T(8,128)(2,1)S(1)} %pad_maximum_fusion.10), channel_id=1, source_target_pairs={{0,1},{1,0},{2,3},{3,2},{4,5},{5,4},{6,7},{7,6},{8,9},{9,8},{10,11... | collective-permute-start | bytes 294920 | tf_op jit(solution)/shard_map/ppermute | solution.py:67
  30.7 7.9 %collective-permute-start.7 = (bf16[1,2,32,768]{3,2,1,0:T(8,128)(2,1)S(1)}, bf16[1,2,32,768]{3,2,1,0:T(8,128)(2,1)S(1)}, u32[]{:S(2)}, u32[]{:S(2)}) collective-permute-start(bf16[1,2,32,768]{3,2,1,0:T(8,128)(2,1)S(1)} %pad_maximum_fusion.11), channel_id=1, source_target_pairs={{0,7},{1,2},{2,1},{3,4},{4,3},{5,6},{6,5},{7,0},{8,15},{9,10},{10,... | collective-permute-start | bytes 294920 | tf_op jit(solution)/shard_map/ppermute | solution.py:67
  38.6 6.2 %collective-permute-start.8 = (bf16[2,2,32,768]{3,2,1,0:T(8,128)(2,1)S(1)}, bf16[2,2,32,768]{3,2,1,0:T(8,128)(2,1)S(1)}, u32[]{:S(2)}, u32[]{:S(2)}) collective-permute-start(bf16[2,2,32,768]{3,2,1,0:T(8,128)(2,1)S(1)} %pad_maximum_fusion.6), channel_id=1, source_target_pairs={{0,1},{1,0},{2,3},{3,2},{4,5},{5,4},{6,7},{7,6},{8,9},{9,8},{10,11... | collective-permute-start | bytes 589832 | tf_op jit(solution)/shard_map/ppermute | solution.py:67
  38.7 8.7 %collective-permute-start.12 = (bf16[2,2,32,768]{3,2,1,0:T(8,128)(2,1)S(1)}, bf16[2,2,32,768]{3,2,1,0:T(8,128)(2,1)S(1)}, u32[]{:S(2)}, u32[]{:S(2)}) collective-permute-start(bf16[2,2,32,768]{3,2,1,0:T(8,128)(2,1)S(1)} %pad_maximum_fusion.7), channel_id=1, source_target_pairs={{0,7},{1,2},{2,1},{3,4},{4,3},{5,6},{6,5},{7,0},{8,15},{9,10},{10,... | collective-permute-start | bytes 589832 | tf_op jit(solution)/shard_map/ppermute | solution.py:67
  44.8 7.0 %collective-permute-start.9 = (bf16[2,2,32,768]{3,2,1,0:T(8,128)(2,1)S(1)}, bf16[2,2,32,768]{3,2,1,0:T(8,128)(2,1)S(1)}, u32[]{:S(2)}, u32[]{:S(2)}) collective-permute-start(bf16[2,2,32,768]{3,2,1,0:T(8,128)(2,1)S(1)} %fusion.9), channel_id=1, source_target_pairs={{0,7},{1,2},{2,1},{3,4},{4,3},{5,6},{6,5},{7,0},{8,15},{9,10},{10,... | collective-permute-start | bytes 589832 | tf_op jit(solution)/shard_map/ppermute | solution.py:67
  47.5 7.4 %collective-permute-start.13 = (bf16[2,2,32,768]{3,2,1,0:T(8,128)(2,1)S(1)}, bf16[2,2,32,768]{3,2,1,0:T(8,128)(2,1)S(1)}, u32[]{:S(2)}, u32[]{:S(2)}) collective-permute-start(bf16[2,2,32,768]{3,2,1,0:T(8,128)(2,1)S(1)} %fusion.11), channel_id=1, source_target_pairs={{0,1},{1,0},{2,3},{3,2},{4,5},{5,4},{6,7},{7,6},{8,9},{9,8},{10,11... | collective-permute-start | bytes 589832 | tf_op jit(solution)/shard_map/ppermute | solution.py:67
  51.8 5.8 %collective-permute-start.10 = (bf16[2,2,32,768]{3,2,1,0:T(8,128)(2,1)S(1)}, bf16[2,2,32,768]{3,2,1,0:T(8,128)(2,1)S(1)}, u32[]{:S(2)}, u32[]{:S(2)}) collective-permute-start(bf16[2,2,32,768]{3,2,1,0:T(8,128)(2,1)S(1)} %fusion.8), channel_id=1, source_target_pairs={{0,1},{1,0},{2,3},{3,2},{4,5},{5,4},{6,7},{7,6},{8,9},{9,8},{10,11... | collective-permute-start | bytes 589832 | tf_op jit(solution)/shard_map/ppermute | solution.py:67
  54.9 9.2 %collective-permute-start.14 = (bf16[2,2,32,768]{3,2,1,0:T(8,128)(2,1)S(1)}, bf16[2,2,32,768]{3,2,1,0:T(8,128)(2,1)S(1)}, u32[]{:S(2)}, u32[]{:S(2)}) collective-permute-start(bf16[2,2,32,768]{3,2,1,0:T(8,128)(2,1)S(1)} %fusion.10), channel_id=1, source_target_pairs={{0,7},{1,2},{2,1},{3,4},{4,3},{5,6},{6,5},{7,0},{8,15},{9,10},{10,... | collective-permute-start | bytes 589832 | tf_op jit(solution)/shard_map/ppermute | solution.py:67
  56.2 7.9 %copy-start.5 = (f32[768]{0:T(1024)S(1)}, f32[768]{0:T(1024)}, u32[]{:S(2)}) copy-start(f32[768]{0:T(1024)} %param.7) | copy-start | bytes 9220
  64.4 7.9 %collective-permute-start.15 = (bf16[2,2,32,768]{3,2,1,0:T(8,128)(2,1)S(1)}, bf16[2,2,32,768]{3,2,1,0:T(8,128)(2,1)S(1)}, u32[]{:S(2)}, u32[]{:S(2)}) collective-permute-start(bf16[2,2,32,768]{3,2,1,0:T(8,128)(2,1)S(1)} %pad_maximum_fusion.8), channel_id=1, source_target_pairs={{0,1},{1,0},{2,3},{3,2},{4,5},{5,4},{6,7},{7,6},{8,9},{9,8},{10,11... | collective-permute-start | bytes 589832 | tf_op jit(solution)/shard_map/ppermute | solution.py:67
  64.5 7.8 %collective-permute-start.16 = (bf16[2,2,32,768]{3,2,1,0:T(8,128)(2,1)S(1)}, bf16[2,2,32,768]{3,2,1,0:T(8,128)(2,1)S(1)}, u32[]{:S(2)}, u32[]{:S(2)}) collective-permute-start(bf16[2,2,32,768]{3,2,1,0:T(8,128)(2,1)S(1)} %pad_maximum_fusion.8), channel_id=1, source_target_pairs={{0,7},{1,2},{2,1},{3,4},{4,3},{5,6},{6,5},{7,0},{8,15},{9,10},{10,... | collective-permute-start | bytes 589832 | tf_op jit(solution)/shard_map/ppermute | solution.py:67
  72.3 7.8 %collective-permute-start.18 = (bf16[2,2,32,768]{3,2,1,0:T(8,128)(2,1)S(1)}, bf16[2,2,32,768]{3,2,1,0:T(8,128)(2,1)S(1)}, u32[]{:S(2)}, u32[]{:S(2)}) collective-permute-start(bf16[2,2,32,768]{3,2,1,0:T(8,128)(2,1)S(1)} %collective-permute-done.15), channel_id=1, source_target_pairs={{0,7},{1,2},{2,1},{3,4},{4,3},{5,6},{6,5},{7,0},{8,15},{9,10},{10,... | collective-permute-start | bytes 589832 | tf_op jit(solution)/shard_map/ppermute | solution.py:67
  72.3 7.8 %collective-permute-start.17 = (bf16[2,2,32,768]{3,2,1,0:T(8,128)(2,1)S(1)}, bf16[2,2,32,768]{3,2,1,0:T(8,128)(2,1)S(1)}, u32[]{:S(2)}, u32[]{:S(2)}) collective-permute-start(bf16[2,2,32,768]{3,2,1,0:T(8,128)(2,1)S(1)} %collective-permute-done.16), channel_id=1, source_target_pairs={{0,1},{1,0},{2,3},{3,2},{4,5},{5,4},{6,7},{7,6},{8,9},{9,8},{10,11... | collective-permute-start | bytes 589832 | tf_op jit(solution)/shard_map/ppermute | solution.py:67
  80.0 5.7 %collective-permute-start.19 = (bf16[2,2,32,768]{3,2,1,0:T(8,128)(2,1)S(1)}, bf16[2,2,32,768]{3,2,1,0:T(8,128)(2,1)S(1)}, u32[]{:S(2)}, u32[]{:S(2)}) collective-permute-start(bf16[2,2,32,768]{3,2,1,0:T(8,128)(2,1)S(1)} %collective-permute-done.18), channel_id=1, source_target_pairs={{0,1},{1,0},{2,3},{3,2},{4,5},{5,4},{6,7},{7,6},{8,9},{9,8},{10,11... | collective-permute-start | bytes 589832 | tf_op jit(solution)/shard_map/ppermute | solution.py:67
  80.0 6.9 %collective-permute-start.20 = (bf16[2,2,32,768]{3,2,1,0:T(8,128)(2,1)S(1)}, bf16[2,2,32,768]{3,2,1,0:T(8,128)(2,1)S(1)}, u32[]{:S(2)}, u32[]{:S(2)}) collective-permute-start(bf16[2,2,32,768]{3,2,1,0:T(8,128)(2,1)S(1)} %collective-permute-done.17), channel_id=1, source_target_pairs={{0,7},{1,2},{2,1},{3,4},{4,3},{5,6},{6,5},{7,0},{8,15},{9,10},{10,... | collective-permute-start | bytes 589832 | tf_op jit(solution)/shard_map/ppermute | solution.py:67
  85.7 5.9 %collective-permute-start.22 = (bf16[1,2,32,768]{3,2,1,0:T(8,128)(2,1)S(1)}, bf16[1,2,32,768]{3,2,1,0:T(8,128)(2,1)S(1)}, u32[]{:S(2)}, u32[]{:S(2)}) collective-permute-start(bf16[1,2,32,768]{3,2,1,0:T(8,128)(2,1)S(1)} %slice.174), channel_id=1, source_target_pairs={{0,7},{1,2},{2,1},{3,4},{4,3},{5,6},{6,5},{7,0},{8,15},{9,10},{10,... | collective-permute-start | bytes 294920 | tf_op jit(solution)/shard_map/ppermute | solution.py:67
  86.9 4.7 %collective-permute-start.21 = (bf16[1,2,32,768]{3,2,1,0:T(8,128)(2,1)S(1)}, bf16[1,2,32,768]{3,2,1,0:T(8,128)(2,1)S(1)}, u32[]{:S(2)}, u32[]{:S(2)}) collective-permute-start(bf16[1,2,32,768]{3,2,1,0:T(8,128)(2,1)S(1)} %slice.173), channel_id=1, source_target_pairs={{0,1},{1,0},{2,3},{3,2},{4,5},{5,4},{6,7},{7,6},{8,9},{9,8},{10,11... | collective-permute-start | bytes 294920 | tf_op jit(solution)/shard_map/ppermute | solution.py:67
  91.7 1.7 %copy-start.2 = (bf16[768,1536]{1,0:T(8,128)(2,1)S(1)}, bf16[768,1536]{1,0:T(8,128)(2,1)}, u32[]{:S(2)}) copy-start(bf16[768,1536]{1,0:T(8,128)(2,1)} %param.8) | copy-start | bytes 7077892
  92.6 2.4 %collective-permute-start.24 = (bf16[256,1536]{1,0:T(8,128)(2,1)S(1)}, bf16[256,1536]{1,0:T(8,128)(2,1)S(1)}, u32[]{:S(2)}, u32[]{:S(2)}) collective-permute-start(bf16[256,1536]{1,0:T(8,128)(2,1)S(1)} %convolution_convert_fusion), channel_id=1, source_target_pairs={{0,8},{8,0},{16,24},{24,16},{32,40},{40,32},{48,56},{56,48},{64,72... | collective-permute-start | bytes 2359304 | tf_op jit(solution)/shard_map/ppermute | solution.py:63
  94.2 2.4 %collective-permute-start.23 = (bf16[256,1536]{1,0:T(8,128)(2,1)S(1)}, bf16[256,1536]{1,0:T(8,128)(2,1)S(1)}, u32[]{:S(2)}, u32[]{:S(2)}) collective-permute-start(bf16[256,1536]{1,0:T(8,128)(2,1)S(1)} %convolution_convert_fusion.1), channel_id=1, source_target_pairs={{0,8},{8,0},{16,24},{24,16},{32,40},{40,32},{48,56},{56,48},{64,72... | collective-permute-start | bytes 2359304 | tf_op jit(solution)/shard_map/ppermute | solution.py:63
  97.5 4.9 %copy-start.3 = (bf16[512,1536]{1,0:T(8,128)(2,1)S(1)}, bf16[512,1536]{1,0:T(8,128)(2,1)}, u32[]{:S(2)}) copy-start(bf16[512,1536]{1,0:T(8,128)(2,1)} %pad_maximum_fusion.1) | copy-start | bytes 4718596
  97.7 11.9 %collective-permute-start.25 = (bf16[2,4,16,1536]{3,2,0,1:T(8,128)(2,1)S(1)}, bf16[2,4,16,1536]{3,2,0,1:T(8,128)(2,1)S(1)}, u32[]{:S(2)}, u32[]{:S(2)}) collective-permute-start(bf16[2,4,16,1536]{3,2,0,1:T(8,128)(2,1)S(1)} %pad_maximum_fusion.3), channel_id=1, source_target_pairs={{0,64},{8,24},{16,80},{24,8},{32,96},{40,56},{48,112},{56,40},{64,... | collective-permute-start | bytes 1179656 | tf_op jit(solution)/shard_map/ppermute | solution.py:59
  99.1 12.6 %collective-permute-start.26 = (bf16[2,4,16,1536]{3,2,0,1:T(8,128)(2,1)S(1)}, bf16[2,4,16,1536]{3,2,0,1:T(8,128)(2,1)S(1)}, u32[]{:S(2)}, u32[]{:S(2)}) collective-permute-start(bf16[2,4,16,1536]{3,2,0,1:T(8,128)(2,1)S(1)} %pad_maximum_fusion.4), channel_id=1, source_target_pairs={{0,128},{8,40},{16,144},{24,56},{32,160},{40,8},{48,176},{56,24},{... | collective-permute-start | bytes 1179656 | tf_op jit(solution)/shard_map/ppermute | solution.py:59
  101.6 13.2 %collective-permute-start.27 = (bf16[2,4,16,1536]{3,2,0,1:T(8,128)(2,1)S(1)}, bf16[2,4,16,1536]{3,2,0,1:T(8,128)(2,1)S(1)}, u32[]{:S(2)}, u32[]{:S(2)}) collective-permute-start(bf16[2,4,16,1536]{3,2,0,1:T(8,128)(2,1)S(1)} %pad_maximum_fusion.5), channel_id=1, source_target_pairs={{0,192},{8,56},{16,208},{24,40},{32,224},{40,24},{48,240},{56,8},{... | collective-permute-start | bytes 1179656 | tf_op jit(solution)/shard_map/ppermute | solution.py:59
  105.3 1.4 %copy-start.4 = (bf16[512,1536]{1,0:T(8,128)(2,1)S(1)}, bf16[512,1536]{1,0:T(8,128)(2,1)}, u32[]{:S(2)}) copy-start(bf16[512,1536]{1,0:T(8,128)(2,1)} %pad_maximum_fusion) | copy-start | bytes 4718596
  115.0 4.8 %collective-permute-start.28 = (bf16[2,16,1536]{2,1,0:T(8,128)(2,1)S(1)}, bf16[2,16,1536]{2,1,0:T(8,128)(2,1)S(1)}, u32[]{:S(2)}, u32[]{:S(2)}) collective-permute-start(bf16[2,16,1536]{2,1,0:T(8,128)(2,1)S(1)} %get-tuple-element.91), channel_id=1, source_target_pairs={{0,16},{8,72},{16,0},{24,88},{32,48},{40,104},{48,32},{56,120},{64... | collective-permute-start | bytes 294920 | tf_op jit(solution)/shard_map/ppermute | solution.py:59
  116.4 4.6 %collective-permute-start.30 = (bf16[2,16,1536]{2,1,0:T(8,128)(2,1)S(1)}, bf16[2,16,1536]{2,1,0:T(8,128)(2,1)S(1)}, u32[]{:S(2)}, u32[]{:S(2)}) collective-permute-start(bf16[2,16,1536]{2,1,0:T(8,128)(2,1)S(1)} %get-tuple-element.92), channel_id=1, source_target_pairs={{0,48},{8,200},{16,32},{24,216},{32,16},{40,232},{48,0},{56,248},{... | collective-permute-start | bytes 294920 | tf_op jit(solution)/shard_map/ppermute | solution.py:59
  118.4 6.1 %collective-permute-start.29 = (bf16[2,16,1536]{2,1,0:T(8,128)(2,1)S(1)}, bf16[2,16,1536]{2,1,0:T(8,128)(2,1)S(1)}, u32[]{:S(2)}, u32[]{:S(2)}) collective-permute-start(bf16[2,16,1536]{2,1,0:T(8,128)(2,1)S(1)} %get-tuple-element.93), channel_id=1, source_target_pairs={{0,32},{8,136},{16,48},{24,152},{32,0},{40,168},{48,16},{56,184},{... | collective-permute-start | bytes 294920 | tf_op jit(solution)/shard_map/ppermute | solution.py:59
